TPU v7x, 256 devices: a whole 4x4x8 slice. The times are simulated.
256 devices in a mesh: leaf: 8 (over z), node: 32 (over x, y, core).
Axes of the slice: x: 4, y: 4, z: 8, core: 2. Of those that a mesh axis runs over, the one named last changes fastest.
Arguments:
- query_tree: bfloat16 [32768, 4096], P(('leaf', 'node')), may hold values from -6 to 6
- output_tree: bfloat16 [32768, 4096], P(('leaf', 'node')), may hold values from -6 to 6
- cotangent_tree: bfloat16 [32768, 4096], P(('leaf', 'node')), may hold values from -36 to 36
- log_norm_tree: float32 [32, 32768], P(None, ('leaf', 'node')), may hold values from 6.5 to 8
- key_value_tree: bfloat16 [32768, 1024], P(('leaf', 'node')), may hold values from -6 to 6
- query_root: bfloat16 [256, 4096], P(('leaf', 'node')), may hold values from -6 to 6
- output_root: bfloat16 [256, 4096], P(('leaf', 'node')), may hold values from -6 to 6
- cotangent_root: bfloat16 [256, 4096], P(('leaf', 'node')), may hold values from -36 to 36
- log_norm_root: float32 [32, 256], P(None, ('leaf', 'node')), may hold values from 6.5 to 8
- key_value_root: bfloat16 [256, 1024], P(('leaf', 'node')), may hold values from -6 to 6
- parent: int32 [8, 24], P('leaf'), may hold values from 0 to 22, as said below
- node_length: int32 [8, 24], P('leaf'), may hold values from 1 to 512, 4096 in all within a row
Outputs:
- grad_query_tree: float32 [32768, 4096], P(('leaf', 'node'))
- grad_query_root: float32 [256, 4096], P(('leaf', 'node'))
- grad_pairs_tree: float32 [32768, 1024], P(('leaf', 'node'))
- grad_pairs_root: float32 [256, 1024], P(('leaf', 'node'))
Inputs may be any that keep to these rules, and one draw needn't show every extreme that they name: Each row lists, for the nodes of one subtree in the order of their token rows, the position of each node's parent in that row; entry 0 is 0 and marks the subtree's top node; every other node's parent comes before it; the last node's parent is the node just before it. `node_length`: each row holds the token rows of one subtree's nodes, in the same node order as `parent`, summing to 4096.
All inputs are finite; a program needn't handle non-finite values.
Results may differ from a plain program's by a relative error of at most 0.003.
Values may be sent and summed in bfloat16 or wider, within the bound.
No kernel may reach another device: no remote copies, remote signals or barrier semaphores. Data moves between devices by JAX's collectives and lax.ppermute only.
A program may use at most 256 MiB of HBM per device.

v0:
```python
import math

import jax
import jax.numpy as jnp
from jax import lax
from jax.experimental import pallas as pl
from jax.experimental.pallas import tpu as pltpu
from jax.sharding import Mesh
from jax.sharding import PartitionSpec as P

HD = 128
NODES = 24
BLK = 128
TREE_BLOCKS = 32
FACTOR = HD ** (-0.5)
LOG2E = math.log2(math.e)
SCALE2 = FACTOR * LOG2E
BF = jnp.bfloat16
F4 = jnp.float32
Q0, D0, R0, T0, MSG = 0, 512, 1024, 1040, 1088
PAIR = 144
VMEM_LIMIT = 24 * 1024 * 1024


def params(limit=VMEM_LIMIT):
    return pltpu.CompilerParams(vmem_limit_bytes=limit)


def perm(dx, dy, dc):
    pairs = []
    for x in range(4):
        for y in range(4):
            for c in range(2):
                target = ((x + dx) % 4) * 8 + ((y + dy) % 4) * 2 + (c ^ dc)
                pairs.append((x * 8 + y * 2 + c, target))
    return pairs


def shift(array, dx=0, dy=0, dc=0):
    return lax.ppermute(array, ("x", "y", "core"), perm(dx, dy, dc))


def nt(left, right):
    return lax.dot_general(left, right, (((1,), (1,)), ((), ())), preferred_element_type=F4)


def nn(left, right):
    return lax.dot_general(left, right, (((1,), (0,)), ((), ())), preferred_element_type=F4)


def iota(shape, dim):
    return lax.broadcasted_iota(jnp.int32, shape, dim)


def flip(c, dc):
    return c if dc == 0 else 1 - c


def smem():
    return pl.BlockSpec(memory_space=pltpu.SMEM)


def vmem():
    return pl.BlockSpec(memory_space=pltpu.VMEM)


def tables_kernel(ids, parent, length, kbit, qanc, lists, counts, start, anc, kmask, qmask):
    x, y, c = ids[0], ids[1], ids[2]
    for block in range(TREE_BLOCKS):
        kmask[block] = 0
        qmask[block] = 0
    total = jnp.int32(0)
    for n in range(NODES):
        start[n] = total
        bits = jnp.int32(1 << n)
        if n > 0:
            bits = bits | anc[parent[0, n]]
        anc[n] = bits
        first = total // BLK
        total = total + length[0, n]
        last = (total - 1) // BLK

        def mark(block, carry):
            kmask[block] = kmask[block] | jnp.int32(1 << n)
            qmask[block] = qmask[block] | bits
            return carry

        lax.fori_loop(first, last + 1, mark, 0)
    positions = iota((TREE_BLOCKS, BLK), 0) * BLK + iota((TREE_BLOCKS, BLK), 1)
    table = jnp.zeros((TREE_BLOCKS, BLK), jnp.int32)
    own_bits = jnp.zeros((TREE_BLOCKS, BLK), jnp.int32)
    for n in range(NODES):
        inside = positions >= start[n]
        table = jnp.where(inside, anc[n], table)
        own_bits = jnp.where(inside, jnp.int32(1 << n), own_bits)
    qanc[...] = table
    for block in range(TREE_BLOCKS):
        row = jnp.broadcast_to(own_bits[block : block + 1, :], (BLK, BLK))
        kbit[block] = row.T
    kbit[TREE_BLOCKS] = jnp.zeros((BLK, BLK), jnp.int32)
    for i in range(8):
        mine = (lax.rem(x - i // 2 + 4, 4)) * 8 + y * 2 + flip(c, i % 2)
        seen = qmask[mine]

        def scan(block, found):
            hit = (seen & kmask[block]) != 0
            lists[i, found] = block
            return found + hit.astype(jnp.int32)

        found = lax.fori_loop(0, mine + 1, scan, jnp.int32(0))
        lists[i, found] = TREE_BLOCKS
        counts[i] = (found + 1) // 2


def make_tables(ids, parent, length):
    return pl.pallas_call(
        tables_kernel,
        in_specs=[smem(), smem(), smem()],
        out_specs=[vmem(), vmem(), smem(), smem()],
        out_shape=[
            jax.ShapeDtypeStruct((TREE_BLOCKS + 1, BLK, BLK), jnp.int32),
            jax.ShapeDtypeStruct((TREE_BLOCKS, BLK), jnp.int32),
            jax.ShapeDtypeStruct((8, 40), jnp.int32),
            jax.ShapeDtypeStruct((8,), jnp.int32),
        ],
        scratch_shapes=[
            pltpu.SMEM((NODES,), jnp.int32),
            pltpu.SMEM((NODES,), jnp.int32),
            pltpu.SMEM((TREE_BLOCKS,), jnp.int32),
            pltpu.SMEM((TREE_BLOCKS,), jnp.int32),
        ],
        compiler_params=params(),
        cost_estimate=pl.CostEstimate(
            flops=10**6, bytes_accessed=4 * 10**6, transcendentals=0
        ),
        name="tables",
    )(ids, parent, length)


def pack_pairs_kernel(pairs, root, out):
    for c in range(2):
        for x in range(4):
            cols = slice(c * 512 + x * HD, c * 512 + (x + 1) * HD)
            out[x * 2 + c, 0:BLK, :] = pairs[:, cols]
            row = jnp.broadcast_to(root[:, cols].astype(F4), (16, HD))
            tail = jnp.where(iota((16, HD), 0) == 0, row, 0.0)
            out[x * 2 + c, BLK:PAIR, :] = tail.astype(BF)


def pack_pairs(pairs, root):
    return pl.pallas_call(
        pack_pairs_kernel,
        in_specs=[vmem()] * 2,
        out_specs=vmem(),
        out_shape=jax.ShapeDtypeStruct((8, PAIR, HD), BF),
        compiler_params=params(),
        name="pack_pairs",
    )(pairs, root)


def split3(value):
    high = value.astype(BF)
    rest = value - high.astype(F4)
    middle = rest.astype(BF)
    low = (rest - middle.astype(F4)).astype(BF)
    return jnp.concatenate([high, middle, low], axis=0)


def pack_rows_kernel(ids, *refs):
    sources, keep, send, held, sems = refs[0:8], refs[8], refs[9], refs[10:18], refs[18]
    copies = [
        pltpu.make_async_copy(source, target, sems.at[n])
        for n, (source, target) in enumerate(zip(sources, held))
    ]
    for copy in copies:
        copy.start()
    for copy in copies:
        copy.wait()
    query, output, cotangent, norm, rquery, routput, rcotangent, rnorm = held
    x, c = ids[0], ids[2]
    norms = rnorm[...] * LOG2E
    for i in range(8):
        k, dc = i // 2, i % 2
        dest = lax.rem(x + k, 4) * 2 + flip(c, dc)
        out = send if dc else keep
        deltas = []
        for h in range(4):
            cols = pl.ds(pl.multiple_of(dest * 512 + h * HD, HD), HD)
            out[k, Q0 + h * BLK : Q0 + (h + 1) * BLK, :] = query[:, cols]
            grad = cotangent[:, cols]
            out[k, D0 + h * BLK : D0 + (h + 1) * BLK, :] = grad
            product = grad.astype(F4) * output[:, cols].astype(F4)
            deltas.append(jnp.sum(product.T, axis=0, keepdims=True))
        lane = iota((1, HD), 1)
        rnorm_row = jnp.zeros((1, HD), F4)
        rdelta_row = jnp.zeros((1, HD), F4)
        rquery_rows, rgrad_rows = [], []
        for h in range(4):
            cols = pl.ds(pl.multiple_of(dest * 512 + h * HD, HD), HD)
            rgrad = rcotangent[:, cols].astype(F4)
            rquery_rows.append(rquery[:, cols].astype(F4))
            rgrad_rows.append(rgrad)
            rdelta = jnp.sum(rgrad * routput[:, cols].astype(F4), axis=1, keepdims=True)
            here = lane == i * 4 + h
            mine = jnp.where(iota((1, 32), 1) == dest * 4 + h, norms, 0.0)
            mine = jnp.broadcast_to(jnp.sum(mine, axis=1, keepdims=True), (1, HD))
            rnorm_row = jnp.where(here, mine, rnorm_row)
            rdelta_row = jnp.where(here, jnp.broadcast_to(rdelta, (1, HD)), rdelta_row)
        rows = jnp.concatenate(
            [norm[pl.ds(dest * 4, 4), :] * LOG2E]
            + deltas
            + [rnorm_row, rdelta_row, jnp.zeros((6, HD), F4)],
            axis=0,
        )
        out[k, T0 : T0 + 48, :] = split3(rows)
        tile = jnp.concatenate(rquery_rows + rgrad_rows + [jnp.zeros((8, HD), F4)], axis=0)
        out[k, R0 : R0 + 16, :] = tile.astype(BF)


def pack_rows(ids, query, output, cotangent, norm, rquery, routput, rcotangent, rnorm):
    return pl.pallas_call(
        pack_rows_kernel,
        in_specs=[smem()] + [pl.BlockSpec(memory_space=pl.ANY)] * 8,
        out_specs=[vmem()] * 2,
        out_shape=[jax.ShapeDtypeStruct((4, MSG, HD), BF)] * 2,
        scratch_shapes=[pltpu.VMEM((BLK, 4096), BF)] * 3
        + [pltpu.VMEM((32, BLK), F4)]
        + [pltpu.VMEM((1, 4096), BF)] * 3
        + [pltpu.VMEM((1, 32), F4), pltpu.SemaphoreType.DMA((8,))],
        compiler_params=params(60 * 1024 * 1024),
        name="pack_rows",
    )(ids, query, output, cotangent, norm, rquery, routput, rcotangent, rnorm)


def merge_rows_kernel(keep, other, *outs):
    for k in range(4):
        outs[k][0] = keep[k]
        outs[k][1] = other[k]


def merge_rows(keep, other):
    return pl.pallas_call(
        merge_rows_kernel,
        in_specs=[vmem()] * 2,
        out_specs=[vmem()] * 4,
        out_shape=[jax.ShapeDtypeStruct((2, MSG, HD), BF)] * 4,
        compiler_params=params(),
        name="merge_rows",
    )(keep, other)


def unsplit(rows):
    wide = rows.astype(F4)
    return wide[0:16] + wide[16:32] + wide[32:48]


def pack_root_kernel(joined, out):
    tile = jnp.zeros((16, HD), F4)
    for block in range(8):
        row = joined[block, BLK:PAIR, :].astype(F4)[0:1]
        tile = jnp.where(iota((16, HD), 0) == block, jnp.broadcast_to(row, (16, HD)), tile)
    for target in range(32):
        out[target] = tile.astype(BF)


def pack_root(joined):
    return pl.pallas_call(
        pack_root_kernel,
        in_specs=[vmem()],
        out_specs=vmem(),
        out_shape=jax.ShapeDtypeStruct((32, 16, HD), BF),
        compiler_params=params(),
        name="pack_root",
    )(joined)


def place(y, ky, block):
    return (block // 2) * 8 + lax.rem(y - ky + 4, 4) * 2 + block % 2


def lanes_of(terms, start):
    return jnp.concatenate([terms[start + h : start + h + 1, :] for h in range(4)], axis=1)


def compute_kernel(ids, lists, counts, kbit, qanc, own, other, root_own, root_other, *refs):
    msgs, outs, refs = refs[0:4], refs[4:8], refs[8:]
    keep, send, root_keep, root_send, refs = *refs[0:4], refs[4:]
    keys, values, keys_t, root_rows, acc, dk, dv, rkey, rvalue, rkey_t, rdk, rdv = refs
    x, y, c, z = ids[0], ids[1], ids[2], ids[3]
    first = c == 0

    def load(key_ref, value_ref):
        for ky in range(4):
            for block in range(8):
                to = place(y, ky, block)
                part = key_ref[ky, block, 0:BLK, :]
                keys[to] = part
                keys_t[to] = part.astype(F4).T.astype(BF)
                values[to] = value_ref[ky, block, 0:BLK, :]

    @pl.when(first)
    def _():
        load(own, other)

    @pl.when(c != 0)
    def _():
        load(other, own)

    keys[TREE_BLOCKS] = jnp.zeros((BLK, HD), BF)
    keys_t[TREE_BLOCKS] = jnp.zeros((BLK, HD), BF)
    values[TREE_BLOCKS] = jnp.zeros((BLK, HD), BF)
    dk[...] = jnp.zeros(dk.shape, F4)
    dv[...] = jnp.zeros(dv.shape, F4)

    rows_own = root_own[...].astype(F4)[:, 0:8, :].reshape(256, HD)
    rows_other = root_other[...].astype(F4)[:, 0:8, :].reshape(256, HD)
    key_wide = jnp.where(first, rows_own, rows_other)
    rvalue[...] = jnp.where(first, rows_other, rows_own).astype(BF)
    rkey_t[...] = key_wide.T.astype(BF)
    rkey[...] = key_wide.astype(BF)

    root_rows[...] = jnp.zeros(root_rows.shape, F4)
    special = jnp.zeros((16, HD), F4)
    for i in range(8):
        msg, dc = msgs[i // 2], i % 2
        special = special + unsplit(msg[dc, T0 : T0 + 48, :])
        tile = msg[dc, R0 : R0 + 16, :].astype(F4)
        root_rows[0, i * 4 : i * 4 + 4, :] = tile[0:4]
        root_rows[1, i * 4 : i * 4 + 4, :] = tile[4:8]
    query = root_rows[0].astype(BF)
    grad = root_rows[1].astype(BF)
    lane, row = iota((256, HD), 1), iota((256, HD), 0)
    source = lane // 4
    source_x = lax.rem(x - source // 2 + 16, 4)
    source_c = jnp.where(source % 2 == 0, c, 1 - c)
    root_query_pos = z * 32 + source_x * 8 + y * 2 + source_c
    at = row // 8
    root_key_pos = (at // 4) * 32 + (row % 8 // 2) * 8 + (at % 4) * 2 + row % 2
    mask = (lane < 32) & (root_key_pos <= root_query_pos)
    prob = jnp.where(mask, jnp.exp2(nt(rkey[...], query) * SCALE2 - special[8:9, :]), 0.0)
    dscore = (prob * (nt(rvalue[...], grad) - special[9:10, :])).astype(BF)
    rdv[...] = nn(prob.astype(BF), grad)
    rdk[...] = nn(dscore, query)
    root_dq = nn(rkey_t[...], dscore).T * FACTOR

    pad = jnp.zeros((12, HD), F4)
    base = iota((BLK, BLK), 0)
    for k in range(4):
        msg, out = msgs[k], outs[k]
        for dc in range(2):
            tile = root_dq[8 * k + 4 * dc : 8 * k + 4 * dc + 4]
            out[dc, 512:528, :] = jnp.concatenate([tile, pad], axis=0).astype(BF)

        def query_block(dc, carry):
            i = k * 2 + dc
            mine = lax.rem(x - k + 4, 4) * 8 + y * 2 + jnp.where(dc == 0, c, 1 - c)
            anc_row = jnp.broadcast_to(qanc[pl.ds(mine, 1), :], (2 * BLK, BLK))
            query_pos = iota((2 * BLK, BLK), 1) + mine * BLK
            terms = unsplit(msg[dc, T0 : T0 + 48, :])
            norm, delta = lanes_of(terms, 0), lanes_of(terms, 4)

            def gradients(key, value, key_t, mask):
                query = msg[dc, Q0 : Q0 + 512, :]
                grad = msg[dc, D0 : D0 + 512, :]
                prob = jnp.exp2(nt(key, query) * SCALE2 - norm)
                if mask is not None:
                    prob = jnp.where(jnp.concatenate([mask] * 4, axis=1), prob, 0.0)
                dscore = (prob * (nt(value, grad) - delta)).astype(BF)
                return nn(dscore, query), nn(prob.astype(BF), grad), nn(key_t, dscore)

            dk_part, dv_part, dq_part = gradients(rkey[...], rvalue[...], rkey_t[...], None)
            rdk[...] = rdk[...] + dk_part
            rdv[...] = rdv[...] + dv_part
            acc[...] = dq_part

            def unit(j):
                b0, b1 = lists[i, 2 * j], lists[i, 2 * j + 1]
                key = jnp.concatenate([keys[b0], keys[b1]], axis=0)
                value = jnp.concatenate([values[b0], values[b1]], axis=0)
                key_t = jnp.concatenate([keys_t[b0], keys_t[b1]], axis=1)
                bits = jnp.concatenate([kbit[b0], kbit[b1]], axis=0)
                key_pos = jnp.concatenate([base + b0 * BLK, base + b1 * BLK], axis=0)
                mask = ((bits & anc_row) != 0) & (key_pos <= query_pos)
                dk_part, dv_part, dq_part = gradients(key, value, key_t, mask)
                acc[...] = acc[...] + dq_part
                dk[b0] = dk[b0] + dk_part[0:BLK]
                dv[b0] = dv[b0] + dv_part[0:BLK]
                dk[b1] = dk[b1] + dk_part[BLK:]
                dv[b1] = dv[b1] + dv_part[BLK:]

            def two(j, inner):
                unit(2 * j)
                unit(2 * j + 1)
                return inner

            count = counts[i]
            lax.fori_loop(0, count // 2, two, 0)

            @pl.when(count % 2 == 1)
            def _():
                unit(count - 1)

            for h in range(4):
                done = acc[:, h * BLK : (h + 1) * BLK].T * FACTOR
                out[dc, h * BLK : (h + 1) * BLK, :] = done.astype(BF)
            return carry

        lax.fori_loop(0, 2, query_block, 0)

    def store(keep_from, send_from, root_keep_from, root_send_from):
        for ky in range(4):
            for block in range(8):
                at = place(y, ky, block)
                keep[ky * 8 + block] = keep_from[at]
                send[ky * 8 + block] = send_from[at].astype(BF)
        root_keep[...] = root_keep_from[...].reshape(32, 8, HD)
        root_send[...] = root_send_from[...].reshape(32, 8, HD)

    @pl.when(first)
    def _():
        store(dk, dv, rdk, rdv)

    @pl.when(c != 0)
    def _():
        store(dv, dk, rdv, rdk)


def compute(ids, lists, counts, kbit, qanc, own, other, root_own, root_other, msgs):
    half = (TREE_BLOCKS, BLK, HD)
    blocks = pltpu.VMEM((TREE_BLOCKS + 1, BLK, HD), BF)
    sums = pltpu.VMEM((TREE_BLOCKS + 1, BLK, HD), F4)
    return pl.pallas_call(
        compute_kernel,
        in_specs=[smem()] * 3 + [vmem()] * 10,
        out_specs=[vmem()] * 8,
        out_shape=[jax.ShapeDtypeStruct((2, 528, HD), BF)] * 4
        + [jax.ShapeDtypeStruct(half, F4), jax.ShapeDtypeStruct(half, BF)]
        + [jax.ShapeDtypeStruct((32, 8, HD), F4)] * 2,
        scratch_shapes=[
            blocks,
            blocks,
            blocks,
            pltpu.VMEM((2, HD, HD), F4),
            pltpu.VMEM((HD, 512), F4),
            sums,
            sums,
            pltpu.VMEM((256, HD), BF),
            pltpu.VMEM((256, HD), BF),
            pltpu.VMEM((HD, 256), BF),
            pltpu.VMEM((256, HD), F4),
            pltpu.VMEM((256, HD), F4),
        ],
        compiler_params=params(32 * 1024 * 1024),
        cost_estimate=pl.CostEstimate(
            flops=10**10, bytes_accessed=16 * 10**6, transcendentals=8 * 10**6
        ),
        name="compute",
    )(ids, lists, counts, kbit, qanc, own, other, root_own, root_other, *msgs)


def unpack_query_kernel(ids, *refs):
    x, c = ids[0], ids[2]
    straight, crossed, out, root_out = refs[0:4], refs[4], refs[5], refs[6]
    for i in range(8):
        k, dc = i // 2, i % 2
        dest = lax.rem(x + k, 4) * 2 + flip(c, dc)
        part = crossed[k] if dc else straight[k][0]
        for h in range(4):
            cols = pl.ds(pl.multiple_of(dest * 512 + h * HD, HD), HD)
            out[:, cols] = part[h * BLK : (h + 1) * BLK, :].astype(F4)
        root_out[dest] = part[512:528, :].astype(F4)[0:4]


def unpack_query(ids, parts, crossed):
    return pl.pallas_call(
        unpack_query_kernel,
        in_specs=[smem()] + [vmem()] * 5,
        out_specs=[vmem()] * 2,
        out_shape=[
            jax.ShapeDtypeStruct((BLK, 4096), F4),
            jax.ShapeDtypeStruct((8, 4, HD), F4),
        ],
        compiler_params=params(),
        name="unpack_query",
    )(ids, *parts, crossed)


def join_cores_kernel(keep, other, stay, *outs):
    for block in range(TREE_BLOCKS):
        ky, at = block // 8, block % 8
        total = keep[block] + other[block].astype(F4)
        if ky == 0:
            stay[at] = total
        else:
            outs[ky - 1][at] = total.astype(BF)


def join_cores(keep, other):
    return pl.pallas_call(
        join_cores_kernel,
        in_specs=[vmem()] * 2,
        out_specs=[vmem()] * 4,
        out_shape=[jax.ShapeDtypeStruct((8, BLK, HD), F4)]
        + [jax.ShapeDtypeStruct((8, BLK, HD), BF)] * 3,
        compiler_params=params(),
        name="join_cores",
    )(keep, other)


def sum_pairs_kernel(stay, r1, r2, r3, roots, out):
    total = roots[0]
    for n in range(1, 32):
        total = total + roots[n]
    for block in range(8):
        rest = r1[block].astype(F4) + r2[block].astype(F4) + r3[block].astype(F4)
        out[block, 0:BLK, :] = stay[block] + rest
        out[block, BLK : BLK + 8, :] = jnp.broadcast_to(total[block : block + 1], (8, HD))


def sum_pairs(stay, received, roots):
    return pl.pallas_call(
        sum_pairs_kernel,
        in_specs=[vmem()] * 5,
        out_specs=vmem(),
        out_shape=jax.ShapeDtypeStruct((8, BLK + 8, HD), F4),
        compiler_params=params(),
        name="sum_pairs",
    )(stay, *received, roots)


def unpack_pairs_kernel(parts, out, root_out):
    for c in range(2):
        for x in range(4):
            total = parts[x * 2 + c]
            if c == 0:
                total = total * FACTOR
            cols = slice(c * 512 + x * HD, c * 512 + (x + 1) * HD)
            out[:, cols] = total[0:BLK]
            root_out[:, cols] = total[BLK : BLK + 1]


def unpack_pairs(parts):
    return pl.pallas_call(
        unpack_pairs_kernel,
        in_specs=[vmem()],
        out_specs=[vmem()] * 2,
        out_shape=[
            jax.ShapeDtypeStruct((BLK, 1024), F4),
            jax.ShapeDtypeStruct((1, 1024), F4),
        ],
        compiler_params=params(),
        name="unpack_pairs",
    )(parts)


def across(array):
    return lax.all_to_all(array, ("x", "core"), 0, 0, tiled=True)


def along(array):
    return lax.all_to_all(array, ("leaf", "y"), 0, 0, tiled=True)


def shards(
    query_tree,
    output_tree,
    cotangent_tree,
    log_norm_tree,
    key_value_tree,
    query_root,
    output_root,
    cotangent_root,
    log_norm_root,
    key_value_root,
    parent,
    node_length,
):
    ids = jnp.stack([lax.axis_index(name) for name in ("x", "y", "core", "leaf")])
    ids = ids.astype(jnp.int32)
    together = lax.optimization_barrier

    joined = across(pack_pairs(key_value_tree, key_value_root))
    joined, ids = together((joined, ids))
    keep, send = pack_rows(
        ids,
        query_tree,
        output_tree,
        cotangent_tree,
        log_norm_tree,
        query_root,
        output_root,
        cotangent_root,
        log_norm_root.reshape(1, 32),
    )
    merged = merge_rows(keep, shift(send, dc=1))
    joined, *merged = together((joined, *merged))

    msg1, msg3 = shift(merged[1], dx=1), shift(merged[3], dx=3)
    own = [joined] + [shift(joined, dy=ky) for ky in range(1, 4)]
    root_own = along(pack_root(joined))
    msg1, msg3, merged[2], root_own, *own = together(
        (msg1, msg3, merged[2], root_own, *own)
    )

    msgs = [merged[0], msg1, shift(merged[2], dx=2), msg3]
    own = jnp.stack(own, axis=0)
    other, root_other = shift(own, dc=1), shift(root_own, dc=1)
    kbit, qanc, lists, counts = make_tables(ids, parent, node_length)
    *parts, keep, send, root_keep, root_send = compute(
        ids, lists, counts, kbit, qanc, own, other, root_own, root_other, msgs
    )

    stay, *low = join_cores(keep, shift(send, dc=1))
    root_sums = root_keep + shift(root_send, dc=1)
    stay, root_sums, *rest = together((stay, root_sums, *low, *parts))
    low, parts = rest[0:3], rest[3:7]

    received = [shift(low[ky - 1], dy=-ky) for ky in range(1, 4)]
    back1, back3 = shift(parts[1], dx=-1), shift(parts[3], dx=-3)
    roots = along(root_sums)
    stay, roots, back1, back3, part2, *received = together(
        (stay, roots, back1, back3, parts[2], *received)
    )

    grads = across(sum_pairs(stay, received, roots))
    back2 = shift(part2, dx=-2)
    grads, back2 = together((grads, back2))

    back = [parts[0], back1, back2, back3]
    crossed = shift(jnp.stack([part[1] for part in back], axis=0), dc=1)
    grad_pairs, grad_root = unpack_pairs(grads)
    grad_query, grad_query_root = unpack_query(ids, back, crossed)
    return grad_query, grad_query_root.reshape(1, 4096), grad_pairs, grad_root


def solution(mesh):
    axes = ("leaf", "x", "y", "core")
    finer = Mesh(mesh.devices.reshape(8, 4, 4, 2), axes)
    rows = P(axes, None)
    lanes = P(None, axes)
    tree = P("leaf", None)
    return jax.shard_map(
        shards,
        mesh=finer,
        in_specs=(rows, rows, rows, lanes, rows, rows, rows, rows, lanes, rows, tree, tree),
        out_specs=(rows, rows, rows, rows),
        check_vma=False,
    )
```

profile of v0, /device:TPU:1, one launch (start us, length us, event | category | flops | bytes accessed | tf_op | source)
XLA Modules:
  0.0 151.8 jit_solution(15210471600447927239)
XLA Ops:
  0.6 0.0 copy-start.1
  0.6 0.9 copy-done.1
  1.6 0.7 copy-done.3
  2.3 0.8 pack_pairs.1
  3.0 6.6 %all-to-all-start = ((bf16[8,144,128]{2,1,0:T(8,128)(2,1)}), bf16[8,144,128]{2,1,0:T(8,128)(2,1)S(1)}, u32[]{:S(2)}, u32[]{:S(2)}) async-start(bf16[8,144,128]{2,1,0:T(8,128)(2,1)} %pack_pairs.1), calls=%async_computation | async-start | bytes 589824 | tf_op jit(solution)/shard_map/all_to_all | solution.py:557
  9.6 0.7 pad_add_fusion.ids
  10.3 6.2 %all-to-all-done.joined = bf16[8,144,128]{2,1,0:T(8,128)(2,1)S(1)} async-done(((bf16[8,144,128]{2,1,0:T(8,128)(2,1)}), bf16[8,144,128]{2,1,0:T(8,128)(2,1)S(1)}, u32[]{:S(2)}, u32[]{:S(2)}) %all-to-all-start) | async-done | bytes 294944 | tf_op jit(solution)/shard_map/all_to_all | solution.py:557
  16.4 5.0 %pack_rows.1 = (bf16[4,1088,128]{2,1,0:T(8,128)(2,1)}, bf16[4,1088,128]{2,1,0:T(8,128)(2,1)}) custom-call(s32[4]{0:T(128)} %pad_add_fusion.ids, bf16[128,4096]{1,0:T(8,128)(2,1)} %refs_0_.1, bf16[128,4096]{1,0:T(8,128)(2,1)} %refs_1_.1, bf16[128,4096]{1,0:T(8,128)(2,1)} %refs_2_.1, f32[32,128]{1,0:T(8,128)} %refs_3_.1, bf16[1,4096]{1,0:T(2,128)(2,1)} %refs_4_.1, ...), custom_call_target="tpu_custom_call" | custom-call | tf_op jit(solution)/shard_map/pack_rows/pallas_call | solution.py:221
  21.5 1.2 collective-permute-start
  22.7 2.6 %collective-permute-done.other = bf16[4,1088,128]{2,1,0:T(8,128)(2,1)S(1)} collective-permute-done((bf16[4,1088,128]{2,1,0:T(8,128)(2,1)}, bf16[4,1088,128]{2,1,0:T(8,128)(2,1)S(1)}, u32[]{:S(2)}, u32[]{:S(2)}) %collective-permute-start) | collective-permute-done | bytes 1114144 | tf_op jit(solution)/shard_map/ppermute | solution.py:40
  25.3 1.2 copy-done
  26.5 0.1 merge_rows.1
  26.6 0.4 collective-permute-start.1
  27.0 2.4 %collective-permute-start.2 = (bf16[2,1088,128]{2,1,0:T(8,128)(2,1)S(1)}, bf16[2,1088,128]{2,1,0:T(8,128)(2,1)S(1)}, u32[]{:S(2)}, u32[]{:S(2)}) collective-permute-start(bf16[2,1088,128]{2,1,0:T(8,128)(2,1)S(1)} %get-tuple-element.77), channel_id=1, source_target_pairs={{0,24},{1,25},{2,26},{3,27},{4,28},{5,29},{6,30},{7,31},{8,0},{9,1... | collective-permute-start | bytes 1671176 | tf_op jit(solution)/shard_map/ppermute | solution.py:40
  29.4 2.0 %collective-permute-start.5 = (bf16[8,144,128]{2,1,0:T(8,128)(2,1)S(1)}, bf16[8,144,128]{2,1,0:T(8,128)(2,1)S(1)}, u32[]{:S(2)}, u32[]{:S(2)}) collective-permute-start(bf16[8,144,128]{2,1,0:T(8,128)(2,1)S(1)} %all-to-all-done.joined), channel_id=1, source_target_pairs={{0,6},{1,7},{2,0},{3,1},{4,2},{5,3},{6,4},{7,5},{8,14},{9,15},{10,... | collective-permute-start | bytes 884744 | tf_op jit(solution)/shard_map/ppermute | solution.py:40
  31.3 0.3 collective-permute-start.4
  31.7 0.7 collective-permute-start.3
  32.4 19.4 %all_to_all.20.root_own = bf16[32,16,128]{2,1,0:T(8,128)(2,1)S(1)} all-to-all(bf16[32,16,128]{2,1,0:T(8,128)(2,1)S(1)} %pack_root.1), channel_id=1, replica_groups=mesh['leaf'=8,'x'=4,'y'=4,'core'=2] {'leaf','y'}, dimensions={0} | all-to-all | bytes 262144 | tf_op jit(solution)/shard_map/all_to_all | solution.py:561
  51.8 0.0 collective-permute-done.5
  51.8 0.0 collective-permute-done.4
  51.8 0.0 collective-permute-done.3
  51.8 0.0 collective-permute-done.1.refs_1_
  51.9 0.0 collective-permute-done.2.refs_3_
  51.9 0.0 copy-start.2
  51.9 0.0 copy-start.4
  51.9 0.0 copy-start.5
  51.9 0.2 pad_maximum_fusion.own
  52.1 3.4 %collective-permute-start.6 = (bf16[4,8,144,128]{3,2,1,0:T(8,128)(2,1)S(1)}, bf16[4,8,144,128]{3,2,1,0:T(8,128)(2,1)S(1)}, u32[]{:S(2)}, u32[]{:S(2)}) collective-permute-start(bf16[4,8,144,128]{3,2,1,0:T(8,128)(2,1)S(1)} %pad_maximum_fusion.own), channel_id=1, source_target_pairs={{0,1},{1,0},{2,3},{3,2},{4,5},{5,4},{6,7},{7,6},{8,9},{9,8},{10,11... | collective-permute-start | bytes 3538952 | tf_op jit(solution)/shard_map/ppermute | solution.py:40
  55.4 0.0 collective-permute-start.8
  55.4 0.2 collective-permute-start.7
  55.6 0.0 copy-done.2
  55.6 0.0 copy-done.4
  55.6 0.0 copy-done.5
  55.6 3.5 %tables.1 = (s32[33,128,128]{2,1,0:T(8,128)S(1)}, s32[32,128]{1,0:T(8,128)S(1)}, s32[8,40]{1,0:T(8,128)S(1)}, s32[8]{0:T(128)S(1)}) custom-call(s32[4]{0:T(128)S(1)} %copy-done.2, s32[1,24]{1,0:T(1,128)S(1)} %copy-done.4, s32[1,24]{1,0:T(1,128)S(1)} %copy-done.5), custom_call_target="tpu_custom_call" | custom-call | flops 1000000 | bytes 4000000 | tf_op jit(solution)/shard_map/tables/pallas_call | solution.py:116
  59.1 0.0 collective-permute-done.7.root_other
  59.2 12.0 %collective-permute-done.8.refs_2_ = bf16[2,1088,128]{2,1,0:T(8,128)(2,1)S(1)} collective-permute-done((bf16[2,1088,128]{2,1,0:T(8,128)(2,1)S(1)}, bf16[2,1088,128]{2,1,0:T(8,128)(2,1)S(1)}, u32[]{:S(2)}, u32[]{:S(2)}) %collective-permute-start.8) | collective-permute-done | bytes 557088 | tf_op jit(solution)/shard_map/ppermute | solution.py:40
  71.1 0.0 collective-permute-done.6.other
  71.1 23.9 %compute.1 = (bf16[2,528,128]{2,1,0:T(8,128)(2,1)S(1)}, bf16[2,528,128]{2,1,0:T(8,128)(2,1)S(1)}, bf16[2,528,128]{2,1,0:T(8,128)(2,1)S(1)}, bf16[2,528,128]{2,1,...) custom-call(s32[4]{0:T(128)S(1)} %copy-done.2, ...), custom_call_target="tpu_custom_call" | custom-call | flops 10000000000 | bytes 16000000 | tf_op jit(solution)/shard_map/compute/pallas_call | solution.py:432
  95.1 1.0 collective-permute-start.9
  96.0 0.1 collective-permute-start.10
  96.1 2.4 %collective-permute-done.10 = f32[32,8,128]{2,1,0:T(8,128)S(1)} collective-permute-done((f32[32,8,128]{2,1,0:T(8,128)S(1)}, f32[32,8,128]{2,1,0:T(8,128)S(1)}, u32[]{:S(2)}, u32[]{:S(2)}) %collective-permute-start.10) | collective-permute-done | bytes 131104 | tf_op jit(solution)/shard_map/ppermute | solution.py:40
  98.5 0.0 collective-permute-done.9.other
  98.5 0.3 join_cores.1
  98.8 0.1 collective-permute-start.11
  98.9 1.5 collective-permute-start.12
  100.3 2.5 %collective-permute-start.13 = (bf16[8,128,128]{2,1,0:T(8,128)(2,1)S(1)}, bf16[8,128,128]{2,1,0:T(8,128)(2,1)S(1)}, u32[]{:S(2)}, u32[]{:S(2)}) collective-permute-start(bf16[8,128,128]{2,1,0:T(8,128)(2,1)S(1)} %get-tuple-element.107), channel_id=1, source_target_pairs={{0,6},{1,7},{2,0},{3,1},{4,2},{5,3},{6,4},{7,5},{8,14},{9,15},{10,... | collective-permute-start | bytes 786440 | tf_op jit(solution)/shard_map/ppermute | solution.py:40
  102.8 0.0 collective-permute-start.14
  102.8 0.6 collective-permute-start.15
  103.4 20.6 %all_to_all.21.roots = f32[32,8,128]{2,1,0:T(8,128)S(1)} all-to-all(f32[32,8,128]{2,1,0:T(8,128)S(1)} %add.3), channel_id=1, replica_groups=mesh['leaf'=8,'x'=4,'y'=4,'core'=2] {'leaf','y'}, dimensions={0} | all-to-all | bytes 262144 | tf_op jit(solution)/shard_map/all_to_all | solution.py:561
  124.0 0.0 collective-permute-done.13.r1
  124.0 0.0 collective-permute-done.14.r2
  124.0 0.0 collective-permute-done.15.r3
  124.0 0.0 collective-permute-done.11.refs_1_
  124.0 0.0 collective-permute-done.12.refs_3_
  124.0 0.9 sum_pairs.1
  124.9 6.5 %all-to-all-start.3 = ((f32[8,136,128]{2,1,0:T(8,128)}), f32[8,136,128]{2,1,0:T(8,128)S(1)}, u32[]{:S(2)}, u32[]{:S(2)}) async-start(f32[8,136,128]{2,1,0:T(8,128)} %sum_pairs.1), calls=%async_computation.3 | async-start | bytes 1114112 | tf_op jit(solution)/shard_map/all_to_all | solution.py:557
  131.4 2.9 %collective-permute-start.16 = (bf16[2,528,128]{2,1,0:T(8,128)(2,1)S(1)}, bf16[2,528,128]{2,1,0:T(8,128)(2,1)S(1)}, u32[]{:S(2)}, u32[]{:S(2)}) collective-permute-start(bf16[2,528,128]{2,1,0:T(8,128)(2,1)S(1)} %get-tuple-element.116), channel_id=1, source_target_pairs={{0,16},{1,17},{2,18},{3,19},{4,20},{5,21},{6,22},{7,23},{8,24},{9,... | collective-permute-start | bytes 811016 | tf_op jit(solution)/shard_map/ppermute | solution.py:40
  134.4 12.7 %collective-permute-done.16.refs_2_ = bf16[2,528,128]{2,1,0:T(8,128)(2,1)S(1)} collective-permute-done((bf16[2,528,128]{2,1,0:T(8,128)(2,1)S(1)}, bf16[2,528,128]{2,1,0:T(8,128)(2,1)S(1)}, u32[]{:S(2)}, u32[]{:S(2)}) %collective-permute-start.16) | collective-permute-done | bytes 270368 | tf_op jit(solution)/shard_map/ppermute | solution.py:40
  147.1 0.0 all-to-all-done.3.parts
  147.1 0.1 pad_maximum_fusion.1
  147.2 1.0 collective-permute-start.17
  148.1 0.9 unpack_pairs.1
  149.0 0.7 collective-permute-done.17.refs_4_
  149.7 2.1 %unpack_query.1 = (f32[128,4096]{1,0:T(8,128)}, f32[8,4,128]{2,1,0:T(4,128)}) custom-call(s32[4]{0:T(128)S(1)} %copy-done.2, bf16[2,528,128]{2,1,0:T(8,128)(2,1)S(1)} %get-tuple-element.101.refs_0_, bf16[2,528,128]{2,1,0:T(8,128)(2,1)S(1)} %collective-permute-done.11.refs_1_, bf16[2,528,128]{2,1,0:T(8,128)(2,1)S(1)} %collective-permute-done.16.refs_2_, ...), custom_call_target="tpu_custom_call" | custom-call | tf_op jit(solution)/shard_map/unpack_query/pallas_call | solution.py:475
  (8 shorter events, 0.1 us)
Async XLA Ops:
  0.6 1.0 copy-start.1
  1.6 0.7 copy-start.3
  3.0 13.4 %all-to-all-start = ((bf16[8,144,128]{2,1,0:T(8,128)(2,1)}), bf16[8,144,128]{2,1,0:T(8,128)(2,1)S(1)}, u32[]{:S(2)}, u32[]{:S(2)}) async-start(bf16[8,144,128]{2,1,0:T(8,128)(2,1)} %pack_pairs.1), calls=%async_computation | async-start | bytes 589824 | tf_op jit(solution)/shard_map/all_to_all | solution.py:557
  21.5 3.8 %collective-permute-start = (bf16[4,1088,128]{2,1,0:T(8,128)(2,1)}, bf16[4,1088,128]{2,1,0:T(8,128)(2,1)S(1)}, u32[]{:S(2)}, u32[]{:S(2)}) collective-permute-start(bf16[4,1088,128]{2,1,0:T(8,128)(2,1)} %get-tuple-element.71), channel_id=1, source_target_pairs={{0,1},{1,0},{2,3},{3,2},{4,5},{5,4},{6,7},{7,6},{8,9},{9,8},{10,11... | collective-permute-start | bytes 3342344 | tf_op jit(solution)/shard_map/ppermute | solution.py:40
  25.2 1.2 copy-start
  26.6 25.2 %collective-permute-start.1 = (bf16[2,1088,128]{2,1,0:T(8,128)(2,1)S(1)}, bf16[2,1088,128]{2,1,0:T(8,128)(2,1)S(1)}, u32[]{:S(2)}, u32[]{:S(2)}) collective-permute-start(bf16[2,1088,128]{2,1,0:T(8,128)(2,1)S(1)} %get-tuple-element.76), channel_id=1, source_target_pairs={{0,8},{1,9},{2,10},{3,11},{4,12},{5,13},{6,14},{7,15},{8,16},{9,17... | collective-permute-start | bytes 1671176 | tf_op jit(solution)/shard_map/ppermute | solution.py:40
  27.0 24.8 %collective-permute-start.2 = (bf16[2,1088,128]{2,1,0:T(8,128)(2,1)S(1)}, bf16[2,1088,128]{2,1,0:T(8,128)(2,1)S(1)}, u32[]{:S(2)}, u32[]{:S(2)}) collective-permute-start(bf16[2,1088,128]{2,1,0:T(8,128)(2,1)S(1)} %get-tuple-element.77), channel_id=1, source_target_pairs={{0,24},{1,25},{2,26},{3,27},{4,28},{5,29},{6,30},{7,31},{8,0},{9,1... | collective-permute-start | bytes 1671176 | tf_op jit(solution)/shard_map/ppermute | solution.py:40
  29.4 22.4 %collective-permute-start.5 = (bf16[8,144,128]{2,1,0:T(8,128)(2,1)S(1)}, bf16[8,144,128]{2,1,0:T(8,128)(2,1)S(1)}, u32[]{:S(2)}, u32[]{:S(2)}) collective-permute-start(bf16[8,144,128]{2,1,0:T(8,128)(2,1)S(1)} %all-to-all-done.joined), channel_id=1, source_target_pairs={{0,6},{1,7},{2,0},{3,1},{4,2},{5,3},{6,4},{7,5},{8,14},{9,15},{10,... | collective-permute-start | bytes 884744 | tf_op jit(solution)/shard_map/ppermute | solution.py:40
  31.3 20.5 %collective-permute-start.4 = (bf16[8,144,128]{2,1,0:T(8,128)(2,1)S(1)}, bf16[8,144,128]{2,1,0:T(8,128)(2,1)S(1)}, u32[]{:S(2)}, u32[]{:S(2)}) collective-permute-start(bf16[8,144,128]{2,1,0:T(8,128)(2,1)S(1)} %all-to-all-done.joined), channel_id=1, source_target_pairs={{0,4},{1,5},{2,6},{3,7},{4,0},{5,1},{6,2},{7,3},{8,12},{9,13},{10,... | collective-permute-start | bytes 884744 | tf_op jit(solution)/shard_map/ppermute | solution.py:40
  31.7 20.1 %collective-permute-start.3 = (bf16[8,144,128]{2,1,0:T(8,128)(2,1)S(1)}, bf16[8,144,128]{2,1,0:T(8,128)(2,1)S(1)}, u32[]{:S(2)}, u32[]{:S(2)}) collective-permute-start(bf16[8,144,128]{2,1,0:T(8,128)(2,1)S(1)} %all-to-all-done.joined), channel_id=1, source_target_pairs={{0,2},{1,3},{2,4},{3,5},{4,6},{5,7},{6,0},{7,1},{8,10},{9,11},{10,... | collective-permute-start | bytes 884744 | tf_op jit(solution)/shard_map/ppermute | solution.py:40
  51.9 3.8 %copy-start.2 = (s32[4]{0:T(128)S(1)}, s32[4]{0:T(128)}, u32[]{:S(2)}) copy-start(s32[4]{0:T(128)} %pad_add_fusion.ids) | copy-start | bytes 52
  51.9 3.8 %copy-start.4 = (s32[1,24]{1,0:T(1,128)S(1)}, s32[1,24]{1,0:T(1,128)}, u32[]{:S(2)}) copy-start(s32[1,24]{1,0:T(1,128)} %parent.1) | copy-start | bytes 292
  51.9 3.8 %copy-start.5 = (s32[1,24]{1,0:T(1,128)S(1)}, s32[1,24]{1,0:T(1,128)}, u32[]{:S(2)}) copy-start(s32[1,24]{1,0:T(1,128)} %length.1) | copy-start | bytes 292
  52.1 19.1 %collective-permute-start.6 = (bf16[4,8,144,128]{3,2,1,0:T(8,128)(2,1)S(1)}, bf16[4,8,144,128]{3,2,1,0:T(8,128)(2,1)S(1)}, u32[]{:S(2)}, u32[]{:S(2)}) collective-permute-start(bf16[4,8,144,128]{3,2,1,0:T(8,128)(2,1)S(1)} %pad_maximum_fusion.own), channel_id=1, source_target_pairs={{0,1},{1,0},{2,3},{3,2},{4,5},{5,4},{6,7},{7,6},{8,9},{9,8},{10,11... | collective-permute-start | bytes 3538952 | tf_op jit(solution)/shard_map/ppermute | solution.py:40
  55.4 15.7 %collective-permute-start.8 = (bf16[2,1088,128]{2,1,0:T(8,128)(2,1)S(1)}, bf16[2,1088,128]{2,1,0:T(8,128)(2,1)S(1)}, u32[]{:S(2)}, u32[]{:S(2)}) collective-permute-start(bf16[2,1088,128]{2,1,0:T(8,128)(2,1)S(1)} %get-tuple-element.87), channel_id=1, source_target_pairs={{0,16},{1,17},{2,18},{3,19},{4,20},{5,21},{6,22},{7,23},{8,24},{9,... | collective-permute-start | bytes 1671176 | tf_op jit(solution)/shard_map/ppermute | solution.py:40
  55.4 3.7 %collective-permute-start.7 = (bf16[32,16,128]{2,1,0:T(8,128)(2,1)S(1)}, bf16[32,16,128]{2,1,0:T(8,128)(2,1)S(1)}, u32[]{:S(2)}, u32[]{:S(2)}) collective-permute-start(bf16[32,16,128]{2,1,0:T(8,128)(2,1)S(1)} %all_to_all.20.root_own), channel_id=1, source_target_pairs={{0,1},{1,0},{2,3},{3,2},{4,5},{5,4},{6,7},{7,6},{8,9},{9,8},{10,11... | collective-permute-start | bytes 393224 | tf_op jit(solution)/shard_map/ppermute | solution.py:40
  95.1 3.5 %collective-permute-start.9 = (bf16[32,128,128]{2,1,0:T(8,128)(2,1)S(1)}, bf16[32,128,128]{2,1,0:T(8,128)(2,1)S(1)}, u32[]{:S(2)}, u32[]{:S(2)}) collective-permute-start(bf16[32,128,128]{2,1,0:T(8,128)(2,1)S(1)} %get-tuple-element.90), channel_id=1, source_target_pairs={{0,1},{1,0},{2,3},{3,2},{4,5},{5,4},{6,7},{7,6},{8,9},{9,8},{10,11... | collective-permute-start | bytes 3145736 | tf_op jit(solution)/shard_map/ppermute | solution.py:40
  96.0 2.5 %collective-permute-start.10 = (f32[32,8,128]{2,1,0:T(8,128)S(1)}, f32[32,8,128]{2,1,0:T(8,128)S(1)}, u32[]{:S(2)}, u32[]{:S(2)}) collective-permute-start(f32[32,8,128]{2,1,0:T(8,128)S(1)} %get-tuple-element.93), channel_id=1, source_target_pairs={{0,1},{1,0},{2,3},{3,2},{4,5},{5,4},{6,7},{7,6},{8,9},{9,8},{10,11... | collective-permute-start | bytes 393224 | tf_op jit(solution)/shard_map/ppermute | solution.py:40
  98.8 25.2 %collective-permute-start.11 = (bf16[2,528,128]{2,1,0:T(8,128)(2,1)S(1)}, bf16[2,528,128]{2,1,0:T(8,128)(2,1)S(1)}, u32[]{:S(2)}, u32[]{:S(2)}) collective-permute-start(bf16[2,528,128]{2,1,0:T(8,128)(2,1)S(1)} %get-tuple-element.104), channel_id=1, source_target_pairs={{0,24},{1,25},{2,26},{3,27},{4,28},{5,29},{6,30},{7,31},{8,0},{9,1... | collective-permute-start | bytes 811016 | tf_op jit(solution)/shard_map/ppermute | solution.py:40
  98.9 25.1 %collective-permute-start.12 = (bf16[2,528,128]{2,1,0:T(8,128)(2,1)S(1)}, bf16[2,528,128]{2,1,0:T(8,128)(2,1)S(1)}, u32[]{:S(2)}, u32[]{:S(2)}) collective-permute-start(bf16[2,528,128]{2,1,0:T(8,128)(2,1)S(1)} %get-tuple-element.105), channel_id=1, source_target_pairs={{0,8},{1,9},{2,10},{3,11},{4,12},{5,13},{6,14},{7,15},{8,16},{9,17... | collective-permute-start | bytes 811016 | tf_op jit(solution)/shard_map/ppermute | solution.py:40
  100.3 23.7 %collective-permute-start.13 = (bf16[8,128,128]{2,1,0:T(8,128)(2,1)S(1)}, bf16[8,128,128]{2,1,0:T(8,128)(2,1)S(1)}, u32[]{:S(2)}, u32[]{:S(2)}) collective-permute-start(bf16[8,128,128]{2,1,0:T(8,128)(2,1)S(1)} %get-tuple-element.107), channel_id=1, source_target_pairs={{0,6},{1,7},{2,0},{3,1},{4,2},{5,3},{6,4},{7,5},{8,14},{9,15},{10,... | collective-permute-start | bytes 786440 | tf_op jit(solution)/shard_map/ppermute | solution.py:40
  102.8 21.2 %collective-permute-start.14 = (bf16[8,128,128]{2,1,0:T(8,128)(2,1)S(1)}, bf16[8,128,128]{2,1,0:T(8,128)(2,1)S(1)}, u32[]{:S(2)}, u32[]{:S(2)}) collective-permute-start(bf16[8,128,128]{2,1,0:T(8,128)(2,1)S(1)} %get-tuple-element.108), channel_id=1, source_target_pairs={{0,4},{1,5},{2,6},{3,7},{4,0},{5,1},{6,2},{7,3},{8,12},{9,13},{10,... | collective-permute-start | bytes 786440 | tf_op jit(solution)/shard_map/ppermute | solution.py:40
  102.8 21.2 %collective-permute-start.15 = (bf16[8,128,128]{2,1,0:T(8,128)(2,1)S(1)}, bf16[8,128,128]{2,1,0:T(8,128)(2,1)S(1)}, u32[]{:S(2)}, u32[]{:S(2)}) collective-permute-start(bf16[8,128,128]{2,1,0:T(8,128)(2,1)S(1)} %get-tuple-element.109), channel_id=1, source_target_pairs={{0,2},{1,3},{2,4},{3,5},{4,6},{5,7},{6,0},{7,1},{8,10},{9,11},{10,... | collective-permute-start | bytes 786440 | tf_op jit(solution)/shard_map/ppermute | solution.py:40
  124.9 22.1 %all-to-all-start.3 = ((f32[8,136,128]{2,1,0:T(8,128)}), f32[8,136,128]{2,1,0:T(8,128)S(1)}, u32[]{:S(2)}, u32[]{:S(2)}) async-start(f32[8,136,128]{2,1,0:T(8,128)} %sum_pairs.1), calls=%async_computation.3 | async-start | bytes 1114112 | tf_op jit(solution)/shard_map/all_to_all | solution.py:557
  131.4 15.6 %collective-permute-start.16 = (bf16[2,528,128]{2,1,0:T(8,128)(2,1)S(1)}, bf16[2,528,128]{2,1,0:T(8,128)(2,1)S(1)}, u32[]{:S(2)}, u32[]{:S(2)}) collective-permute-start(bf16[2,528,128]{2,1,0:T(8,128)(2,1)S(1)} %get-tuple-element.116), channel_id=1, source_target_pairs={{0,16},{1,17},{2,18},{3,19},{4,20},{5,21},{6,22},{7,23},{8,24},{9,... | collective-permute-start | bytes 811016 | tf_op jit(solution)/shard_map/ppermute | solution.py:40
  147.2 2.5 %collective-permute-start.17 = (bf16[4,528,128]{2,1,0:T(8,128)(2,1)S(1)}, bf16[4,528,128]{2,1,0:T(8,128)(2,1)S(1)}, u32[]{:S(2)}, u32[]{:S(2)}) collective-permute-start(bf16[4,528,128]{2,1,0:T(8,128)(2,1)S(1)} %pad_maximum_fusion.1), channel_id=1, source_target_pairs={{0,1},{1,0},{2,3},{3,2},{4,5},{5,4},{6,7},{7,6},{8,9},{9,8},{10,11... | collective-permute-start | bytes 1622024 | tf_op jit(solution)/shard_map/ppermute | solution.py:40
where the time goes:
time: 152 us
  blocking collectives  40 us (26%)
  Pallas kernels  37.5 us (25%)
  waiting for transfers between devices  36.5 us (24%)
  starting transfers between devices  33.1 us (22%)
  local copies, waits for them, and re-layouts  2.94 us (2%)
    all_to_all x2, blocking collectives, along(): return lax.all_to_all(array, ('leaf', 'y'), 0, 0, tiled=True)  40 us
    ppermute x18, waiting for transfers between devices, shift(): return lax.ppermute(array, ('x', 'y', 'core'), perm(dx, dy, dc))  30.4 us
    pallas_call x1, Pallas kernels, compute(): pl.pallas_call(compute_kernel, in_specs=[smem()] * 3 + [vmem()] * 10, out...  23.9 us
    ppermute x18, starting transfers between devices, shift(): return lax.ppermute(array, ('x', 'y', 'core'), perm(dx, dy, dc))  20 us
    all_to_all x2, starting transfers between devices, across(): return lax.all_to_all(array, ('x', 'core'), 0, 0, tiled=True)  13.1 us
    all_to_all x2, waiting for transfers between devices, across(): return lax.all_to_all(array, ('x', 'core'), 0, 0, tiled=True)  6.18 us
    pallas_call x1, Pallas kernels, pack_rows(): pl.pallas_call(pack_rows_kernel, in_specs=[smem()] + [pl.BlockSpec(memory...  5.04 us
    pallas_call x1, Pallas kernels, make_tables(): pl.pallas_call(tables_kernel, in_specs=[smem(), smem(), smem()], out_spec...  3.48 us
  transfers between devices with their start and end apart: 20, of which 6 were waited for; matrix products, arithmetic and copies ran while one was open for 0% of the time, Pallas kernels for 3%

commit v1 on v0

--- a/solution.py
+++ b/solution.py
@@ -137,25 +137,27 @@
     )(ids, parent, length)
 
 
-def pack_pairs_kernel(pairs, root, out):
-    for c in range(2):
-        for x in range(4):
-            cols = slice(c * 512 + x * HD, c * 512 + (x + 1) * HD)
-            out[x * 2 + c, 0:BLK, :] = pairs[:, cols]
+def pack_pairs_kernel(ids, pairs, root, *outs):
+    x, c = ids[0], ids[2]
+    for k in range(4):
+        for s in range(2):
+            col = flip(c, s) * 4 + lax.rem(x + k, 4)
+            cols = pl.ds(pl.multiple_of(col * HD, HD), HD)
+            outs[k][s, 0:BLK, :] = pairs[:, cols]
             row = jnp.broadcast_to(root[:, cols].astype(F4), (16, HD))
             tail = jnp.where(iota((16, HD), 0) == 0, row, 0.0)
-            out[x * 2 + c, BLK:PAIR, :] = tail.astype(BF)
-
-
-def pack_pairs(pairs, root):
+            outs[k][s, BLK:PAIR, :] = tail.astype(BF)
+
+
+def pack_pairs(ids, pairs, root):
     return pl.pallas_call(
         pack_pairs_kernel,
-        in_specs=[vmem()] * 2,
-        out_specs=vmem(),
-        out_shape=jax.ShapeDtypeStruct((8, PAIR, HD), BF),
+        in_specs=[smem()] + [vmem()] * 2,
+        out_specs=[vmem()] * 4,
+        out_shape=[jax.ShapeDtypeStruct((2, PAIR, HD), BF)] * 4,
         compiler_params=params(),
         name="pack_pairs",
-    )(pairs, root)
+    )(ids, pairs, root)
 
 
 def split3(value):
@@ -168,21 +170,35 @@
 
 def pack_rows_kernel(ids, *refs):
     sources, keep, send, held, sems = refs[0:8], refs[8], refs[9], refs[10:18], refs[18]
-    copies = [
-        pltpu.make_async_copy(source, target, sems.at[n])
-        for n, (source, target) in enumerate(zip(sources, held))
+    x, c = ids[0], ids[2]
+
+    def target(i):
+        return lax.rem(x + i // 2, 4) * 2 + flip(c, i % 2)
+
+    small = [
+        pltpu.make_async_copy(sources[n], held[n], sems.at[8, n - 3]) for n in range(3, 8)
     ]
-    for copy in copies:
+    pieces = []
+    for i in range(8):
+        cols = pl.ds(pl.multiple_of(target(i) * 512, 512), 512)
+        pieces.append(
+            [
+                pltpu.make_async_copy(sources[n].at[:, cols], held[n].at[:, cols], sems.at[i, n])
+                for n in range(3)
+            ]
+        )
+    for copy in small + sum(pieces, []):
         copy.start()
-    for copy in copies:
+    for copy in small:
         copy.wait()
     query, output, cotangent, norm, rquery, routput, rcotangent, rnorm = held
-    x, c = ids[0], ids[2]
     norms = rnorm[...] * LOG2E
     for i in range(8):
         k, dc = i // 2, i % 2
-        dest = lax.rem(x + k, 4) * 2 + flip(c, dc)
+        dest = target(i)
         out = send if dc else keep
+        for copy in pieces[i]:
+            copy.wait()
         deltas = []
         for h in range(4):
             cols = pl.ds(pl.multiple_of(dest * 512 + h * HD, HD), HD)
@@ -226,7 +242,7 @@
         scratch_shapes=[pltpu.VMEM((BLK, 4096), BF)] * 3
         + [pltpu.VMEM((32, BLK), F4)]
         + [pltpu.VMEM((1, 4096), BF)] * 3
-        + [pltpu.VMEM((1, 32), F4), pltpu.SemaphoreType.DMA((8,))],
+        + [pltpu.VMEM((1, 32), F4), pltpu.SemaphoreType.DMA((9, 5))],
         compiler_params=params(60 * 1024 * 1024),
         name="pack_rows",
     )(ids, query, output, cotangent, norm, rquery, routput, rcotangent, rnorm)
@@ -254,24 +270,32 @@
     return wide[0:16] + wide[16:32] + wide[32:48]
 
 
-def pack_root_kernel(joined, out):
+def join_pairs_kernel(ids, g0, g1, g2, g3, crossed, out, root_out):
+    x, c = ids[0], ids[2]
     tile = jnp.zeros((16, HD), F4)
-    for block in range(8):
-        row = joined[block, BLK:PAIR, :].astype(F4)[0:1]
-        tile = jnp.where(iota((16, HD), 0) == block, jnp.broadcast_to(row, (16, HD)), tile)
+    for k, straight in enumerate((g0, g1, g2, g3)):
+        for dc in range(2):
+            block = lax.rem(x - k + 4, 4) * 2 + flip(c, dc)
+            part = crossed[k] if dc else straight[0]
+            out[block] = part[0:BLK]
+            row = jnp.broadcast_to(part[BLK:PAIR].astype(F4)[0:1], (16, HD))
+            tile = jnp.where(iota((16, HD), 0) == block, row, tile)
     for target in range(32):
-        out[target] = tile.astype(BF)
-
-
-def pack_root(joined):
-    return pl.pallas_call(
-        pack_root_kernel,
-        in_specs=[vmem()],
-        out_specs=vmem(),
-        out_shape=jax.ShapeDtypeStruct((32, 16, HD), BF),
-        compiler_params=params(),
-        name="pack_root",
-    )(joined)
+        root_out[target] = tile.astype(BF)
+
+
+def join_pairs(ids, parts, crossed):
+    return pl.pallas_call(
+        join_pairs_kernel,
+        in_specs=[smem()] + [vmem()] * 5,
+        out_specs=[vmem()] * 2,
+        out_shape=[
+            jax.ShapeDtypeStruct((8, BLK, HD), BF),
+            jax.ShapeDtypeStruct((32, 16, HD), BF),
+        ],
+        compiler_params=params(),
+        name="join_pairs",
+    )(ids, *parts, crossed)
 
 
 def place(y, ky, block):
@@ -293,10 +317,10 @@
         for ky in range(4):
             for block in range(8):
                 to = place(y, ky, block)
-                part = key_ref[ky, block, 0:BLK, :]
+                part = key_ref[ky, block]
                 keys[to] = part
                 keys_t[to] = part.astype(F4).T.astype(BF)
-                values[to] = value_ref[ky, block, 0:BLK, :]
+                values[to] = value_ref[ky, block]
 
     @pl.when(first)
     def _():
@@ -354,8 +378,8 @@
         def query_block(dc, carry):
             i = k * 2 + dc
             mine = lax.rem(x - k + 4, 4) * 8 + y * 2 + jnp.where(dc == 0, c, 1 - c)
-            anc_row = jnp.broadcast_to(qanc[pl.ds(mine, 1), :], (2 * BLK, BLK))
-            query_pos = iota((2 * BLK, BLK), 1) + mine * BLK
+            anc_row = jnp.broadcast_to(qanc[pl.ds(mine, 1), :], (BLK, BLK))
+            query_pos = iota((BLK, BLK), 1) + mine * BLK
             terms = unsplit(msg[dc, T0 : T0 + 48, :])
             norm, delta = lanes_of(terms, 0), lanes_of(terms, 4)
 
@@ -373,32 +397,31 @@
             rdv[...] = rdv[...] + dv_part
             acc[...] = dq_part
 
-            def unit(j):
-                b0, b1 = lists[i, 2 * j], lists[i, 2 * j + 1]
-                key = jnp.concatenate([keys[b0], keys[b1]], axis=0)
-                value = jnp.concatenate([values[b0], values[b1]], axis=0)
-                key_t = jnp.concatenate([keys_t[b0], keys_t[b1]], axis=1)
-                bits = jnp.concatenate([kbit[b0], kbit[b1]], axis=0)
-                key_pos = jnp.concatenate([base + b0 * BLK, base + b1 * BLK], axis=0)
-                mask = ((bits & anc_row) != 0) & (key_pos <= query_pos)
+            def unit(start, width):
+                at = [lists[i, start + n] for n in range(width)]
+                key = jnp.concatenate([keys[b] for b in at], axis=0)
+                value = jnp.concatenate([values[b] for b in at], axis=0)
+                key_t = jnp.concatenate([keys_t[b] for b in at], axis=1)
+                masks = [
+                    ((kbit[b] & anc_row) != 0) & (base + b * BLK <= query_pos) for b in at
+                ]
+                mask = jnp.concatenate(masks, axis=0)
                 dk_part, dv_part, dq_part = gradients(key, value, key_t, mask)
                 acc[...] = acc[...] + dq_part
-                dk[b0] = dk[b0] + dk_part[0:BLK]
-                dv[b0] = dv[b0] + dv_part[0:BLK]
-                dk[b1] = dk[b1] + dk_part[BLK:]
-                dv[b1] = dv[b1] + dv_part[BLK:]
-
-            def two(j, inner):
-                unit(2 * j)
-                unit(2 * j + 1)
+                for n, b in enumerate(at):
+                    dk[b] = dk[b] + dk_part[n * BLK : (n + 1) * BLK]
+                    dv[b] = dv[b] + dv_part[n * BLK : (n + 1) * BLK]
+
+            def four(j, inner):
+                unit(4 * j, 4)
                 return inner
 
             count = counts[i]
-            lax.fori_loop(0, count // 2, two, 0)
+            lax.fori_loop(0, count // 2, four, 0)
 
             @pl.when(count % 2 == 1)
             def _():
-                unit(count - 1)
+                unit(2 * count - 2, 2)
 
             for h in range(4):
                 done = acc[:, h * BLK : (h + 1) * BLK].T * FACTOR
@@ -507,42 +530,50 @@
     )(keep, other)
 
 
-def sum_pairs_kernel(stay, r1, r2, r3, roots, out):
+def sum_pairs_kernel(ids, stay, r1, r2, r3, roots, o0, o1, o2, o3, held):
+    x, c = ids[0], ids[2]
     total = roots[0]
     for n in range(1, 32):
         total = total + roots[n]
-    for block in range(8):
-        rest = r1[block].astype(F4) + r2[block].astype(F4) + r3[block].astype(F4)
-        out[block, 0:BLK, :] = stay[block] + rest
-        out[block, BLK : BLK + 8, :] = jnp.broadcast_to(total[block : block + 1], (8, HD))
-
-
-def sum_pairs(stay, received, roots):
+    held[...] = total
+    for k, out in enumerate((o0, o1, o2, o3)):
+        for dc in range(2):
+            block = lax.rem(x + k, 4) * 2 + flip(c, dc)
+            rest = r1[block].astype(F4) + r2[block].astype(F4) + r3[block].astype(F4)
+            out[dc, 0:BLK, :] = stay[block] + rest
+            row = held[pl.ds(block, 1), :]
+            out[dc, BLK : BLK + 8, :] = jnp.broadcast_to(row, (8, HD))
+
+
+def sum_pairs(ids, stay, received, roots):
     return pl.pallas_call(
         sum_pairs_kernel,
-        in_specs=[vmem()] * 5,
-        out_specs=vmem(),
-        out_shape=jax.ShapeDtypeStruct((8, BLK + 8, HD), F4),
+        in_specs=[smem()] + [vmem()] * 5,
+        out_specs=[vmem()] * 4,
+        out_shape=[jax.ShapeDtypeStruct((2, BLK + 8, HD), F4)] * 4,
+        scratch_shapes=[pltpu.VMEM((8, HD), F4)],
         compiler_params=params(),
         name="sum_pairs",
-    )(stay, *received, roots)
-
-
-def unpack_pairs_kernel(parts, out, root_out):
-    for c in range(2):
-        for x in range(4):
-            total = parts[x * 2 + c]
-            if c == 0:
-                total = total * FACTOR
-            cols = slice(c * 512 + x * HD, c * 512 + (x + 1) * HD)
-            out[:, cols] = total[0:BLK]
-            root_out[:, cols] = total[BLK : BLK + 1]
-
-
-def unpack_pairs(parts):
+    )(ids, stay, *received, roots)
+
+
+def unpack_pairs_kernel(ids, g0, g1, g2, g3, crossed, out, root_out):
+    x, c = ids[0], ids[2]
+    for k, straight in enumerate((g0, g1, g2, g3)):
+        for dc in range(2):
+            kind = flip(c, dc)
+            part = crossed[k] if dc else straight[0]
+            scale = jnp.where(kind == 0, FACTOR, 1.0).astype(F4)
+            col = kind * 512 + lax.rem(x - k + 4, 4) * HD
+            cols = pl.ds(pl.multiple_of(col, HD), HD)
+            out[:, cols] = part[0:BLK] * scale
+            root_out[:, cols] = part[BLK : BLK + 1] * scale
+
+
+def unpack_pairs(ids, parts, crossed):
     return pl.pallas_call(
         unpack_pairs_kernel,
-        in_specs=[vmem()],
+        in_specs=[smem()] + [vmem()] * 5,
         out_specs=[vmem()] * 2,
         out_shape=[
             jax.ShapeDtypeStruct((BLK, 1024), F4),
@@ -550,11 +581,7 @@
         ],
         compiler_params=params(),
         name="unpack_pairs",
-    )(parts)
-
-
-def across(array):
-    return lax.all_to_all(array, ("x", "core"), 0, 0, tiled=True)
+    )(ids, *parts, crossed)
 
 
 def along(array):
@@ -579,8 +606,8 @@
     ids = ids.astype(jnp.int32)
     together = lax.optimization_barrier
 
-    joined = across(pack_pairs(key_value_tree, key_value_root))
-    joined, ids = together((joined, ids))
+    pair_parts = pack_pairs(ids, key_value_tree, key_value_root)
+    pair_parts = [pair_parts[0]] + [shift(pair_parts[k], dx=k) for k in range(1, 4)]
     keep, send = pack_rows(
         ids,
         query_tree,
@@ -592,12 +619,16 @@
         cotangent_root,
         log_norm_root.reshape(1, 32),
     )
+    keep, send, *pair_parts = together((keep, send, *pair_parts))
+
     merged = merge_rows(keep, shift(send, dc=1))
-    joined, *merged = together((joined, *merged))
+    crossed = shift(jnp.stack([part[1] for part in pair_parts], axis=0), dc=1)
+    joined, root_rows = join_pairs(ids, pair_parts, crossed)
+    joined, root_rows, *merged = together((joined, root_rows, *merged))
 
     msg1, msg3 = shift(merged[1], dx=1), shift(merged[3], dx=3)
     own = [joined] + [shift(joined, dy=ky) for ky in range(1, 4)]
-    root_own = along(pack_root(joined))
+    root_own = along(root_rows)
     msg1, msg3, merged[2], root_own, *own = together(
         (msg1, msg3, merged[2], root_own, *own)
     )
@@ -616,19 +647,21 @@
     low, parts = rest[0:3], rest[3:7]
 
     received = [shift(low[ky - 1], dy=-ky) for ky in range(1, 4)]
-    back1, back3 = shift(parts[1], dx=-1), shift(parts[3], dx=-3)
+    back2 = shift(parts[2], dx=-2)
     roots = along(root_sums)
-    stay, roots, back1, back3, part2, *received = together(
-        (stay, roots, back1, back3, parts[2], *received)
+    stay, roots, back2, part1, part3, *received = together(
+        (stay, roots, back2, parts[1], parts[3], *received)
     )
 
-    grads = across(sum_pairs(stay, received, roots))
-    back2 = shift(part2, dx=-2)
-    grads, back2 = together((grads, back2))
+    sums = sum_pairs(ids, stay, received, roots)
+    sums = [sums[0]] + [shift(sums[k], dx=k) for k in range(1, 4)]
+    back1, back3 = shift(part1, dx=-1), shift(part3, dx=-3)
+    back1, back3, *sums = together((back1, back3, *sums))
 
     back = [parts[0], back1, back2, back3]
     crossed = shift(jnp.stack([part[1] for part in back], axis=0), dc=1)
-    grad_pairs, grad_root = unpack_pairs(grads)
+    crossed_sums = shift(jnp.stack([part[1] for part in sums], axis=0), dc=1)
+    grad_pairs, grad_root = unpack_pairs(ids, sums, crossed_sums)
     grad_query, grad_query_root = unpack_query(ids, back, crossed)
     return grad_query, grad_query_root.reshape(1, 4096), grad_pairs, grad_root
 

time: 152 us -> 137 us (0.901)
  waiting for transfers between devices: 36.5 us -> 24.8 us
  blocking collectives: 40 us -> 35.9 us
  Pallas kernels: 37.5 us -> 39.5 us
    all_to_all x2 -> x0, starting transfers between devices: 13.1 us -> none  [across(): return lax.all_to_all(array, ('x', 'core'), 0, 0, tiled=True)]
    ppermute x18 -> x26, starting transfers between devices: 20 us -> 32.2 us  [shift(): return lax.ppermute(array, ('x', 'y', 'core'), perm(dx, dy, dc))]
    all_to_all x2 -> x0, waiting for transfers between devices: 6.18 us -> none  [across(): return lax.all_to_all(array, ('x', 'core'), 0, 0, tiled=True)]
    ppermute x18 -> x26, waiting for transfers between devices: 30.4 us -> 24.8 us  [shift(): return lax.ppermute(array, ('x', 'y', 'core'), perm(dx, dy, dc))]
    all_to_all x2, blocking collectives: 40 us -> 35.9 us  [along(): return lax.all_to_all(array, ('leaf', 'y'), 0, 0, tiled=True)]
    unnamed x12 -> x16, local copies, waits for them, and re-layouts: 2.89 us -> 3.55 us
  transfers between devices with their start and end apart: 20 -> 26, of which waited for: 6 -> 6; matrix products, arithmetic and copies ran while one was open for 0% -> 0% of each run, Pallas kernels for 3% -> 8%
where the time goes in v1:
time: 137 us
  Pallas kernels  39.5 us (29%)
  blocking collectives  35.9 us (26%)
  starting transfers between devices  32.2 us (24%)
  waiting for transfers between devices  24.8 us (18%)
  local copies, waits for them, and re-layouts  3.64 us (3%)
    all_to_all x2, blocking collectives, along(): return lax.all_to_all(array, ('leaf', 'y'), 0, 0, tiled=True)  35.9 us
    ppermute x26, starting transfers between devices, shift(): return lax.ppermute(array, ('x', 'y', 'core'), perm(dx, dy, dc))  32.2 us
    ppermute x26, waiting for transfers between devices, shift(): return lax.ppermute(array, ('x', 'y', 'core'), perm(dx, dy, dc))  24.8 us
    pallas_call x1, Pallas kernels, compute(): pl.pallas_call(compute_kernel, in_specs=[smem()] * 3 + [vmem()] * 10, out...  24.8 us
    pallas_call x1, Pallas kernels, pack_rows(): pl.pallas_call(pack_rows_kernel, in_specs=[smem()] + [pl.BlockSpec(memory...  5.35 us
    pallas_call x1, Pallas kernels, make_tables(): pl.pallas_call(tables_kernel, in_specs=[smem(), smem(), smem()], out_spec...  3.66 us
    unnamed x16, local copies, waits for them, and re-layouts  3.55 us
  transfers between devices with their start and end apart: 26, of which 6 were waited for; matrix products, arithmetic and copies ran while one was open for 0% of the time, Pallas kernels for 8%

profile of v1, /device:TPU:1, one launch (start us, length us, event | category | flops | bytes accessed | tf_op | source)
XLA Modules:
  0.0 137.3 jit_solution(15560035286285267706)
XLA Ops:
  0.6 0.1 pad_add_fusion.ids
  0.7 0.9 copy-done.1
  1.7 0.7 copy-done.5
  2.4 0.6 pack_pairs.1
  3.0 2.1 %collective-permute-start = (bf16[2,144,128]{2,1,0:T(8,128)(2,1)S(1)}, bf16[2,144,128]{2,1,0:T(8,128)(2,1)S(1)}, u32[]{:S(2)}, u32[]{:S(2)}) collective-permute-start(bf16[2,144,128]{2,1,0:T(8,128)(2,1)S(1)} %get-tuple-element.90), channel_id=1, source_target_pairs={{0,8},{1,9},{2,10},{3,11},{4,12},{5,13},{6,14},{7,15},{8,16},{9,17... | collective-permute-start | bytes 221192 | tf_op jit(solution)/shard_map/ppermute | solution.py:40
  5.1 2.5 %collective-permute-start.1 = (bf16[2,144,128]{2,1,0:T(8,128)(2,1)S(1)}, bf16[2,144,128]{2,1,0:T(8,128)(2,1)S(1)}, u32[]{:S(2)}, u32[]{:S(2)}) collective-permute-start(bf16[2,144,128]{2,1,0:T(8,128)(2,1)S(1)} %get-tuple-element.91), channel_id=1, source_target_pairs={{0,16},{1,17},{2,18},{3,19},{4,20},{5,21},{6,22},{7,23},{8,24},{9,... | collective-permute-start | bytes 221192 | tf_op jit(solution)/shard_map/ppermute | solution.py:40
  7.6 1.2 collective-permute-start.2
  8.7 5.3 %pack_rows.1 = (bf16[4,1088,128]{2,1,0:T(8,128)(2,1)}, bf16[4,1088,128]{2,1,0:T(8,128)(2,1)}) custom-call(s32[4]{0:T(128)} %copy-done.2, bf16[128,4096]{1,0:T(8,128)(2,1)} %refs_0_.1, bf16[128,4096]{1,0:T(8,128)(2,1)} %refs_1_.1, bf16[128,4096]{1,0:T(8,128)(2,1)} %refs_2_.1, f32[32,128]{1,0:T(8,128)} %refs_3_.1, bf16[1,4096]{1,0:T(2,128)(2,1)} %refs_4_.1, ...), custom_call_target="tpu_custom_call" | custom-call | tf_op jit(solution)/shard_map/pack_rows/pallas_call | solution.py:237
  14.1 0.0 collective-permute-done.g1
  14.1 0.0 collective-permute-done.1.g2
  14.1 0.0 collective-permute-done.2.g3
  14.1 1.6 %collective-permute-start.4 = (bf16[4,1088,128]{2,1,0:T(8,128)(2,1)}, bf16[4,1088,128]{2,1,0:T(8,128)(2,1)S(1)}, u32[]{:S(2)}, u32[]{:S(2)}) collective-permute-start(bf16[4,1088,128]{2,1,0:T(8,128)(2,1)} %get-tuple-element.100), channel_id=1, source_target_pairs={{0,1},{1,0},{2,3},{3,2},{4,5},{5,4},{6,7},{7,6},{8,9},{9,8},{10,11... | collective-permute-start | bytes 3342344 | tf_op jit(solution)/shard_map/ppermute | solution.py:40
  15.8 0.1 collective-permute-start.3
  15.9 2.4 %collective-permute-done.3.crossed = bf16[4,144,128]{2,1,0:T(8,128)(2,1)S(1)} collective-permute-done((bf16[4,144,128]{2,1,0:T(8,128)(2,1)S(1)}, bf16[4,144,128]{2,1,0:T(8,128)(2,1)S(1)}, u32[]{:S(2)}, u32[]{:S(2)}) %collective-permute-start.3) | collective-permute-done | bytes 147488 | tf_op jit(solution)/shard_map/ppermute | solution.py:40
  18.3 0.7 copy-done.3
  19.0 0.6 join_pairs.1
  19.5 0.0 collective-permute-done.4.other
  19.5 0.0 copy-start
  19.6 1.2 copy-done
  20.8 0.1 merge_rows.1
  20.9 0.4 collective-permute-start.5
  21.3 2.4 %collective-permute-start.6 = (bf16[2,1088,128]{2,1,0:T(8,128)(2,1)S(1)}, bf16[2,1088,128]{2,1,0:T(8,128)(2,1)S(1)}, u32[]{:S(2)}, u32[]{:S(2)}) collective-permute-start(bf16[2,1088,128]{2,1,0:T(8,128)(2,1)S(1)} %get-tuple-element.106), channel_id=1, source_target_pairs={{0,24},{1,25},{2,26},{3,27},{4,28},{5,29},{6,30},{7,31},{8,0},{9,1... | collective-permute-start | bytes 1671176 | tf_op jit(solution)/shard_map/ppermute | solution.py:40
  23.7 2.7 %collective-permute-start.9 = (bf16[8,128,128]{2,1,0:T(8,128)(2,1)S(1)}, bf16[8,128,128]{2,1,0:T(8,128)(2,1)S(1)}, u32[]{:S(2)}, u32[]{:S(2)}) collective-permute-start(bf16[8,128,128]{2,1,0:T(8,128)(2,1)S(1)} %get-tuple-element.110), channel_id=1, source_target_pairs={{0,6},{1,7},{2,0},{3,1},{4,2},{5,3},{6,4},{7,5},{8,14},{9,15},{10,... | collective-permute-start | bytes 786440 | tf_op jit(solution)/shard_map/ppermute | solution.py:40
  26.4 0.3 collective-permute-start.8
  26.8 0.7 collective-permute-start.7
  27.5 19.4 %all_to_all.10.root_own = bf16[32,16,128]{2,1,0:T(8,128)(2,1)S(1)} all-to-all(bf16[32,16,128]{2,1,0:T(8,128)(2,1)S(1)} %get-tuple-element.108), channel_id=1, replica_groups=mesh['leaf'=8,'x'=4,'y'=4,'core'=2] {'leaf','y'}, dimensions={0} | all-to-all | bytes 262144 | tf_op jit(solution)/shard_map/all_to_all | solution.py:588
  46.9 0.0 collective-permute-done.9
  46.9 0.0 collective-permute-done.8
  46.9 0.0 collective-permute-done.7
  46.9 0.0 collective-permute-done.5.refs_1_
  46.9 0.1 pad_maximum_fusion.own
  47.1 3.4 %collective-permute-start.10 = (bf16[4,8,128,128]{3,2,1,0:T(8,128)(2,1)S(1)}, bf16[4,8,128,128]{3,2,1,0:T(8,128)(2,1)S(1)}, u32[]{:S(2)}, u32[]{:S(2)}) collective-permute-start(bf16[4,8,128,128]{3,2,1,0:T(8,128)(2,1)S(1)} %pad_maximum_fusion.own), channel_id=1, source_target_pairs={{0,1},{1,0},{2,3},{3,2},{4,5},{5,4},{6,7},{7,6},{8,9},{9,8},{10,11... | collective-permute-start | bytes 3145736 | tf_op jit(solution)/shard_map/ppermute | solution.py:40
  50.4 0.0 collective-permute-start.12
  50.4 0.2 collective-permute-start.11
  50.7 3.7 %tables.1 = (s32[33,128,128]{2,1,0:T(8,128)S(1)}, s32[32,128]{1,0:T(8,128)S(1)}, s32[8,40]{1,0:T(8,128)S(1)}, s32[8]{0:T(128)S(1)}) custom-call(s32[4]{0:T(128)S(1)} %copy-done.4, s32[1,24]{1,0:T(1,128)S(1)} %copy-done.6, s32[1,24]{1,0:T(1,128)S(1)} %copy-done.7), custom_call_target="tpu_custom_call" | custom-call | flops 1000000 | bytes 4000000 | tf_op jit(solution)/shard_map/tables/pallas_call | solution.py:116
  54.3 0.0 collective-permute-done.11.root_other
  54.3 11.8 %collective-permute-done.12.refs_2_ = bf16[2,1088,128]{2,1,0:T(8,128)(2,1)S(1)} collective-permute-done((bf16[2,1088,128]{2,1,0:T(8,128)(2,1)S(1)}, bf16[2,1088,128]{2,1,0:T(8,128)(2,1)S(1)}, u32[]{:S(2)}, u32[]{:S(2)}) %collective-permute-start.12) | collective-permute-done | bytes 557088 | tf_op jit(solution)/shard_map/ppermute | solution.py:40
  66.1 0.0 collective-permute-done.10.other
  66.1 24.8 %compute.1 = (bf16[2,528,128]{2,1,0:T(8,128)(2,1)S(1)}, bf16[2,528,128]{2,1,0:T(8,128)(2,1)S(1)}, bf16[2,528,128]{2,1,0:T(8,128)(2,1)S(1)}, bf16[2,528,128]{2,1,...) custom-call(s32[4]{0:T(128)S(1)} %copy-done.4, ...), custom_call_target="tpu_custom_call" | custom-call | flops 10000000000 | bytes 16000000 | tf_op jit(solution)/shard_map/compute/pallas_call | solution.py:455
  90.9 0.9 collective-permute-start.13
  91.9 0.1 collective-permute-start.14
  92.0 2.4 %collective-permute-done.14 = f32[32,8,128]{2,1,0:T(8,128)S(1)} collective-permute-done((f32[32,8,128]{2,1,0:T(8,128)S(1)}, f32[32,8,128]{2,1,0:T(8,128)S(1)}, u32[]{:S(2)}, u32[]{:S(2)}) %collective-permute-start.14) | collective-permute-done | bytes 131104 | tf_op jit(solution)/shard_map/ppermute | solution.py:40
  94.4 0.3 join_cores.1
  94.6 0.1 collective-permute-start.15
  94.8 0.8 collective-permute-start.16
  95.6 1.9 %collective-permute-start.17 = (bf16[8,128,128]{2,1,0:T(8,128)(2,1)S(1)}, bf16[8,128,128]{2,1,0:T(8,128)(2,1)S(1)}, u32[]{:S(2)}, u32[]{:S(2)}) collective-permute-start(bf16[8,128,128]{2,1,0:T(8,128)(2,1)S(1)} %get-tuple-element.138), channel_id=1, source_target_pairs={{0,4},{1,5},{2,6},{3,7},{4,0},{5,1},{6,2},{7,3},{8,12},{9,13},{10,... | collective-permute-start | bytes 786440 | tf_op jit(solution)/shard_map/ppermute | solution.py:40
  97.4 16.4 %all_to_all.11.roots = f32[32,8,128]{2,1,0:T(8,128)S(1)} all-to-all(f32[32,8,128]{2,1,0:T(8,128)S(1)} %add.3), channel_id=1, replica_groups=mesh['leaf'=8,'x'=4,'y'=4,'core'=2] {'leaf','y'}, dimensions={0} | all-to-all | bytes 262144 | tf_op jit(solution)/shard_map/all_to_all | solution.py:588
  113.9 0.0 collective-permute-done.16.r1
  113.9 0.0 collective-permute-done.17.r2
  113.9 1.4 collective-permute-start.19
  115.3 0.2 collective-permute-start.20
  115.5 0.7 sum_pairs.1
  116.1 1.2 collective-permute-start.21
  117.3 2.6 %collective-permute-start.22 = (f32[2,136,128]{2,1,0:T(8,128)S(1)}, f32[2,136,128]{2,1,0:T(8,128)S(1)}, u32[]{:S(2)}, u32[]{:S(2)}) collective-permute-start(f32[2,136,128]{2,1,0:T(8,128)S(1)} %get-tuple-element.149), channel_id=1, source_target_pairs={{0,16},{1,17},{2,18},{3,19},{4,20},{5,21},{6,22},{7,23},{8,24},{9,... | collective-permute-start | bytes 417800 | tf_op jit(solution)/shard_map/ppermute | solution.py:40
  119.9 1.2 collective-permute-start.23
  121.1 3.4 %collective-permute-done.21.g1 = f32[2,136,128]{2,1,0:T(8,128)S(1)} collective-permute-done((f32[2,136,128]{2,1,0:T(8,128)S(1)}, f32[2,136,128]{2,1,0:T(8,128)S(1)}, u32[]{:S(2)}, u32[]{:S(2)}) %collective-permute-start.21) | collective-permute-done | bytes 139296 | tf_op jit(solution)/shard_map/ppermute | solution.py:40
  124.5 3.0 %collective-permute-done.22.g2 = f32[2,136,128]{2,1,0:T(8,128)S(1)} collective-permute-done((f32[2,136,128]{2,1,0:T(8,128)S(1)}, f32[2,136,128]{2,1,0:T(8,128)S(1)}, u32[]{:S(2)}, u32[]{:S(2)}) %collective-permute-start.22) | collective-permute-done | bytes 139296 | tf_op jit(solution)/shard_map/ppermute | solution.py:40
  127.5 0.1 pad_maximum_fusion.1
  127.6 4.3 %collective-permute-start.24 = (bf16[4,528,128]{2,1,0:T(8,128)(2,1)S(1)}, bf16[4,528,128]{2,1,0:T(8,128)(2,1)S(1)}, u32[]{:S(2)}, u32[]{:S(2)}) collective-permute-start(bf16[4,528,128]{2,1,0:T(8,128)(2,1)S(1)} %pad_maximum_fusion.1), channel_id=1, source_target_pairs={{0,1},{1,0},{2,3},{3,2},{4,5},{5,4},{6,7},{7,6},{8,9},{9,8},{10,11... | collective-permute-start | bytes 1622024 | tf_op jit(solution)/shard_map/ppermute | solution.py:40
  131.9 0.1 collective-permute-start.25
  132.0 1.8 %collective-permute-done.25.crossed = f32[4,136,128]{2,1,0:T(8,128)S(1)} collective-permute-done((f32[4,136,128]{2,1,0:T(8,128)S(1)}, f32[4,136,128]{2,1,0:T(8,128)S(1)}, u32[]{:S(2)}, u32[]{:S(2)}) %collective-permute-start.25) | collective-permute-done | bytes 278560 | tf_op jit(solution)/shard_map/ppermute | solution.py:40
  133.8 1.4 %unpack_pairs.1 = (f32[128,1024]{1,0:T(8,128)}, f32[1,1024]{1,0:T(1,128)}) custom-call(s32[4]{0:T(128)S(1)} %copy-done.4, f32[2,136,128]{2,1,0:T(8,128)S(1)} %get-tuple-element.156.g0, f32[2,136,128]{2,1,0:T(8,128)S(1)} %collective-permute-done.21.g1, f32[2,136,128]{2,1,0:T(8,128)S(1)} %collective-permute-done.22.g2, ...), custom_call_target="tpu_custom_call" | custom-call | tf_op jit(solution)/shard_map/unpack_pairs/pallas_call | solution.py:574
  135.2 0.0 collective-permute-done.24.refs_4_
  135.2 2.1 %unpack_query.1 = (f32[128,4096]{1,0:T(8,128)}, f32[8,4,128]{2,1,0:T(4,128)}) custom-call(s32[4]{0:T(128)S(1)} %copy-done.4, bf16[2,528,128]{2,1,0:T(8,128)(2,1)S(1)} %get-tuple-element.131.refs_0_, bf16[2,528,128]{2,1,0:T(8,128)(2,1)S(1)} %collective-permute-done.19.refs_1_, bf16[2,528,128]{2,1,0:T(8,128)(2,1)S(1)} %collective-permute-done.15.refs_2_, ...), custom_call_target="tpu_custom_call" | custom-call | tf_op jit(solution)/shard_map/unpack_query/pallas_call | solution.py:498
  (34 shorter events, 0.2 us)
Async XLA Ops:
  0.7 1.0 copy-start.1
  1.7 0.7 copy-start.5
  2.4 6.4 %copy-start.2 = (s32[4]{0:T(128)}, s32[4]{0:T(128)S(1)}, u32[]{:S(2)}) copy-start(s32[4]{0:T(128)S(1)} %pad_add_fusion.ids) | copy-start | bytes 52
  3.0 11.1 %collective-permute-start = (bf16[2,144,128]{2,1,0:T(8,128)(2,1)S(1)}, bf16[2,144,128]{2,1,0:T(8,128)(2,1)S(1)}, u32[]{:S(2)}, u32[]{:S(2)}) collective-permute-start(bf16[2,144,128]{2,1,0:T(8,128)(2,1)S(1)} %get-tuple-element.90), channel_id=1, source_target_pairs={{0,8},{1,9},{2,10},{3,11},{4,12},{5,13},{6,14},{7,15},{8,16},{9,17... | collective-permute-start | bytes 221192 | tf_op jit(solution)/shard_map/ppermute | solution.py:40
  5.1 9.0 %collective-permute-start.1 = (bf16[2,144,128]{2,1,0:T(8,128)(2,1)S(1)}, bf16[2,144,128]{2,1,0:T(8,128)(2,1)S(1)}, u32[]{:S(2)}, u32[]{:S(2)}) collective-permute-start(bf16[2,144,128]{2,1,0:T(8,128)(2,1)S(1)} %get-tuple-element.91), channel_id=1, source_target_pairs={{0,16},{1,17},{2,18},{3,19},{4,20},{5,21},{6,22},{7,23},{8,24},{9,... | collective-permute-start | bytes 221192 | tf_op jit(solution)/shard_map/ppermute | solution.py:40
  7.6 6.5 %collective-permute-start.2 = (bf16[2,144,128]{2,1,0:T(8,128)(2,1)S(1)}, bf16[2,144,128]{2,1,0:T(8,128)(2,1)S(1)}, u32[]{:S(2)}, u32[]{:S(2)}) collective-permute-start(bf16[2,144,128]{2,1,0:T(8,128)(2,1)S(1)} %get-tuple-element.92), channel_id=1, source_target_pairs={{0,24},{1,25},{2,26},{3,27},{4,28},{5,29},{6,30},{7,31},{8,0},{9,1... | collective-permute-start | bytes 221192 | tf_op jit(solution)/shard_map/ppermute | solution.py:40
  14.1 5.4 %collective-permute-start.4 = (bf16[4,1088,128]{2,1,0:T(8,128)(2,1)}, bf16[4,1088,128]{2,1,0:T(8,128)(2,1)S(1)}, u32[]{:S(2)}, u32[]{:S(2)}) collective-permute-start(bf16[4,1088,128]{2,1,0:T(8,128)(2,1)} %get-tuple-element.100), channel_id=1, source_target_pairs={{0,1},{1,0},{2,3},{3,2},{4,5},{5,4},{6,7},{7,6},{8,9},{9,8},{10,11... | collective-permute-start | bytes 3342344 | tf_op jit(solution)/shard_map/ppermute | solution.py:40
  15.8 2.5 %collective-permute-start.3 = (bf16[4,144,128]{2,1,0:T(8,128)(2,1)S(1)}, bf16[4,144,128]{2,1,0:T(8,128)(2,1)S(1)}, u32[]{:S(2)}, u32[]{:S(2)}) collective-permute-start(bf16[4,144,128]{2,1,0:T(8,128)(2,1)S(1)} %pad_maximum_fusion.3), channel_id=1, source_target_pairs={{0,1},{1,0},{2,3},{3,2},{4,5},{5,4},{6,7},{7,6},{8,9},{9,8},{10,11... | collective-permute-start | bytes 442376 | tf_op jit(solution)/shard_map/ppermute | solution.py:40
  18.3 0.7 copy-start.3
  19.5 1.3 copy-start
  20.8 29.9 %copy-start.4 = (s32[4]{0:T(128)S(1)}, s32[4]{0:T(128)}, u32[]{:S(2)}) copy-start(s32[4]{0:T(128)} %copy-done.2) | copy-start | bytes 52
  20.8 29.9 %copy-start.6 = (s32[1,24]{1,0:T(1,128)S(1)}, s32[1,24]{1,0:T(1,128)}, u32[]{:S(2)}) copy-start(s32[1,24]{1,0:T(1,128)} %parent.1) | copy-start | bytes 292
  20.8 29.9 %copy-start.7 = (s32[1,24]{1,0:T(1,128)S(1)}, s32[1,24]{1,0:T(1,128)}, u32[]{:S(2)}) copy-start(s32[1,24]{1,0:T(1,128)} %length.1) | copy-start | bytes 292
  20.9 26.0 %collective-permute-start.5 = (bf16[2,1088,128]{2,1,0:T(8,128)(2,1)S(1)}, bf16[2,1088,128]{2,1,0:T(8,128)(2,1)S(1)}, u32[]{:S(2)}, u32[]{:S(2)}) collective-permute-start(bf16[2,1088,128]{2,1,0:T(8,128)(2,1)S(1)} %get-tuple-element.105), channel_id=1, source_target_pairs={{0,8},{1,9},{2,10},{3,11},{4,12},{5,13},{6,14},{7,15},{8,16},{9,17... | collective-permute-start | bytes 1671176 | tf_op jit(solution)/shard_map/ppermute | solution.py:40
  21.3 25.6 %collective-permute-start.6 = (bf16[2,1088,128]{2,1,0:T(8,128)(2,1)S(1)}, bf16[2,1088,128]{2,1,0:T(8,128)(2,1)S(1)}, u32[]{:S(2)}, u32[]{:S(2)}) collective-permute-start(bf16[2,1088,128]{2,1,0:T(8,128)(2,1)S(1)} %get-tuple-element.106), channel_id=1, source_target_pairs={{0,24},{1,25},{2,26},{3,27},{4,28},{5,29},{6,30},{7,31},{8,0},{9,1... | collective-permute-start | bytes 1671176 | tf_op jit(solution)/shard_map/ppermute | solution.py:40
  23.7 23.2 %collective-permute-start.9 = (bf16[8,128,128]{2,1,0:T(8,128)(2,1)S(1)}, bf16[8,128,128]{2,1,0:T(8,128)(2,1)S(1)}, u32[]{:S(2)}, u32[]{:S(2)}) collective-permute-start(bf16[8,128,128]{2,1,0:T(8,128)(2,1)S(1)} %get-tuple-element.110), channel_id=1, source_target_pairs={{0,6},{1,7},{2,0},{3,1},{4,2},{5,3},{6,4},{7,5},{8,14},{9,15},{10,... | collective-permute-start | bytes 786440 | tf_op jit(solution)/shard_map/ppermute | solution.py:40
  26.4 20.5 %collective-permute-start.8 = (bf16[8,128,128]{2,1,0:T(8,128)(2,1)S(1)}, bf16[8,128,128]{2,1,0:T(8,128)(2,1)S(1)}, u32[]{:S(2)}, u32[]{:S(2)}) collective-permute-start(bf16[8,128,128]{2,1,0:T(8,128)(2,1)S(1)} %get-tuple-element.110), channel_id=1, source_target_pairs={{0,4},{1,5},{2,6},{3,7},{4,0},{5,1},{6,2},{7,3},{8,12},{9,13},{10,... | collective-permute-start | bytes 786440 | tf_op jit(solution)/shard_map/ppermute | solution.py:40
  26.8 20.1 %collective-permute-start.7 = (bf16[8,128,128]{2,1,0:T(8,128)(2,1)S(1)}, bf16[8,128,128]{2,1,0:T(8,128)(2,1)S(1)}, u32[]{:S(2)}, u32[]{:S(2)}) collective-permute-start(bf16[8,128,128]{2,1,0:T(8,128)(2,1)S(1)} %get-tuple-element.110), channel_id=1, source_target_pairs={{0,2},{1,3},{2,4},{3,5},{4,6},{5,7},{6,0},{7,1},{8,10},{9,11},{10,... | collective-permute-start | bytes 786440 | tf_op jit(solution)/shard_map/ppermute | solution.py:40
  47.1 19.1 %collective-permute-start.10 = (bf16[4,8,128,128]{3,2,1,0:T(8,128)(2,1)S(1)}, bf16[4,8,128,128]{3,2,1,0:T(8,128)(2,1)S(1)}, u32[]{:S(2)}, u32[]{:S(2)}) collective-permute-start(bf16[4,8,128,128]{3,2,1,0:T(8,128)(2,1)S(1)} %pad_maximum_fusion.own), channel_id=1, source_target_pairs={{0,1},{1,0},{2,3},{3,2},{4,5},{5,4},{6,7},{7,6},{8,9},{9,8},{10,11... | collective-permute-start | bytes 3145736 | tf_op jit(solution)/shard_map/ppermute | solution.py:40
  50.4 15.7 %collective-permute-start.12 = (bf16[2,1088,128]{2,1,0:T(8,128)(2,1)S(1)}, bf16[2,1088,128]{2,1,0:T(8,128)(2,1)S(1)}, u32[]{:S(2)}, u32[]{:S(2)}) collective-permute-start(bf16[2,1088,128]{2,1,0:T(8,128)(2,1)S(1)} %get-tuple-element.117), channel_id=1, source_target_pairs={{0,16},{1,17},{2,18},{3,19},{4,20},{5,21},{6,22},{7,23},{8,24},{9,... | collective-permute-start | bytes 1671176 | tf_op jit(solution)/shard_map/ppermute | solution.py:40
  50.4 3.9 %collective-permute-start.11 = (bf16[32,16,128]{2,1,0:T(8,128)(2,1)S(1)}, bf16[32,16,128]{2,1,0:T(8,128)(2,1)S(1)}, u32[]{:S(2)}, u32[]{:S(2)}) collective-permute-start(bf16[32,16,128]{2,1,0:T(8,128)(2,1)S(1)} %all_to_all.10.root_own), channel_id=1, source_target_pairs={{0,1},{1,0},{2,3},{3,2},{4,5},{5,4},{6,7},{7,6},{8,9},{9,8},{10,11... | collective-permute-start | bytes 393224 | tf_op jit(solution)/shard_map/ppermute | solution.py:40
  90.9 3.4 %collective-permute-start.13 = (bf16[32,128,128]{2,1,0:T(8,128)(2,1)S(1)}, bf16[32,128,128]{2,1,0:T(8,128)(2,1)S(1)}, u32[]{:S(2)}, u32[]{:S(2)}) collective-permute-start(bf16[32,128,128]{2,1,0:T(8,128)(2,1)S(1)} %get-tuple-element.120), channel_id=1, source_target_pairs={{0,1},{1,0},{2,3},{3,2},{4,5},{5,4},{6,7},{7,6},{8,9},{9,8},{10,11... | collective-permute-start | bytes 3145736 | tf_op jit(solution)/shard_map/ppermute | solution.py:40
  91.9 2.5 %collective-permute-start.14 = (f32[32,8,128]{2,1,0:T(8,128)S(1)}, f32[32,8,128]{2,1,0:T(8,128)S(1)}, u32[]{:S(2)}, u32[]{:S(2)}) collective-permute-start(f32[32,8,128]{2,1,0:T(8,128)S(1)} %get-tuple-element.123), channel_id=1, source_target_pairs={{0,1},{1,0},{2,3},{3,2},{4,5},{5,4},{6,7},{7,6},{8,9},{9,8},{10,11... | collective-permute-start | bytes 393224 | tf_op jit(solution)/shard_map/ppermute | solution.py:40
  94.6 19.3 %collective-permute-start.15 = (bf16[2,528,128]{2,1,0:T(8,128)(2,1)S(1)}, bf16[2,528,128]{2,1,0:T(8,128)(2,1)S(1)}, u32[]{:S(2)}, u32[]{:S(2)}) collective-permute-start(bf16[2,528,128]{2,1,0:T(8,128)(2,1)S(1)} %get-tuple-element.134), channel_id=1, source_target_pairs={{0,16},{1,17},{2,18},{3,19},{4,20},{5,21},{6,22},{7,23},{8,24},{9,... | collective-permute-start | bytes 811016 | tf_op jit(solution)/shard_map/ppermute | solution.py:40
  94.8 19.1 %collective-permute-start.16 = (bf16[8,128,128]{2,1,0:T(8,128)(2,1)S(1)}, bf16[8,128,128]{2,1,0:T(8,128)(2,1)S(1)}, u32[]{:S(2)}, u32[]{:S(2)}) collective-permute-start(bf16[8,128,128]{2,1,0:T(8,128)(2,1)S(1)} %get-tuple-element.137), channel_id=1, source_target_pairs={{0,6},{1,7},{2,0},{3,1},{4,2},{5,3},{6,4},{7,5},{8,14},{9,15},{10,... | collective-permute-start | bytes 786440 | tf_op jit(solution)/shard_map/ppermute | solution.py:40
  95.6 18.3 %collective-permute-start.17 = (bf16[8,128,128]{2,1,0:T(8,128)(2,1)S(1)}, bf16[8,128,128]{2,1,0:T(8,128)(2,1)S(1)}, u32[]{:S(2)}, u32[]{:S(2)}) collective-permute-start(bf16[8,128,128]{2,1,0:T(8,128)(2,1)S(1)} %get-tuple-element.138), channel_id=1, source_target_pairs={{0,4},{1,5},{2,6},{3,7},{4,0},{5,1},{6,2},{7,3},{8,12},{9,13},{10,... | collective-permute-start | bytes 786440 | tf_op jit(solution)/shard_map/ppermute | solution.py:40
  97.4 16.5 %collective-permute-start.18 = (bf16[8,128,128]{2,1,0:T(8,128)(2,1)S(1)}, bf16[8,128,128]{2,1,0:T(8,128)(2,1)S(1)}, u32[]{:S(2)}, u32[]{:S(2)}) collective-permute-start(bf16[8,128,128]{2,1,0:T(8,128)(2,1)S(1)} %get-tuple-element.139), channel_id=1, source_target_pairs={{0,2},{1,3},{2,4},{3,5},{4,6},{5,7},{6,0},{7,1},{8,10},{9,11},{10,... | collective-permute-start | bytes 786440 | tf_op jit(solution)/shard_map/ppermute | solution.py:40
  113.9 13.5 %collective-permute-start.19 = (bf16[2,528,128]{2,1,0:T(8,128)(2,1)S(1)}, bf16[2,528,128]{2,1,0:T(8,128)(2,1)S(1)}, u32[]{:S(2)}, u32[]{:S(2)}) collective-permute-start(bf16[2,528,128]{2,1,0:T(8,128)(2,1)S(1)} %get-tuple-element.140), channel_id=1, source_target_pairs={{0,24},{1,25},{2,26},{3,27},{4,28},{5,29},{6,30},{7,31},{8,0},{9,1... | collective-permute-start | bytes 811016 | tf_op jit(solution)/shard_map/ppermute | solution.py:40
  115.3 12.2 %collective-permute-start.20 = (bf16[2,528,128]{2,1,0:T(8,128)(2,1)S(1)}, bf16[2,528,128]{2,1,0:T(8,128)(2,1)S(1)}, u32[]{:S(2)}, u32[]{:S(2)}) collective-permute-start(bf16[2,528,128]{2,1,0:T(8,128)(2,1)S(1)} %get-tuple-element.141), channel_id=1, source_target_pairs={{0,8},{1,9},{2,10},{3,11},{4,12},{5,13},{6,14},{7,15},{8,16},{9,17... | collective-permute-start | bytes 811016 | tf_op jit(solution)/shard_map/ppermute | solution.py:40
  116.1 8.4 %collective-permute-start.21 = (f32[2,136,128]{2,1,0:T(8,128)S(1)}, f32[2,136,128]{2,1,0:T(8,128)S(1)}, u32[]{:S(2)}, u32[]{:S(2)}) collective-permute-start(f32[2,136,128]{2,1,0:T(8,128)S(1)} %get-tuple-element.148), channel_id=1, source_target_pairs={{0,8},{1,9},{2,10},{3,11},{4,12},{5,13},{6,14},{7,15},{8,16},{9,17... | collective-permute-start | bytes 417800 | tf_op jit(solution)/shard_map/ppermute | solution.py:40
  117.3 10.2 %collective-permute-start.22 = (f32[2,136,128]{2,1,0:T(8,128)S(1)}, f32[2,136,128]{2,1,0:T(8,128)S(1)}, u32[]{:S(2)}, u32[]{:S(2)}) collective-permute-start(f32[2,136,128]{2,1,0:T(8,128)S(1)} %get-tuple-element.149), channel_id=1, source_target_pairs={{0,16},{1,17},{2,18},{3,19},{4,20},{5,21},{6,22},{7,23},{8,24},{9,... | collective-permute-start | bytes 417800 | tf_op jit(solution)/shard_map/ppermute | solution.py:40
  119.9 7.6 %collective-permute-start.23 = (f32[2,136,128]{2,1,0:T(8,128)S(1)}, f32[2,136,128]{2,1,0:T(8,128)S(1)}, u32[]{:S(2)}, u32[]{:S(2)}) collective-permute-start(f32[2,136,128]{2,1,0:T(8,128)S(1)} %get-tuple-element.150), channel_id=1, source_target_pairs={{0,24},{1,25},{2,26},{3,27},{4,28},{5,29},{6,30},{7,31},{8,0},{9,1... | collective-permute-start | bytes 417800 | tf_op jit(solution)/shard_map/ppermute | solution.py:40
  127.6 7.6 %collective-permute-start.24 = (bf16[4,528,128]{2,1,0:T(8,128)(2,1)S(1)}, bf16[4,528,128]{2,1,0:T(8,128)(2,1)S(1)}, u32[]{:S(2)}, u32[]{:S(2)}) collective-permute-start(bf16[4,528,128]{2,1,0:T(8,128)(2,1)S(1)} %pad_maximum_fusion.1), channel_id=1, source_target_pairs={{0,1},{1,0},{2,3},{3,2},{4,5},{5,4},{6,7},{7,6},{8,9},{9,8},{10,11... | collective-permute-start | bytes 1622024 | tf_op jit(solution)/shard_map/ppermute | solution.py:40
  131.9 1.9 %collective-permute-start.25 = (f32[4,136,128]{2,1,0:T(8,128)S(1)}, f32[4,136,128]{2,1,0:T(8,128)S(1)}, u32[]{:S(2)}, u32[]{:S(2)}) collective-permute-start(f32[4,136,128]{2,1,0:T(8,128)S(1)} %pad_maximum_fusion.2), channel_id=1, source_target_pairs={{0,1},{1,0},{2,3},{3,2},{4,5},{5,4},{6,7},{7,6},{8,9},{9,8},{10,11... | collective-permute-start | bytes 835592 | tf_op jit(solution)/shard_map/ppermute | solution.py:40

commit v2 on v1

--- a/solution.py
+++ b/solution.py
@@ -11,7 +11,10 @@
 HD = 128
 NODES = 24
 BLK = 128
+ROOT_BIT = 1 << 24
 TREE_BLOCKS = 32
+ALL_BLOCKS = 35
+ROOT_BLOCK = 33
 FACTOR = HD ** (-0.5)
 LOG2E = math.log2(math.e)
 SCALE2 = FACTOR * LOG2E
@@ -87,27 +90,31 @@
 
         lax.fori_loop(first, last + 1, mark, 0)
     positions = iota((TREE_BLOCKS, BLK), 0) * BLK + iota((TREE_BLOCKS, BLK), 1)
-    table = jnp.zeros((TREE_BLOCKS, BLK), jnp.int32)
+    table = jnp.full((TREE_BLOCKS, BLK), ROOT_BIT, jnp.int32)
     own_bits = jnp.zeros((TREE_BLOCKS, BLK), jnp.int32)
     for n in range(NODES):
         inside = positions >= start[n]
-        table = jnp.where(inside, anc[n], table)
+        table = jnp.where(inside, anc[n] | ROOT_BIT, table)
         own_bits = jnp.where(inside, jnp.int32(1 << n), own_bits)
     qanc[...] = table
     for block in range(TREE_BLOCKS):
         row = jnp.broadcast_to(own_bits[block : block + 1, :], (BLK, BLK))
         kbit[block] = row.T
     kbit[TREE_BLOCKS] = jnp.zeros((BLK, BLK), jnp.int32)
+    for block in range(ROOT_BLOCK, ALL_BLOCKS):
+        kbit[block] = jnp.full((BLK, BLK), ROOT_BIT, jnp.int32)
     for i in range(8):
         mine = (lax.rem(x - i // 2 + 4, 4)) * 8 + y * 2 + flip(c, i % 2)
         seen = qmask[mine]
+        lists[i, 0] = ROOT_BLOCK
+        lists[i, 1] = ROOT_BLOCK + 1
 
         def scan(block, found):
             hit = (seen & kmask[block]) != 0
             lists[i, found] = block
             return found + hit.astype(jnp.int32)
 
-        found = lax.fori_loop(0, mine + 1, scan, jnp.int32(0))
+        found = lax.fori_loop(0, mine + 1, scan, jnp.int32(2))
         lists[i, found] = TREE_BLOCKS
         counts[i] = (found + 1) // 2
 
@@ -118,7 +125,7 @@
         in_specs=[smem(), smem(), smem()],
         out_specs=[vmem(), vmem(), smem(), smem()],
         out_shape=[
-            jax.ShapeDtypeStruct((TREE_BLOCKS + 1, BLK, BLK), jnp.int32),
+            jax.ShapeDtypeStruct((ALL_BLOCKS, BLK, BLK), jnp.int32),
             jax.ShapeDtypeStruct((TREE_BLOCKS, BLK), jnp.int32),
             jax.ShapeDtypeStruct((8, 40), jnp.int32),
             jax.ShapeDtypeStruct((8,), jnp.int32),
@@ -169,7 +176,15 @@
 
 
 def pack_rows_kernel(ids, *refs):
-    sources, keep, send, held, sems = refs[0:8], refs[8], refs[9], refs[10:18], refs[18]
+    sources, keep, send, held, stage, sems = (
+        refs[0:8],
+        refs[8],
+        refs[9],
+        refs[10:18],
+        refs[18],
+        refs[19],
+    )
+    written = []
     x, c = ids[0], ids[2]
 
     def target(i):
@@ -196,15 +211,14 @@
     for i in range(8):
         k, dc = i // 2, i % 2
         dest = target(i)
-        out = send if dc else keep
         for copy in pieces[i]:
             copy.wait()
         deltas = []
         for h in range(4):
             cols = pl.ds(pl.multiple_of(dest * 512 + h * HD, HD), HD)
-            out[k, Q0 + h * BLK : Q0 + (h + 1) * BLK, :] = query[:, cols]
+            stage[i, Q0 + h * BLK : Q0 + (h + 1) * BLK, :] = query[:, cols]
             grad = cotangent[:, cols]
-            out[k, D0 + h * BLK : D0 + (h + 1) * BLK, :] = grad
+            stage[i, D0 + h * BLK : D0 + (h + 1) * BLK, :] = grad
             product = grad.astype(F4) * output[:, cols].astype(F4)
             deltas.append(jnp.sum(product.T, axis=0, keepdims=True))
         lane = iota((1, HD), 1)
@@ -228,21 +242,30 @@
             + [rnorm_row, rdelta_row, jnp.zeros((6, HD), F4)],
             axis=0,
         )
-        out[k, T0 : T0 + 48, :] = split3(rows)
+        stage[i, T0 : T0 + 48, :] = split3(rows)
         tile = jnp.concatenate(rquery_rows + rgrad_rows + [jnp.zeros((8, HD), F4)], axis=0)
-        out[k, R0 : R0 + 16, :] = tile.astype(BF)
+        stage[i, R0 : R0 + 16, :] = tile.astype(BF)
+        home = (send if dc else keep).at[k]
+        written.append(pltpu.make_async_copy(stage.at[i], home, sems.at[i, 3]))
+        written[-1].start()
+    for copy in written:
+        copy.wait()
 
 
 def pack_rows(ids, query, output, cotangent, norm, rquery, routput, rcotangent, rnorm):
     return pl.pallas_call(
         pack_rows_kernel,
         in_specs=[smem()] + [pl.BlockSpec(memory_space=pl.ANY)] * 8,
-        out_specs=[vmem()] * 2,
+        out_specs=[pl.BlockSpec(memory_space=pl.ANY)] * 2,
         out_shape=[jax.ShapeDtypeStruct((4, MSG, HD), BF)] * 2,
         scratch_shapes=[pltpu.VMEM((BLK, 4096), BF)] * 3
         + [pltpu.VMEM((32, BLK), F4)]
         + [pltpu.VMEM((1, 4096), BF)] * 3
-        + [pltpu.VMEM((1, 32), F4), pltpu.SemaphoreType.DMA((9, 5))],
+        + [
+            pltpu.VMEM((1, 32), F4),
+            pltpu.VMEM((8, MSG, HD), BF),
+            pltpu.SemaphoreType.DMA((9, 5)),
+        ],
         compiler_params=params(60 * 1024 * 1024),
         name="pack_rows",
     )(ids, query, output, cotangent, norm, rquery, routput, rcotangent, rnorm)
@@ -309,7 +332,7 @@
 def compute_kernel(ids, lists, counts, kbit, qanc, own, other, root_own, root_other, *refs):
     msgs, outs, refs = refs[0:4], refs[4:8], refs[8:]
     keep, send, root_keep, root_send, refs = *refs[0:4], refs[4:]
-    keys, values, keys_t, root_rows, acc, dk, dv, rkey, rvalue, rkey_t, rdk, rdv = refs
+    keys, values, keys_t, root_rows, acc, dk, dv = refs
     x, y, c, z = ids[0], ids[1], ids[2], ids[3]
     first = c == 0
 
@@ -339,9 +362,13 @@
     rows_own = root_own[...].astype(F4)[:, 0:8, :].reshape(256, HD)
     rows_other = root_other[...].astype(F4)[:, 0:8, :].reshape(256, HD)
     key_wide = jnp.where(first, rows_own, rows_other)
-    rvalue[...] = jnp.where(first, rows_other, rows_own).astype(BF)
-    rkey_t[...] = key_wide.T.astype(BF)
-    rkey[...] = key_wide.astype(BF)
+    rkey, rkey_t = key_wide.astype(BF), key_wide.T.astype(BF)
+    rvalue = jnp.where(first, rows_other, rows_own).astype(BF)
+    for n in range(2):
+        rows = slice(n * BLK, (n + 1) * BLK)
+        keys[ROOT_BLOCK + n] = rkey[rows]
+        values[ROOT_BLOCK + n] = rvalue[rows]
+        keys_t[ROOT_BLOCK + n] = rkey_t[:, rows]
 
     root_rows[...] = jnp.zeros(root_rows.shape, F4)
     special = jnp.zeros((16, HD), F4)
@@ -361,11 +388,11 @@
     at = row // 8
     root_key_pos = (at // 4) * 32 + (row % 8 // 2) * 8 + (at % 4) * 2 + row % 2
     mask = (lane < 32) & (root_key_pos <= root_query_pos)
-    prob = jnp.where(mask, jnp.exp2(nt(rkey[...], query) * SCALE2 - special[8:9, :]), 0.0)
-    dscore = (prob * (nt(rvalue[...], grad) - special[9:10, :])).astype(BF)
-    rdv[...] = nn(prob.astype(BF), grad)
-    rdk[...] = nn(dscore, query)
-    root_dq = nn(rkey_t[...], dscore).T * FACTOR
+    prob = jnp.where(mask, jnp.exp2(nt(rkey, query) * SCALE2 - special[8:9, :]), 0.0)
+    dscore = (prob * (nt(rvalue, grad) - special[9:10, :])).astype(BF)
+    dv[ROOT_BLOCK : ROOT_BLOCK + 2] = nn(prob.astype(BF), grad).reshape(2, BLK, HD)
+    dk[ROOT_BLOCK : ROOT_BLOCK + 2] = nn(dscore, query).reshape(2, BLK, HD)
+    root_dq = nn(rkey_t, dscore).T * FACTOR
 
     pad = jnp.zeros((12, HD), F4)
     base = iota((BLK, BLK), 0)
@@ -387,15 +414,14 @@
                 query = msg[dc, Q0 : Q0 + 512, :]
                 grad = msg[dc, D0 : D0 + 512, :]
                 prob = jnp.exp2(nt(key, query) * SCALE2 - norm)
-                if mask is not None:
-                    prob = jnp.where(jnp.concatenate([mask] * 4, axis=1), prob, 0.0)
+                prob = jnp.where(jnp.concatenate([mask] * 4, axis=1), prob, 0.0)
                 dscore = (prob * (nt(value, grad) - delta)).astype(BF)
                 return nn(dscore, query), nn(prob.astype(BF), grad), nn(key_t, dscore)
 
-            dk_part, dv_part, dq_part = gradients(rkey[...], rvalue[...], rkey_t[...], None)
-            rdk[...] = rdk[...] + dk_part
-            rdv[...] = rdv[...] + dv_part
-            acc[...] = dq_part
+            acc[...] = jnp.zeros(acc.shape, F4)
+
+            def position(block):
+                return jnp.where(block < ROOT_BLOCK, block, -2) * BLK
 
             def unit(start, width):
                 at = [lists[i, start + n] for n in range(width)]
@@ -403,7 +429,7 @@
                 value = jnp.concatenate([values[b] for b in at], axis=0)
                 key_t = jnp.concatenate([keys_t[b] for b in at], axis=1)
                 masks = [
-                    ((kbit[b] & anc_row) != 0) & (base + b * BLK <= query_pos) for b in at
+                    ((kbit[b] & anc_row) != 0) & (base + position(b) <= query_pos) for b in at
                 ]
                 mask = jnp.concatenate(masks, axis=0)
                 dk_part, dv_part, dq_part = gradients(key, value, key_t, mask)
@@ -430,28 +456,29 @@
 
         lax.fori_loop(0, 2, query_block, 0)
 
-    def store(keep_from, send_from, root_keep_from, root_send_from):
+    def store(keep_from, send_from):
         for ky in range(4):
             for block in range(8):
                 at = place(y, ky, block)
                 keep[ky * 8 + block] = keep_from[at]
                 send[ky * 8 + block] = send_from[at].astype(BF)
-        root_keep[...] = root_keep_from[...].reshape(32, 8, HD)
-        root_send[...] = root_send_from[...].reshape(32, 8, HD)
+        rows = slice(ROOT_BLOCK, ROOT_BLOCK + 2)
+        root_keep[...] = keep_from[rows].reshape(32, 8, HD)
+        root_send[...] = send_from[rows].reshape(32, 8, HD)
 
     @pl.when(first)
     def _():
-        store(dk, dv, rdk, rdv)
+        store(dk, dv)
 
     @pl.when(c != 0)
     def _():
-        store(dv, dk, rdv, rdk)
+        store(dv, dk)
 
 
 def compute(ids, lists, counts, kbit, qanc, own, other, root_own, root_other, msgs):
     half = (TREE_BLOCKS, BLK, HD)
-    blocks = pltpu.VMEM((TREE_BLOCKS + 1, BLK, HD), BF)
-    sums = pltpu.VMEM((TREE_BLOCKS + 1, BLK, HD), F4)
+    blocks = pltpu.VMEM((ALL_BLOCKS, BLK, HD), BF)
+    sums = pltpu.VMEM((ALL_BLOCKS, BLK, HD), F4)
     return pl.pallas_call(
         compute_kernel,
         in_specs=[smem()] * 3 + [vmem()] * 10,
@@ -467,11 +494,6 @@
             pltpu.VMEM((HD, 512), F4),
             sums,
             sums,
-            pltpu.VMEM((256, HD), BF),
-            pltpu.VMEM((256, HD), BF),
-            pltpu.VMEM((HD, 256), BF),
-            pltpu.VMEM((256, HD), F4),
-            pltpu.VMEM((256, HD), F4),
         ],
         compiler_params=params(32 * 1024 * 1024),
         cost_estimate=pl.CostEstimate(
@@ -479,33 +501,6 @@
         ),
         name="compute",
     )(ids, lists, counts, kbit, qanc, own, other, root_own, root_other, *msgs)
-
-
-def unpack_query_kernel(ids, *refs):
-    x, c = ids[0], ids[2]
-    straight, crossed, out, root_out = refs[0:4], refs[4], refs[5], refs[6]
-    for i in range(8):
-        k, dc = i // 2, i % 2
-        dest = lax.rem(x + k, 4) * 2 + flip(c, dc)
-        part = crossed[k] if dc else straight[k][0]
-        for h in range(4):
-            cols = pl.ds(pl.multiple_of(dest * 512 + h * HD, HD), HD)
-            out[:, cols] = part[h * BLK : (h + 1) * BLK, :].astype(F4)
-        root_out[dest] = part[512:528, :].astype(F4)[0:4]
-
-
-def unpack_query(ids, parts, crossed):
-    return pl.pallas_call(
-        unpack_query_kernel,
-        in_specs=[smem()] + [vmem()] * 5,
-        out_specs=[vmem()] * 2,
-        out_shape=[
-            jax.ShapeDtypeStruct((BLK, 4096), F4),
-            jax.ShapeDtypeStruct((8, 4, HD), F4),
-        ],
-        compiler_params=params(),
-        name="unpack_query",
-    )(ids, *parts, crossed)
 
 
 def join_cores_kernel(keep, other, stay, *outs):
@@ -557,31 +552,56 @@
     )(ids, stay, *received, roots)
 
 
-def unpack_pairs_kernel(ids, g0, g1, g2, g3, crossed, out, root_out):
+def unpack_kernel(ids, *refs):
     x, c = ids[0], ids[2]
-    for k, straight in enumerate((g0, g1, g2, g3)):
+    back, crossed, sums, crossed_sums = refs[0:4], refs[4], refs[5:9], refs[9]
+    out, root_out, pair_out, root_pair_out, held, pairs, sems = refs[10:]
+    for k in range(4):
         for dc in range(2):
             kind = flip(c, dc)
-            part = crossed[k] if dc else straight[0]
+            part = crossed_sums[k] if dc else sums[k][0]
             scale = jnp.where(kind == 0, FACTOR, 1.0).astype(F4)
             col = kind * 512 + lax.rem(x - k + 4, 4) * HD
             cols = pl.ds(pl.multiple_of(col, HD), HD)
-            out[:, cols] = part[0:BLK] * scale
-            root_out[:, cols] = part[BLK : BLK + 1] * scale
-
-
-def unpack_pairs(ids, parts, crossed):
-    return pl.pallas_call(
-        unpack_pairs_kernel,
-        in_specs=[smem()] + [vmem()] * 5,
-        out_specs=[vmem()] * 2,
+            pairs[:, cols] = part[0:BLK] * scale
+            root_pair_out[:, cols] = part[BLK : BLK + 1] * scale
+    copies = [pltpu.make_async_copy(pairs, pair_out, sems.at[8])]
+    copies[0].start()
+    for i in range(8):
+        k, dc = i // 2, i % 2
+        dest = lax.rem(x + k, 4) * 2 + flip(c, dc)
+        part = crossed[k] if dc else back[k][0]
+        for h in range(4):
+            cols = pl.ds(pl.multiple_of(dest * 512 + h * HD, HD), HD)
+            held[:, cols] = part[h * BLK : (h + 1) * BLK, :].astype(F4)
+        root_out[dest] = part[512:528, :].astype(F4)[0:4]
+        cols = pl.ds(pl.multiple_of(dest * 512, 512), 512)
+        copies.append(pltpu.make_async_copy(held.at[:, cols], out.at[:, cols], sems.at[i]))
+        copies[-1].start()
+    for copy in copies:
+        copy.wait()
+
+
+def unpack(ids, back, crossed, sums, crossed_sums):
+    anywhere = pl.BlockSpec(memory_space=pl.ANY)
+    return pl.pallas_call(
+        unpack_kernel,
+        in_specs=[smem()] + [vmem()] * 10,
+        out_specs=[anywhere, vmem(), anywhere, vmem()],
         out_shape=[
+            jax.ShapeDtypeStruct((BLK, 4096), F4),
+            jax.ShapeDtypeStruct((8, 4, HD), F4),
             jax.ShapeDtypeStruct((BLK, 1024), F4),
             jax.ShapeDtypeStruct((1, 1024), F4),
         ],
+        scratch_shapes=[
+            pltpu.VMEM((BLK, 4096), F4),
+            pltpu.VMEM((BLK, 1024), F4),
+            pltpu.SemaphoreType.DMA((9,)),
+        ],
         compiler_params=params(),
-        name="unpack_pairs",
-    )(ids, *parts, crossed)
+        name="unpack",
+    )(ids, *back, crossed, *sums, crossed_sums)
 
 
 def along(array):
@@ -626,14 +646,14 @@
     joined, root_rows = join_pairs(ids, pair_parts, crossed)
     joined, root_rows, *merged = together((joined, root_rows, *merged))
 
-    msg1, msg3 = shift(merged[1], dx=1), shift(merged[3], dx=3)
+    msg2 = shift(merged[2], dx=2)
     own = [joined] + [shift(joined, dy=ky) for ky in range(1, 4)]
     root_own = along(root_rows)
-    msg1, msg3, merged[2], root_own, *own = together(
-        (msg1, msg3, merged[2], root_own, *own)
+    msg2, merged[1], merged[3], root_own, *own = together(
+        (msg2, merged[1], merged[3], root_own, *own)
     )
 
-    msgs = [merged[0], msg1, shift(merged[2], dx=2), msg3]
+    msgs = [merged[0], shift(merged[1], dx=1), msg2, shift(merged[3], dx=3)]
     own = jnp.stack(own, axis=0)
     other, root_other = shift(own, dc=1), shift(root_own, dc=1)
     kbit, qanc, lists, counts = make_tables(ids, parent, node_length)
@@ -661,8 +681,9 @@
     back = [parts[0], back1, back2, back3]
     crossed = shift(jnp.stack([part[1] for part in back], axis=0), dc=1)
     crossed_sums = shift(jnp.stack([part[1] for part in sums], axis=0), dc=1)
-    grad_pairs, grad_root = unpack_pairs(ids, sums, crossed_sums)
-    grad_query, grad_query_root = unpack_query(ids, back, crossed)
+    grad_query, grad_query_root, grad_pairs, grad_root = unpack(
+        ids, back, crossed, sums, crossed_sums
+    )
     return grad_query, grad_query_root.reshape(1, 4096), grad_pairs, grad_root
 
 

time: 137 us -> 137 us (level); the launches traced: 137 us -> 135 us
  Pallas kernels: 39.5 us -> 32.9 us
  starting transfers between devices: 32.2 us -> 37.2 us
  waiting for transfers between devices: 24.8 us -> 21.9 us
  blocking collectives: 35.9 us -> 38.5 us
    pallas_call x1, Pallas kernels: 24.8 us -> 19.4 us  [compute(): pl.pallas_call(compute_kernel, in_specs=[smem()] * 3 + [vmem()] * 10, out...]
    ppermute x26, starting transfers between devices: 32.2 us -> 37.2 us  [shift(): return lax.ppermute(array, ('x', 'y', 'core'), perm(dx, dy, dc))]
    ppermute x26, waiting for transfers between devices: 24.8 us -> 21.9 us  [shift(): return lax.ppermute(array, ('x', 'y', 'core'), perm(dx, dy, dc))]
    all_to_all x2, blocking collectives: 35.9 us -> 38.5 us  [along(): return lax.all_to_all(array, ('leaf', 'y'), 0, 0, tiled=True)]
    pallas_call x2 -> x1, Pallas kernels: 3.49 us -> 2.8 us  [unpack(): pl.pallas_call(unpack_kernel, in_specs=[smem()] + [vmem()] * 10, out_spec...]
  transfers between devices with their start and end apart: 26 -> 26, of which waited for: 6 -> 6; matrix products, arithmetic and copies ran while one was open for 0% -> 0% of each run, Pallas kernels for 8% -> 7%
where the time goes in v2:
time: 137 us; the launch traced here: 135 us
  blocking collectives  38.5 us (28%)
  starting transfers between devices  37.2 us (27%)
  Pallas kernels  32.9 us (24%)
  waiting for transfers between devices  21.9 us (16%)
  local copies, waits for them, and re-layouts  3.63 us (3%)
    all_to_all x2, blocking collectives, along(): return lax.all_to_all(array, ('leaf', 'y'), 0, 0, tiled=True)  38.5 us
    ppermute x26, starting transfers between devices, shift(): return lax.ppermute(array, ('x', 'y', 'core'), perm(dx, dy, dc))  37.2 us
    ppermute x26, waiting for transfers between devices, shift(): return lax.ppermute(array, ('x', 'y', 'core'), perm(dx, dy, dc))  21.9 us
    pallas_call x1, Pallas kernels, compute(): pl.pallas_call(compute_kernel, in_specs=[smem()] * 3 + [vmem()] * 10, out...  19.4 us
    pallas_call x1, Pallas kernels, pack_rows(): pl.pallas_call(pack_rows_kernel, in_specs=[smem()] + [pl.BlockSpec(memory...  4.73 us
    pallas_call x1, Pallas kernels, make_tables(): pl.pallas_call(tables_kernel, in_specs=[smem(), smem(), smem()], out_spec...  3.67 us
    unnamed x16, local copies, waits for them, and re-layouts  3.55 us
    pallas_call x1, Pallas kernels, unpack(): pl.pallas_call(unpack_kernel, in_specs=[smem()] + [vmem()] * 10, out_spec...  2.8 us
  transfers between devices with their start and end apart: 26, of which 6 were waited for; matrix products, arithmetic and copies ran while one was open for 0% of the time, Pallas kernels for 7%

profile of v2, /device:TPU:1, one launch (start us, length us, event | category | flops | bytes accessed | tf_op | source)
XLA Modules:
  0.0 135.5 jit_solution(8288129921149905400)
XLA Ops:
  0.6 0.1 pad_add_fusion.ids
  0.7 0.9 copy-done.1
  1.7 0.7 copy-done.5
  2.4 0.6 pack_pairs.1
  3.0 2.1 %collective-permute-start = (bf16[2,144,128]{2,1,0:T(8,128)(2,1)S(1)}, bf16[2,144,128]{2,1,0:T(8,128)(2,1)S(1)}, u32[]{:S(2)}, u32[]{:S(2)}) collective-permute-start(bf16[2,144,128]{2,1,0:T(8,128)(2,1)S(1)} %get-tuple-element.90), channel_id=1, source_target_pairs={{0,8},{1,9},{2,10},{3,11},{4,12},{5,13},{6,14},{7,15},{8,16},{9,17... | collective-permute-start | bytes 221192 | tf_op jit(solution)/shard_map/ppermute | solution.py:43
  5.1 2.5 %collective-permute-start.1 = (bf16[2,144,128]{2,1,0:T(8,128)(2,1)S(1)}, bf16[2,144,128]{2,1,0:T(8,128)(2,1)S(1)}, u32[]{:S(2)}, u32[]{:S(2)}) collective-permute-start(bf16[2,144,128]{2,1,0:T(8,128)(2,1)S(1)} %get-tuple-element.91), channel_id=1, source_target_pairs={{0,16},{1,17},{2,18},{3,19},{4,20},{5,21},{6,22},{7,23},{8,24},{9,... | collective-permute-start | bytes 221192 | tf_op jit(solution)/shard_map/ppermute | solution.py:43
  7.6 1.2 collective-permute-start.2
  8.7 4.7 %pack_rows.1 = (bf16[4,1088,128]{2,1,0:T(8,128)(2,1)}, bf16[4,1088,128]{2,1,0:T(8,128)(2,1)}) custom-call(s32[4]{0:T(128)} %copy-done.2, bf16[128,4096]{1,0:T(8,128)(2,1)} %refs_0_.1, bf16[128,4096]{1,0:T(8,128)(2,1)} %refs_1_.1, bf16[128,4096]{1,0:T(8,128)(2,1)} %refs_2_.1, f32[32,128]{1,0:T(8,128)} %refs_3_.1, bf16[1,4096]{1,0:T(2,128)(2,1)} %refs_4_.1, ...), custom_call_target="tpu_custom_call" | custom-call | tf_op jit(solution)/shard_map/pack_rows/pallas_call | solution.py:256
  13.5 0.0 collective-permute-done.g1
  13.5 0.0 collective-permute-done.1.g2
  13.5 0.0 collective-permute-done.2.g3
  13.5 1.6 %collective-permute-start.4 = (bf16[4,1088,128]{2,1,0:T(8,128)(2,1)}, bf16[4,1088,128]{2,1,0:T(8,128)(2,1)S(1)}, u32[]{:S(2)}, u32[]{:S(2)}) collective-permute-start(bf16[4,1088,128]{2,1,0:T(8,128)(2,1)} %get-tuple-element.100), channel_id=1, source_target_pairs={{0,1},{1,0},{2,3},{3,2},{4,5},{5,4},{6,7},{7,6},{8,9},{9,8},{10,11... | collective-permute-start | bytes 3342344 | tf_op jit(solution)/shard_map/ppermute | solution.py:43
  15.2 0.1 collective-permute-start.3
  15.3 2.4 %collective-permute-done.3.crossed = bf16[4,144,128]{2,1,0:T(8,128)(2,1)S(1)} collective-permute-done((bf16[4,144,128]{2,1,0:T(8,128)(2,1)S(1)}, bf16[4,144,128]{2,1,0:T(8,128)(2,1)S(1)}, u32[]{:S(2)}, u32[]{:S(2)}) %collective-permute-start.3) | collective-permute-done | bytes 147488 | tf_op jit(solution)/shard_map/ppermute | solution.py:43
  17.7 0.7 copy-done.3
  18.3 0.6 join_pairs.1
  18.9 0.0 copy-start
  18.9 1.2 copy-done
  20.2 0.1 merge_rows.1
  20.3 2.0 %collective-permute-start.5 = (bf16[2,1088,128]{2,1,0:T(8,128)(2,1)S(1)}, bf16[2,1088,128]{2,1,0:T(8,128)(2,1)S(1)}, u32[]{:S(2)}, u32[]{:S(2)}) collective-permute-start(bf16[2,1088,128]{2,1,0:T(8,128)(2,1)S(1)} %get-tuple-element.105), channel_id=1, source_target_pairs={{0,16},{1,17},{2,18},{3,19},{4,20},{5,21},{6,22},{7,23},{8,24},{9,... | collective-permute-start | bytes 1671176 | tf_op jit(solution)/shard_map/ppermute | solution.py:43
  22.4 1.0 collective-permute-start.8
  23.4 0.3 collective-permute-start.7
  23.7 0.7 collective-permute-start.6
  24.4 19.4 %all_to_all.10.root_own = bf16[32,16,128]{2,1,0:T(8,128)(2,1)S(1)} all-to-all(bf16[32,16,128]{2,1,0:T(8,128)(2,1)S(1)} %get-tuple-element.108), channel_id=1, replica_groups=mesh['leaf'=8,'x'=4,'y'=4,'core'=2] {'leaf','y'}, dimensions={0} | all-to-all | bytes 262144 | tf_op jit(solution)/shard_map/all_to_all | solution.py:608
  43.8 0.0 collective-permute-done.8
  43.8 0.0 collective-permute-done.7
  43.8 0.0 collective-permute-done.6
  43.9 0.1 pad_maximum_fusion.own
  44.0 3.1 %collective-permute-start.9 = (bf16[4,8,128,128]{3,2,1,0:T(8,128)(2,1)S(1)}, bf16[4,8,128,128]{3,2,1,0:T(8,128)(2,1)S(1)}, u32[]{:S(2)}, u32[]{:S(2)}) collective-permute-start(bf16[4,8,128,128]{3,2,1,0:T(8,128)(2,1)S(1)} %pad_maximum_fusion.own), channel_id=1, source_target_pairs={{0,1},{1,0},{2,3},{3,2},{4,5},{5,4},{6,7},{7,6},{8,9},{9,8},{10,11... | collective-permute-start | bytes 3145736 | tf_op jit(solution)/shard_map/ppermute | solution.py:43
  47.1 0.8 collective-permute-start.11
  47.9 1.9 %collective-permute-start.12 = (bf16[2,1088,128]{2,1,0:T(8,128)(2,1)S(1)}, bf16[2,1088,128]{2,1,0:T(8,128)(2,1)S(1)}, u32[]{:S(2)}, u32[]{:S(2)}) collective-permute-start(bf16[2,1088,128]{2,1,0:T(8,128)(2,1)S(1)} %get-tuple-element.118), channel_id=1, source_target_pairs={{0,24},{1,25},{2,26},{3,27},{4,28},{5,29},{6,30},{7,31},{8,0},{9,1... | collective-permute-start | bytes 1671176 | tf_op jit(solution)/shard_map/ppermute | solution.py:43
  49.8 0.6 collective-permute-start.10
  50.5 3.7 %tables.1 = (s32[35,128,128]{2,1,0:T(8,128)S(1)}, s32[32,128]{1,0:T(8,128)S(1)}, s32[8,40]{1,0:T(8,128)S(1)}, s32[8]{0:T(128)S(1)}) custom-call(s32[4]{0:T(128)S(1)} %copy-done.4, s32[1,24]{1,0:T(1,128)S(1)} %copy-done.6, s32[1,24]{1,0:T(1,128)S(1)} %copy-done.7), custom_call_target="tpu_custom_call" | custom-call | flops 1000000 | bytes 4000000 | tf_op jit(solution)/shard_map/tables/pallas_call | solution.py:123
  54.2 0.0 collective-permute-done.10.root_other
  54.2 8.4 %collective-permute-done.11.refs_1_ = bf16[2,1088,128]{2,1,0:T(8,128)(2,1)S(1)} collective-permute-done((bf16[2,1088,128]{2,1,0:T(8,128)(2,1)S(1)}, bf16[2,1088,128]{2,1,0:T(8,128)(2,1)S(1)}, u32[]{:S(2)}, u32[]{:S(2)}) %collective-permute-start.11) | collective-permute-done | bytes 557088 | tf_op jit(solution)/shard_map/ppermute | solution.py:43
  62.6 19.4 %compute.1 = (bf16[2,528,128]{2,1,0:T(8,128)(2,1)S(1)}, bf16[2,528,128]{2,1,0:T(8,128)(2,1)S(1)}, bf16[2,528,128]{2,1,0:T(8,128)(2,1)S(1)}, bf16[2,528,128]{2,1,...) custom-call(s32[4]{0:T(128)S(1)} %copy-done.4, ...), custom_call_target="tpu_custom_call" | custom-call | flops 10000000000 | bytes 16000000 | tf_op jit(solution)/shard_map/compute/pallas_call | solution.py:482
  82.0 0.9 collective-permute-start.13
  82.9 0.1 collective-permute-start.14
  83.0 2.4 %collective-permute-done.14 = f32[32,8,128]{2,1,0:T(8,128)S(1)} collective-permute-done((f32[32,8,128]{2,1,0:T(8,128)S(1)}, f32[32,8,128]{2,1,0:T(8,128)S(1)}, u32[]{:S(2)}, u32[]{:S(2)}) %collective-permute-start.14) | collective-permute-done | bytes 131104 | tf_op jit(solution)/shard_map/ppermute | solution.py:43
  85.4 0.0 collective-permute-done.13.other
  85.4 0.3 join_cores.1
  85.7 2.6 %collective-permute-start.15 = (bf16[2,528,128]{2,1,0:T(8,128)(2,1)S(1)}, bf16[2,528,128]{2,1,0:T(8,128)(2,1)S(1)}, u32[]{:S(2)}, u32[]{:S(2)}) collective-permute-start(bf16[2,528,128]{2,1,0:T(8,128)(2,1)S(1)} %get-tuple-element.134), channel_id=1, source_target_pairs={{0,16},{1,17},{2,18},{3,19},{4,20},{5,21},{6,22},{7,23},{8,24},{9,... | collective-permute-start | bytes 811016 | tf_op jit(solution)/shard_map/ppermute | solution.py:43
  88.2 4.9 %collective-permute-start.16 = (bf16[8,128,128]{2,1,0:T(8,128)(2,1)S(1)}, bf16[8,128,128]{2,1,0:T(8,128)(2,1)S(1)}, u32[]{:S(2)}, u32[]{:S(2)}) collective-permute-start(bf16[8,128,128]{2,1,0:T(8,128)(2,1)S(1)} %get-tuple-element.137), channel_id=1, source_target_pairs={{0,6},{1,7},{2,0},{3,1},{4,2},{5,3},{6,4},{7,5},{8,14},{9,15},{10,... | collective-permute-start | bytes 786440 | tf_op jit(solution)/shard_map/ppermute | solution.py:43
  93.1 0.6 collective-permute-start.18
  93.7 19.1 %all_to_all.11.roots = f32[32,8,128]{2,1,0:T(8,128)S(1)} all-to-all(f32[32,8,128]{2,1,0:T(8,128)S(1)} %add.3), channel_id=1, replica_groups=mesh['leaf'=8,'x'=4,'y'=4,'core'=2] {'leaf','y'}, dimensions={0} | all-to-all | bytes 262144 | tf_op jit(solution)/shard_map/all_to_all | solution.py:608
  112.8 0.0 collective-permute-done.16.r1
  112.8 0.0 collective-permute-done.17.r2
  112.8 1.4 %collective-permute-start.19 = (bf16[2,528,128]{2,1,0:T(8,128)(2,1)S(1)}, bf16[2,528,128]{2,1,0:T(8,128)(2,1)S(1)}, u32[]{:S(2)}, u32[]{:S(2)}) collective-permute-start(bf16[2,528,128]{2,1,0:T(8,128)(2,1)S(1)} %get-tuple-element.140), channel_id=1, source_target_pairs={{0,24},{1,25},{2,26},{3,27},{4,28},{5,29},{6,30},{7,31},{8,0},{9,1... | collective-permute-start | bytes 811016 | tf_op jit(solution)/shard_map/ppermute | solution.py:43
  114.3 0.3 collective-permute-start.20
  114.6 0.7 sum_pairs.1
  115.2 0.9 collective-permute-start.21
  116.1 2.7 %collective-permute-start.22 = (f32[2,136,128]{2,1,0:T(8,128)S(1)}, f32[2,136,128]{2,1,0:T(8,128)S(1)}, u32[]{:S(2)}, u32[]{:S(2)}) collective-permute-start(f32[2,136,128]{2,1,0:T(8,128)S(1)} %get-tuple-element.149), channel_id=1, source_target_pairs={{0,16},{1,17},{2,18},{3,19},{4,20},{5,21},{6,22},{7,23},{8,24},{9,... | collective-permute-start | bytes 417800 | tf_op jit(solution)/shard_map/ppermute | solution.py:43
  118.9 0.0 collective-permute-start.23
  118.9 4.9 %collective-permute-done.21.refs_6_ = f32[2,136,128]{2,1,0:T(8,128)S(1)} collective-permute-done((f32[2,136,128]{2,1,0:T(8,128)S(1)}, f32[2,136,128]{2,1,0:T(8,128)S(1)}, u32[]{:S(2)}, u32[]{:S(2)}) %collective-permute-start.21) | collective-permute-done | bytes 139296 | tf_op jit(solution)/shard_map/ppermute | solution.py:43
  123.8 1.9 %collective-permute-done.22.refs_7_ = f32[2,136,128]{2,1,0:T(8,128)S(1)} collective-permute-done((f32[2,136,128]{2,1,0:T(8,128)S(1)}, f32[2,136,128]{2,1,0:T(8,128)S(1)}, u32[]{:S(2)}, u32[]{:S(2)}) %collective-permute-start.22) | collective-permute-done | bytes 139296 | tf_op jit(solution)/shard_map/ppermute | solution.py:43
  125.8 0.0 collective-permute-done.23.refs_8_
  125.8 0.0 collective-permute-done.19.refs_1_
  125.8 0.0 collective-permute-done.20.refs_3_
  125.8 0.1 pad_maximum_fusion.1
  125.9 4.7 %collective-permute-start.24 = (bf16[4,528,128]{2,1,0:T(8,128)(2,1)S(1)}, bf16[4,528,128]{2,1,0:T(8,128)(2,1)S(1)}, u32[]{:S(2)}, u32[]{:S(2)}) collective-permute-start(bf16[4,528,128]{2,1,0:T(8,128)(2,1)S(1)} %pad_maximum_fusion.1), channel_id=1, source_target_pairs={{0,1},{1,0},{2,3},{3,2},{4,5},{5,4},{6,7},{7,6},{8,9},{9,8},{10,11... | collective-permute-start | bytes 1622024 | tf_op jit(solution)/shard_map/ppermute | solution.py:43
  130.6 0.1 collective-permute-start.25
  130.7 1.8 %collective-permute-done.25.refs_9_ = f32[4,136,128]{2,1,0:T(8,128)S(1)} collective-permute-done((f32[4,136,128]{2,1,0:T(8,128)S(1)}, f32[4,136,128]{2,1,0:T(8,128)S(1)}, u32[]{:S(2)}, u32[]{:S(2)}) %collective-permute-start.25) | collective-permute-done | bytes 278560 | tf_op jit(solution)/shard_map/ppermute | solution.py:43
  132.5 0.0 collective-permute-done.24.refs_4_
  132.5 2.8 %unpack.1 = (f32[128,4096]{1,0:T(8,128)}, f32[8,4,128]{2,1,0:T(4,128)}, f32[128,1024]{1,0:T(8,128)}, f32[1,1024]{1,0:T(1,128)}) custom-call(s32[4]{0:T(128)S(1)} %copy-done.4, bf16[2,528,128]{2,1,0:T(8,128)(2,1)S(1)} %get-tuple-element.131.refs_0_, bf16[2,528,128]{2,1,0:T(8,128)(2,1)S(1)} %collective-permute-done.19.refs_1_, ...), custom_call_target="tpu_custom_call" | custom-call | tf_op jit(solution)/shard_map/unpack/pallas_call | solution.py:587
  (33 shorter events, 0.2 us)
Async XLA Ops:
  0.7 1.0 copy-start.1
  1.7 0.7 copy-start.5
  2.4 6.4 %copy-start.2 = (s32[4]{0:T(128)}, s32[4]{0:T(128)S(1)}, u32[]{:S(2)}) copy-start(s32[4]{0:T(128)S(1)} %pad_add_fusion.ids) | copy-start | bytes 52
  3.0 10.5 %collective-permute-start = (bf16[2,144,128]{2,1,0:T(8,128)(2,1)S(1)}, bf16[2,144,128]{2,1,0:T(8,128)(2,1)S(1)}, u32[]{:S(2)}, u32[]{:S(2)}) collective-permute-start(bf16[2,144,128]{2,1,0:T(8,128)(2,1)S(1)} %get-tuple-element.90), channel_id=1, source_target_pairs={{0,8},{1,9},{2,10},{3,11},{4,12},{5,13},{6,14},{7,15},{8,16},{9,17... | collective-permute-start | bytes 221192 | tf_op jit(solution)/shard_map/ppermute | solution.py:43
  5.1 8.4 %collective-permute-start.1 = (bf16[2,144,128]{2,1,0:T(8,128)(2,1)S(1)}, bf16[2,144,128]{2,1,0:T(8,128)(2,1)S(1)}, u32[]{:S(2)}, u32[]{:S(2)}) collective-permute-start(bf16[2,144,128]{2,1,0:T(8,128)(2,1)S(1)} %get-tuple-element.91), channel_id=1, source_target_pairs={{0,16},{1,17},{2,18},{3,19},{4,20},{5,21},{6,22},{7,23},{8,24},{9,... | collective-permute-start | bytes 221192 | tf_op jit(solution)/shard_map/ppermute | solution.py:43
  7.6 5.9 %collective-permute-start.2 = (bf16[2,144,128]{2,1,0:T(8,128)(2,1)S(1)}, bf16[2,144,128]{2,1,0:T(8,128)(2,1)S(1)}, u32[]{:S(2)}, u32[]{:S(2)}) collective-permute-start(bf16[2,144,128]{2,1,0:T(8,128)(2,1)S(1)} %get-tuple-element.92), channel_id=1, source_target_pairs={{0,24},{1,25},{2,26},{3,27},{4,28},{5,29},{6,30},{7,31},{8,0},{9,1... | collective-permute-start | bytes 221192 | tf_op jit(solution)/shard_map/ppermute | solution.py:43
  13.5 5.4 %collective-permute-start.4 = (bf16[4,1088,128]{2,1,0:T(8,128)(2,1)}, bf16[4,1088,128]{2,1,0:T(8,128)(2,1)S(1)}, u32[]{:S(2)}, u32[]{:S(2)}) collective-permute-start(bf16[4,1088,128]{2,1,0:T(8,128)(2,1)} %get-tuple-element.100), channel_id=1, source_target_pairs={{0,1},{1,0},{2,3},{3,2},{4,5},{5,4},{6,7},{7,6},{8,9},{9,8},{10,11... | collective-permute-start | bytes 3342344 | tf_op jit(solution)/shard_map/ppermute | solution.py:43
  15.2 2.5 %collective-permute-start.3 = (bf16[4,144,128]{2,1,0:T(8,128)(2,1)S(1)}, bf16[4,144,128]{2,1,0:T(8,128)(2,1)S(1)}, u32[]{:S(2)}, u32[]{:S(2)}) collective-permute-start(bf16[4,144,128]{2,1,0:T(8,128)(2,1)S(1)} %pad_maximum_fusion.3), channel_id=1, source_target_pairs={{0,1},{1,0},{2,3},{3,2},{4,5},{5,4},{6,7},{7,6},{8,9},{9,8},{10,11... | collective-permute-start | bytes 442376 | tf_op jit(solution)/shard_map/ppermute | solution.py:43
  17.7 0.7 copy-start.3
  18.9 1.3 copy-start
  20.2 30.3 %copy-start.4 = (s32[4]{0:T(128)S(1)}, s32[4]{0:T(128)}, u32[]{:S(2)}) copy-start(s32[4]{0:T(128)} %copy-done.2) | copy-start | bytes 52
  20.2 30.3 %copy-start.6 = (s32[1,24]{1,0:T(1,128)S(1)}, s32[1,24]{1,0:T(1,128)}, u32[]{:S(2)}) copy-start(s32[1,24]{1,0:T(1,128)} %parent.1) | copy-start | bytes 292
  20.2 30.3 %copy-start.7 = (s32[1,24]{1,0:T(1,128)S(1)}, s32[1,24]{1,0:T(1,128)}, u32[]{:S(2)}) copy-start(s32[1,24]{1,0:T(1,128)} %length.1) | copy-start | bytes 292
  20.3 23.5 %collective-permute-start.5 = (bf16[2,1088,128]{2,1,0:T(8,128)(2,1)S(1)}, bf16[2,1088,128]{2,1,0:T(8,128)(2,1)S(1)}, u32[]{:S(2)}, u32[]{:S(2)}) collective-permute-start(bf16[2,1088,128]{2,1,0:T(8,128)(2,1)S(1)} %get-tuple-element.105), channel_id=1, source_target_pairs={{0,16},{1,17},{2,18},{3,19},{4,20},{5,21},{6,22},{7,23},{8,24},{9,... | collective-permute-start | bytes 1671176 | tf_op jit(solution)/shard_map/ppermute | solution.py:43
  22.4 21.5 %collective-permute-start.8 = (bf16[8,128,128]{2,1,0:T(8,128)(2,1)S(1)}, bf16[8,128,128]{2,1,0:T(8,128)(2,1)S(1)}, u32[]{:S(2)}, u32[]{:S(2)}) collective-permute-start(bf16[8,128,128]{2,1,0:T(8,128)(2,1)S(1)} %get-tuple-element.110), channel_id=1, source_target_pairs={{0,6},{1,7},{2,0},{3,1},{4,2},{5,3},{6,4},{7,5},{8,14},{9,15},{10,... | collective-permute-start | bytes 786440 | tf_op jit(solution)/shard_map/ppermute | solution.py:43
  23.4 20.5 %collective-permute-start.7 = (bf16[8,128,128]{2,1,0:T(8,128)(2,1)S(1)}, bf16[8,128,128]{2,1,0:T(8,128)(2,1)S(1)}, u32[]{:S(2)}, u32[]{:S(2)}) collective-permute-start(bf16[8,128,128]{2,1,0:T(8,128)(2,1)S(1)} %get-tuple-element.110), channel_id=1, source_target_pairs={{0,4},{1,5},{2,6},{3,7},{4,0},{5,1},{6,2},{7,3},{8,12},{9,13},{10,... | collective-permute-start | bytes 786440 | tf_op jit(solution)/shard_map/ppermute | solution.py:43
  23.7 20.1 %collective-permute-start.6 = (bf16[8,128,128]{2,1,0:T(8,128)(2,1)S(1)}, bf16[8,128,128]{2,1,0:T(8,128)(2,1)S(1)}, u32[]{:S(2)}, u32[]{:S(2)}) collective-permute-start(bf16[8,128,128]{2,1,0:T(8,128)(2,1)S(1)} %get-tuple-element.110), channel_id=1, source_target_pairs={{0,2},{1,3},{2,4},{3,5},{4,6},{5,7},{6,0},{7,1},{8,10},{9,11},{10,... | collective-permute-start | bytes 786440 | tf_op jit(solution)/shard_map/ppermute | solution.py:43
  44.0 18.6 %collective-permute-start.9 = (bf16[4,8,128,128]{3,2,1,0:T(8,128)(2,1)S(1)}, bf16[4,8,128,128]{3,2,1,0:T(8,128)(2,1)S(1)}, u32[]{:S(2)}, u32[]{:S(2)}) collective-permute-start(bf16[4,8,128,128]{3,2,1,0:T(8,128)(2,1)S(1)} %pad_maximum_fusion.own), channel_id=1, source_target_pairs={{0,1},{1,0},{2,3},{3,2},{4,5},{5,4},{6,7},{7,6},{8,9},{9,8},{10,11... | collective-permute-start | bytes 3145736 | tf_op jit(solution)/shard_map/ppermute | solution.py:43
  47.1 15.4 %collective-permute-start.11 = (bf16[2,1088,128]{2,1,0:T(8,128)(2,1)S(1)}, bf16[2,1088,128]{2,1,0:T(8,128)(2,1)S(1)}, u32[]{:S(2)}, u32[]{:S(2)}) collective-permute-start(bf16[2,1088,128]{2,1,0:T(8,128)(2,1)S(1)} %get-tuple-element.116), channel_id=1, source_target_pairs={{0,8},{1,9},{2,10},{3,11},{4,12},{5,13},{6,14},{7,15},{8,16},{9,17... | collective-permute-start | bytes 1671176 | tf_op jit(solution)/shard_map/ppermute | solution.py:43
  47.9 14.6 %collective-permute-start.12 = (bf16[2,1088,128]{2,1,0:T(8,128)(2,1)S(1)}, bf16[2,1088,128]{2,1,0:T(8,128)(2,1)S(1)}, u32[]{:S(2)}, u32[]{:S(2)}) collective-permute-start(bf16[2,1088,128]{2,1,0:T(8,128)(2,1)S(1)} %get-tuple-element.118), channel_id=1, source_target_pairs={{0,24},{1,25},{2,26},{3,27},{4,28},{5,29},{6,30},{7,31},{8,0},{9,1... | collective-permute-start | bytes 1671176 | tf_op jit(solution)/shard_map/ppermute | solution.py:43
  49.8 4.3 %collective-permute-start.10 = (bf16[32,16,128]{2,1,0:T(8,128)(2,1)S(1)}, bf16[32,16,128]{2,1,0:T(8,128)(2,1)S(1)}, u32[]{:S(2)}, u32[]{:S(2)}) collective-permute-start(bf16[32,16,128]{2,1,0:T(8,128)(2,1)S(1)} %all_to_all.10.root_own), channel_id=1, source_target_pairs={{0,1},{1,0},{2,3},{3,2},{4,5},{5,4},{6,7},{7,6},{8,9},{9,8},{10,11... | collective-permute-start | bytes 393224 | tf_op jit(solution)/shard_map/ppermute | solution.py:43
  82.0 3.4 %collective-permute-start.13 = (bf16[32,128,128]{2,1,0:T(8,128)(2,1)S(1)}, bf16[32,128,128]{2,1,0:T(8,128)(2,1)S(1)}, u32[]{:S(2)}, u32[]{:S(2)}) collective-permute-start(bf16[32,128,128]{2,1,0:T(8,128)(2,1)S(1)} %get-tuple-element.120), channel_id=1, source_target_pairs={{0,1},{1,0},{2,3},{3,2},{4,5},{5,4},{6,7},{7,6},{8,9},{9,8},{10,11... | collective-permute-start | bytes 3145736 | tf_op jit(solution)/shard_map/ppermute | solution.py:43
  82.9 2.5 %collective-permute-start.14 = (f32[32,8,128]{2,1,0:T(8,128)S(1)}, f32[32,8,128]{2,1,0:T(8,128)S(1)}, u32[]{:S(2)}, u32[]{:S(2)}) collective-permute-start(f32[32,8,128]{2,1,0:T(8,128)S(1)} %get-tuple-element.123), channel_id=1, source_target_pairs={{0,1},{1,0},{2,3},{3,2},{4,5},{5,4},{6,7},{7,6},{8,9},{9,8},{10,11... | collective-permute-start | bytes 393224 | tf_op jit(solution)/shard_map/ppermute | solution.py:43
  85.7 27.1 %collective-permute-start.15 = (bf16[2,528,128]{2,1,0:T(8,128)(2,1)S(1)}, bf16[2,528,128]{2,1,0:T(8,128)(2,1)S(1)}, u32[]{:S(2)}, u32[]{:S(2)}) collective-permute-start(bf16[2,528,128]{2,1,0:T(8,128)(2,1)S(1)} %get-tuple-element.134), channel_id=1, source_target_pairs={{0,16},{1,17},{2,18},{3,19},{4,20},{5,21},{6,22},{7,23},{8,24},{9,... | collective-permute-start | bytes 811016 | tf_op jit(solution)/shard_map/ppermute | solution.py:43
  88.2 24.6 %collective-permute-start.16 = (bf16[8,128,128]{2,1,0:T(8,128)(2,1)S(1)}, bf16[8,128,128]{2,1,0:T(8,128)(2,1)S(1)}, u32[]{:S(2)}, u32[]{:S(2)}) collective-permute-start(bf16[8,128,128]{2,1,0:T(8,128)(2,1)S(1)} %get-tuple-element.137), channel_id=1, source_target_pairs={{0,6},{1,7},{2,0},{3,1},{4,2},{5,3},{6,4},{7,5},{8,14},{9,15},{10,... | collective-permute-start | bytes 786440 | tf_op jit(solution)/shard_map/ppermute | solution.py:43
  93.1 19.7 %collective-permute-start.17 = (bf16[8,128,128]{2,1,0:T(8,128)(2,1)S(1)}, bf16[8,128,128]{2,1,0:T(8,128)(2,1)S(1)}, u32[]{:S(2)}, u32[]{:S(2)}) collective-permute-start(bf16[8,128,128]{2,1,0:T(8,128)(2,1)S(1)} %get-tuple-element.138), channel_id=1, source_target_pairs={{0,4},{1,5},{2,6},{3,7},{4,0},{5,1},{6,2},{7,3},{8,12},{9,13},{10,... | collective-permute-start | bytes 786440 | tf_op jit(solution)/shard_map/ppermute | solution.py:43
  93.1 19.7 %collective-permute-start.18 = (bf16[8,128,128]{2,1,0:T(8,128)(2,1)S(1)}, bf16[8,128,128]{2,1,0:T(8,128)(2,1)S(1)}, u32[]{:S(2)}, u32[]{:S(2)}) collective-permute-start(bf16[8,128,128]{2,1,0:T(8,128)(2,1)S(1)} %get-tuple-element.139), channel_id=1, source_target_pairs={{0,2},{1,3},{2,4},{3,5},{4,6},{5,7},{6,0},{7,1},{8,10},{9,11},{10,... | collective-permute-start | bytes 786440 | tf_op jit(solution)/shard_map/ppermute | solution.py:43
  112.8 12.9 %collective-permute-start.19 = (bf16[2,528,128]{2,1,0:T(8,128)(2,1)S(1)}, bf16[2,528,128]{2,1,0:T(8,128)(2,1)S(1)}, u32[]{:S(2)}, u32[]{:S(2)}) collective-permute-start(bf16[2,528,128]{2,1,0:T(8,128)(2,1)S(1)} %get-tuple-element.140), channel_id=1, source_target_pairs={{0,24},{1,25},{2,26},{3,27},{4,28},{5,29},{6,30},{7,31},{8,0},{9,1... | collective-permute-start | bytes 811016 | tf_op jit(solution)/shard_map/ppermute | solution.py:43
  114.3 11.5 %collective-permute-start.20 = (bf16[2,528,128]{2,1,0:T(8,128)(2,1)S(1)}, bf16[2,528,128]{2,1,0:T(8,128)(2,1)S(1)}, u32[]{:S(2)}, u32[]{:S(2)}) collective-permute-start(bf16[2,528,128]{2,1,0:T(8,128)(2,1)S(1)} %get-tuple-element.141), channel_id=1, source_target_pairs={{0,8},{1,9},{2,10},{3,11},{4,12},{5,13},{6,14},{7,15},{8,16},{9,17... | collective-permute-start | bytes 811016 | tf_op jit(solution)/shard_map/ppermute | solution.py:43
  115.2 8.6 %collective-permute-start.21 = (f32[2,136,128]{2,1,0:T(8,128)S(1)}, f32[2,136,128]{2,1,0:T(8,128)S(1)}, u32[]{:S(2)}, u32[]{:S(2)}) collective-permute-start(f32[2,136,128]{2,1,0:T(8,128)S(1)} %get-tuple-element.148), channel_id=1, source_target_pairs={{0,8},{1,9},{2,10},{3,11},{4,12},{5,13},{6,14},{7,15},{8,16},{9,17... | collective-permute-start | bytes 417800 | tf_op jit(solution)/shard_map/ppermute | solution.py:43
  116.1 9.6 %collective-permute-start.22 = (f32[2,136,128]{2,1,0:T(8,128)S(1)}, f32[2,136,128]{2,1,0:T(8,128)S(1)}, u32[]{:S(2)}, u32[]{:S(2)}) collective-permute-start(f32[2,136,128]{2,1,0:T(8,128)S(1)} %get-tuple-element.149), channel_id=1, source_target_pairs={{0,16},{1,17},{2,18},{3,19},{4,20},{5,21},{6,22},{7,23},{8,24},{9,... | collective-permute-start | bytes 417800 | tf_op jit(solution)/shard_map/ppermute | solution.py:43
  118.9 6.9 %collective-permute-start.23 = (f32[2,136,128]{2,1,0:T(8,128)S(1)}, f32[2,136,128]{2,1,0:T(8,128)S(1)}, u32[]{:S(2)}, u32[]{:S(2)}) collective-permute-start(f32[2,136,128]{2,1,0:T(8,128)S(1)} %get-tuple-element.150), channel_id=1, source_target_pairs={{0,24},{1,25},{2,26},{3,27},{4,28},{5,29},{6,30},{7,31},{8,0},{9,1... | collective-permute-start | bytes 417800 | tf_op jit(solution)/shard_map/ppermute | solution.py:43
  125.9 6.6 %collective-permute-start.24 = (bf16[4,528,128]{2,1,0:T(8,128)(2,1)S(1)}, bf16[4,528,128]{2,1,0:T(8,128)(2,1)S(1)}, u32[]{:S(2)}, u32[]{:S(2)}) collective-permute-start(bf16[4,528,128]{2,1,0:T(8,128)(2,1)S(1)} %pad_maximum_fusion.1), channel_id=1, source_target_pairs={{0,1},{1,0},{2,3},{3,2},{4,5},{5,4},{6,7},{7,6},{8,9},{9,8},{10,11... | collective-permute-start | bytes 1622024 | tf_op jit(solution)/shard_map/ppermute | solution.py:43
  130.6 1.9 %collective-permute-start.25 = (f32[4,136,128]{2,1,0:T(8,128)S(1)}, f32[4,136,128]{2,1,0:T(8,128)S(1)}, u32[]{:S(2)}, u32[]{:S(2)}) collective-permute-start(f32[4,136,128]{2,1,0:T(8,128)S(1)} %pad_maximum_fusion.2), channel_id=1, source_target_pairs={{0,1},{1,0},{2,3},{3,2},{4,5},{5,4},{6,7},{7,6},{8,9},{9,8},{10,11... | collective-permute-start | bytes 835592 | tf_op jit(solution)/shard_map/ppermute | solution.py:43

commit v3 on v2

--- a/solution.py
+++ b/solution.py
@@ -1,3 +1,4 @@
+import functools
 import math
 
 import jax
@@ -329,10 +330,22 @@
     return jnp.concatenate([terms[start + h : start + h + 1, :] for h in range(4)], axis=1)
 
 
-def compute_kernel(ids, lists, counts, kbit, qanc, own, other, root_own, root_other, *refs):
-    msgs, outs, refs = refs[0:4], refs[4:8], refs[8:]
-    keep, send, root_keep, root_send, refs = *refs[0:4], refs[4:]
-    keys, values, keys_t, root_rows, acc, dk, dv = refs
+def compute_kernel(ks, ids, lists, counts, kbit, qanc, own, other, root_own, root_other, *refs):
+    msgs, refs = refs[0:2], refs[2:]
+    prior, refs = (refs[0:2], refs[2:]) if ks[0] else ((), refs)
+    outs, refs = refs[0:2], refs[2:]
+    if prior:
+        keep, send, root_keep, root_send, refs = *refs[0:4], refs[4:]
+        keep_held, send_held, sems = refs[7:10]
+        copies = [
+            pltpu.make_async_copy(prior[0], keep_held, sems.at[0]),
+            pltpu.make_async_copy(prior[1], send_held, sems.at[1]),
+        ]
+        for copy in copies:
+            copy.start()
+    else:
+        keep, send, refs = refs[0], refs[1], refs[2:]
+    keys, values, keys_t, root_rows, acc, dk, dv = refs[0:7]
     x, y, c, z = ids[0], ids[1], ids[2], ids[3]
     first = c == 0
 
@@ -372,8 +385,8 @@
 
     root_rows[...] = jnp.zeros(root_rows.shape, F4)
     special = jnp.zeros((16, HD), F4)
-    for i in range(8):
-        msg, dc = msgs[i // 2], i % 2
+    for i in [2 * k + dc for k in ks for dc in range(2)]:
+        msg, dc = msgs[ks.index(i // 2)], i % 2
         special = special + unsplit(msg[dc, T0 : T0 + 48, :])
         tile = msg[dc, R0 : R0 + 16, :].astype(F4)
         root_rows[0, i * 4 : i * 4 + 4, :] = tile[0:4]
@@ -387,7 +400,8 @@
     root_query_pos = z * 32 + source_x * 8 + y * 2 + source_c
     at = row // 8
     root_key_pos = (at // 4) * 32 + (row % 8 // 2) * 8 + (at % 4) * 2 + row % 2
-    mask = (lane < 32) & (root_key_pos <= root_query_pos)
+    here = (source // 2 == ks[0]) | (source // 2 == ks[1])
+    mask = here & (root_key_pos <= root_query_pos)
     prob = jnp.where(mask, jnp.exp2(nt(rkey, query) * SCALE2 - special[8:9, :]), 0.0)
     dscore = (prob * (nt(rvalue, grad) - special[9:10, :])).astype(BF)
     dv[ROOT_BLOCK : ROOT_BLOCK + 2] = nn(prob.astype(BF), grad).reshape(2, BLK, HD)
@@ -396,8 +410,8 @@
 
     pad = jnp.zeros((12, HD), F4)
     base = iota((BLK, BLK), 0)
-    for k in range(4):
-        msg, out = msgs[k], outs[k]
+    for slot, k in enumerate(ks):
+        msg, out = msgs[slot], outs[slot]
         for dc in range(2):
             tile = root_dq[8 * k + 4 * dc : 8 * k + 4 * dc + 4]
             out[dc, 512:528, :] = jnp.concatenate([tile, pad], axis=0).astype(BF)
@@ -457,14 +471,26 @@
         lax.fori_loop(0, 2, query_block, 0)
 
     def store(keep_from, send_from):
+        rows = slice(ROOT_BLOCK, ROOT_BLOCK + 2)
         for ky in range(4):
             for block in range(8):
-                at = place(y, ky, block)
-                keep[ky * 8 + block] = keep_from[at]
-                send[ky * 8 + block] = send_from[at].astype(BF)
-        rows = slice(ROOT_BLOCK, ROOT_BLOCK + 2)
-        root_keep[...] = keep_from[rows].reshape(32, 8, HD)
-        root_send[...] = send_from[rows].reshape(32, 8, HD)
+                at, to = place(y, ky, block), ky * 8 + block
+                if prior:
+                    keep[to] = keep_from[at] + keep_held[to]
+                    send[to] = (send_from[at] + send_held[to]).astype(BF)
+                else:
+                    keep[to] = keep_from[at]
+                    send[to] = send_from[at]
+        if prior:
+            root_keep[...] = (keep_from[rows] + keep_held[32:34]).reshape(32, 8, HD)
+            root_send[...] = (send_from[rows] + send_held[32:34]).reshape(32, 8, HD)
+        else:
+            keep[32:34] = keep_from[rows]
+            send[32:34] = send_from[rows]
+
+    if prior:
+        for copy in copies:
+            copy.wait()
 
     @pl.when(first)
     def _():
@@ -475,17 +501,26 @@
         store(dv, dk)
 
 
-def compute(ids, lists, counts, kbit, qanc, own, other, root_own, root_other, msgs):
-    half = (TREE_BLOCKS, BLK, HD)
+def compute(ks, shared, msgs, prior):
     blocks = pltpu.VMEM((ALL_BLOCKS, BLK, HD), BF)
     sums = pltpu.VMEM((ALL_BLOCKS, BLK, HD), F4)
-    return pl.pallas_call(
-        compute_kernel,
-        in_specs=[smem()] * 3 + [vmem()] * 10,
-        out_specs=[vmem()] * 8,
-        out_shape=[jax.ShapeDtypeStruct((2, 528, HD), BF)] * 4
-        + [jax.ShapeDtypeStruct(half, F4), jax.ShapeDtypeStruct(half, BF)]
-        + [jax.ShapeDtypeStruct((32, 8, HD), F4)] * 2,
+    part = jax.ShapeDtypeStruct((2, 528, HD), BF)
+    half = jax.ShapeDtypeStruct((34, BLK, HD), F4)
+    held = pltpu.VMEM((34, BLK, HD), F4)
+    if prior:
+        sides = [
+            jax.ShapeDtypeStruct((TREE_BLOCKS, BLK, HD), F4),
+            jax.ShapeDtypeStruct((TREE_BLOCKS, BLK, HD), BF),
+        ] + [jax.ShapeDtypeStruct((32, 8, HD), F4)] * 2
+    else:
+        sides = [half, half]
+    return pl.pallas_call(
+        functools.partial(compute_kernel, ks),
+        in_specs=[smem()] * 3
+        + [vmem()] * 8
+        + [pl.BlockSpec(memory_space=pl.ANY)] * len(prior),
+        out_specs=[vmem()] * (2 + len(sides)),
+        out_shape=[part, part] + sides,
         scratch_shapes=[
             blocks,
             blocks,
@@ -494,13 +529,14 @@
             pltpu.VMEM((HD, 512), F4),
             sums,
             sums,
-        ],
+        ]
+        + ([held, held, pltpu.SemaphoreType.DMA((2,))] if prior else []),
         compiler_params=params(32 * 1024 * 1024),
         cost_estimate=pl.CostEstimate(
             flops=10**10, bytes_accessed=16 * 10**6, transcendentals=8 * 10**6
         ),
-        name="compute",
-    )(ids, lists, counts, kbit, qanc, own, other, root_own, root_other, *msgs)
+        name="compute_late" if prior else "compute_early",
+    )(*shared, *msgs, *prior)
 
 
 def join_cores_kernel(keep, other, stay, *outs):
@@ -644,7 +680,10 @@
     merged = merge_rows(keep, shift(send, dc=1))
     crossed = shift(jnp.stack([part[1] for part in pair_parts], axis=0), dc=1)
     joined, root_rows = join_pairs(ids, pair_parts, crossed)
-    joined, root_rows, *merged = together((joined, root_rows, *merged))
+    tables = make_tables(ids, parent, node_length)
+    joined, root_rows, *rest = together((joined, root_rows, *merged, *tables))
+    merged, tables = rest[0:4], rest[4:8]
+    kbit, qanc, lists, counts = tables
 
     msg2 = shift(merged[2], dx=2)
     own = [joined] + [shift(joined, dy=ky) for ky in range(1, 4)]
@@ -656,29 +695,30 @@
     msgs = [merged[0], shift(merged[1], dx=1), msg2, shift(merged[3], dx=3)]
     own = jnp.stack(own, axis=0)
     other, root_other = shift(own, dc=1), shift(root_own, dc=1)
-    kbit, qanc, lists, counts = make_tables(ids, parent, node_length)
-    *parts, keep, send, root_keep, root_send = compute(
-        ids, lists, counts, kbit, qanc, own, other, root_own, root_other, msgs
+    shared = (ids, lists, counts, kbit, qanc, own, other, root_own, root_other)
+    part0, part2, *prior = compute((0, 2), shared, (msgs[0], msgs[2]), ())
+    msg1, msg3, part0, part2, *prior = together((msgs[1], msgs[3], part0, part2, *prior))
+
+    part1, part3, keep, send, root_keep, root_send = compute((1, 3), shared, (msg1, msg3), prior)
+    back2 = shift(part2, dx=-2)
+    back2, part1, part3, keep, send, root_keep, root_send = together(
+        (back2, part1, part3, keep, send, root_keep, root_send)
     )
 
     stay, *low = join_cores(keep, shift(send, dc=1))
     root_sums = root_keep + shift(root_send, dc=1)
-    stay, root_sums, *rest = together((stay, root_sums, *low, *parts))
-    low, parts = rest[0:3], rest[3:7]
+    stay, root_sums, *low = together((stay, root_sums, *low))
 
     received = [shift(low[ky - 1], dy=-ky) for ky in range(1, 4)]
-    back2 = shift(parts[2], dx=-2)
     roots = along(root_sums)
-    stay, roots, back2, part1, part3, *received = together(
-        (stay, roots, back2, parts[1], parts[3], *received)
-    )
+    stay, roots, part1, part3, *received = together((stay, roots, part1, part3, *received))
 
     sums = sum_pairs(ids, stay, received, roots)
     sums = [sums[0]] + [shift(sums[k], dx=k) for k in range(1, 4)]
     back1, back3 = shift(part1, dx=-1), shift(part3, dx=-3)
     back1, back3, *sums = together((back1, back3, *sums))
 
-    back = [parts[0], back1, back2, back3]
+    back = [part0, back1, back2, back3]
     crossed = shift(jnp.stack([part[1] for part in back], axis=0), dc=1)
     crossed_sums = shift(jnp.stack([part[1] for part in sums], axis=0), dc=1)
     grad_query, grad_query_root, grad_pairs, grad_root = unpack(

time: 137 us -> 124 us (0.905)
  waiting for transfers between devices: 21.9 us -> 14.4 us
  blocking collectives: 38.5 us -> 32.9 us
  Pallas kernels: 32.9 us -> 38.3 us
  starting transfers between devices: 37.2 us -> 33.1 us
    ppermute x26, waiting for transfers between devices: 21.9 us -> 14.4 us  [shift(): return lax.ppermute(array, ('x', 'y', 'core'), perm(dx, dy, dc))]
    all_to_all x2, blocking collectives: 38.5 us -> 32.9 us  [along(): return lax.all_to_all(array, ('leaf', 'y'), 0, 0, tiled=True)]
    pallas_call x1 -> x2, Pallas kernels: 19.4 us -> 25 us  [compute(): pl.pallas_call(functools.partial(compute_kernel, ks), in_specs=[smem()] *...]
    ppermute x26, starting transfers between devices: 37.2 us -> 33.1 us  [shift(): return lax.ppermute(array, ('x', 'y', 'core'), perm(dx, dy, dc))]
  transfers between devices with their start and end apart: 26 -> 26, of which waited for: 6 -> 6; matrix products, arithmetic and copies ran while one was open for 0% -> 0% of each run, Pallas kernels for 7% -> 28%
where the time goes in v3:
time: 124 us
  Pallas kernels  38.3 us (31%)
  starting transfers between devices  33.1 us (27%)
  blocking collectives  32.9 us (27%)
  waiting for transfers between devices  14.4 us (12%)
  local copies, waits for them, and re-layouts  3.63 us (3%)
    ppermute x26, starting transfers between devices, shift(): return lax.ppermute(array, ('x', 'y', 'core'), perm(dx, dy, dc))  33.1 us
    all_to_all x2, blocking collectives, along(): return lax.all_to_all(array, ('leaf', 'y'), 0, 0, tiled=True)  32.9 us
    pallas_call x2, Pallas kernels, compute(): pl.pallas_call(functools.partial(compute_kernel, ks), in_specs=[smem()] *...  25 us
    ppermute x26, waiting for transfers between devices, shift(): return lax.ppermute(array, ('x', 'y', 'core'), perm(dx, dy, dc))  14.4 us
    pallas_call x1, Pallas kernels, pack_rows(): pl.pallas_call(pack_rows_kernel, in_specs=[smem()] + [pl.BlockSpec(memory...  4.73 us
    unnamed x16, local copies, waits for them, and re-layouts  3.55 us
    pallas_call x1, Pallas kernels, make_tables(): pl.pallas_call(tables_kernel, in_specs=[smem(), smem(), smem()], out_spec...  3.49 us
    pallas_call x1, Pallas kernels, unpack(): pl.pallas_call(unpack_kernel, in_specs=[smem()] + [vmem()] * 10, out_spec...  2.8 us
  transfers between devices with their start and end apart: 26, of which 6 were waited for; matrix products, arithmetic and copies ran while one was open for 0% of the time, Pallas kernels for 28%

profile of v3, /device:TPU:1, one launch (start us, length us, event | category | flops | bytes accessed | tf_op | source)
XLA Modules:
  0.0 123.8 jit_solution(901732261920701865)
XLA Ops:
  0.7 0.1 pad_add_fusion.ids
  0.7 0.9 copy-done.1
  1.7 0.7 copy-done.5
  2.4 0.6 pack_pairs.1
  3.0 2.1 %collective-permute-start = (bf16[2,144,128]{2,1,0:T(8,128)(2,1)S(1)}, bf16[2,144,128]{2,1,0:T(8,128)(2,1)S(1)}, u32[]{:S(2)}, u32[]{:S(2)}) collective-permute-start(bf16[2,144,128]{2,1,0:T(8,128)(2,1)S(1)} %get-tuple-element.100), channel_id=1, source_target_pairs={{0,8},{1,9},{2,10},{3,11},{4,12},{5,13},{6,14},{7,15},{8,16},{9,17... | collective-permute-start | bytes 221192 | tf_op jit(solution)/shard_map/ppermute | solution.py:44
  5.1 2.5 %collective-permute-start.1 = (bf16[2,144,128]{2,1,0:T(8,128)(2,1)S(1)}, bf16[2,144,128]{2,1,0:T(8,128)(2,1)S(1)}, u32[]{:S(2)}, u32[]{:S(2)}) collective-permute-start(bf16[2,144,128]{2,1,0:T(8,128)(2,1)S(1)} %get-tuple-element.101), channel_id=1, source_target_pairs={{0,16},{1,17},{2,18},{3,19},{4,20},{5,21},{6,22},{7,23},{8,24},{9,... | collective-permute-start | bytes 221192 | tf_op jit(solution)/shard_map/ppermute | solution.py:44
  7.6 1.2 collective-permute-start.2
  8.7 4.7 %pack_rows.1 = (bf16[4,1088,128]{2,1,0:T(8,128)(2,1)}, bf16[4,1088,128]{2,1,0:T(8,128)(2,1)}) custom-call(s32[4]{0:T(128)} %copy-done.2, bf16[128,4096]{1,0:T(8,128)(2,1)} %refs_0_.1, bf16[128,4096]{1,0:T(8,128)(2,1)} %refs_1_.1, bf16[128,4096]{1,0:T(8,128)(2,1)} %refs_2_.1, f32[32,128]{1,0:T(8,128)} %refs_3_.1, bf16[1,4096]{1,0:T(2,128)(2,1)} %refs_4_.1, ...), custom_call_target="tpu_custom_call" | custom-call | tf_op jit(solution)/shard_map/pack_rows/pallas_call | solution.py:257
  13.5 0.0 collective-permute-done.1.g2
  13.5 0.0 collective-permute-done.2.g3
  13.5 1.6 %collective-permute-start.4 = (bf16[4,1088,128]{2,1,0:T(8,128)(2,1)}, bf16[4,1088,128]{2,1,0:T(8,128)(2,1)S(1)}, u32[]{:S(2)}, u32[]{:S(2)}) collective-permute-start(bf16[4,1088,128]{2,1,0:T(8,128)(2,1)} %get-tuple-element.110), channel_id=1, source_target_pairs={{0,1},{1,0},{2,3},{3,2},{4,5},{5,4},{6,7},{7,6},{8,9},{9,8},{10,11... | collective-permute-start | bytes 3342344 | tf_op jit(solution)/shard_map/ppermute | solution.py:44
  15.2 0.1 collective-permute-start.3
  15.3 0.0 copy-start.3
  15.3 0.6 copy-done.3
  16.0 3.5 %tables.1 = (s32[35,128,128]{2,1,0:T(8,128)S(1)}, s32[32,128]{1,0:T(8,128)S(1)}, s32[8,40]{1,0:T(8,128)S(1)}, s32[8]{0:T(128)S(1)}) custom-call(s32[4]{0:T(128)S(1)} %copy-done.3, s32[1,24]{1,0:T(1,128)S(1)} %copy-done.6, s32[1,24]{1,0:T(1,128)S(1)} %copy-done.7), custom_call_target="tpu_custom_call" | custom-call | flops 1000000 | bytes 4000000 | tf_op jit(solution)/shard_map/tables/pallas_call | solution.py:124
  19.5 0.6 join_pairs.1
  20.0 0.0 collective-permute-done.4.other
  20.1 0.0 copy-start
  20.1 1.2 %copy-done = bf16[4,1088,128]{2,1,0:T(8,128)(2,1)S(1)} copy-done((bf16[4,1088,128]{2,1,0:T(8,128)(2,1)S(1)}, bf16[4,1088,128]{2,1,0:T(8,128)(2,1)}, u32[]{:S(2)}) %copy-start) | copy-done | bytes 1114136
  21.3 0.1 merge_rows.1
  21.5 2.0 %collective-permute-start.5 = (bf16[2,1088,128]{2,1,0:T(8,128)(2,1)S(1)}, bf16[2,1088,128]{2,1,0:T(8,128)(2,1)S(1)}, u32[]{:S(2)}, u32[]{:S(2)}) collective-permute-start(bf16[2,1088,128]{2,1,0:T(8,128)(2,1)S(1)} %get-tuple-element.119), channel_id=1, source_target_pairs={{0,16},{1,17},{2,18},{3,19},{4,20},{5,21},{6,22},{7,23},{8,24},{9,... | collective-permute-start | bytes 1671176 | tf_op jit(solution)/shard_map/ppermute | solution.py:44
  23.5 2.6 %collective-permute-start.7 = (bf16[8,128,128]{2,1,0:T(8,128)(2,1)S(1)}, bf16[8,128,128]{2,1,0:T(8,128)(2,1)S(1)}, u32[]{:S(2)}, u32[]{:S(2)}) collective-permute-start(bf16[8,128,128]{2,1,0:T(8,128)(2,1)S(1)} %get-tuple-element.130), channel_id=1, source_target_pairs={{0,4},{1,5},{2,6},{3,7},{4,0},{5,1},{6,2},{7,3},{8,12},{9,13},{10,... | collective-permute-start | bytes 786440 | tf_op jit(solution)/shard_map/ppermute | solution.py:44
  26.0 0.9 collective-permute-start.8
  27.0 18.0 %all_to_all.10.root_own = bf16[32,16,128]{2,1,0:T(8,128)(2,1)S(1)} all-to-all(bf16[32,16,128]{2,1,0:T(8,128)(2,1)S(1)} %get-tuple-element.122), channel_id=1, replica_groups=mesh['leaf'=8,'x'=4,'y'=4,'core'=2] {'leaf','y'}, dimensions={0} | all-to-all | bytes 262144 | tf_op jit(solution)/shard_map/all_to_all | solution.py:644
  44.9 0.0 collective-permute-done.7
  45.0 0.0 collective-permute-done.8
  45.0 0.0 collective-permute-done.5.refs_1_
  45.0 0.1 pad_maximum_fusion.own
  45.1 3.2 %collective-permute-start.11 = (bf16[4,8,128,128]{3,2,1,0:T(8,128)(2,1)S(1)}, bf16[4,8,128,128]{3,2,1,0:T(8,128)(2,1)S(1)}, u32[]{:S(2)}, u32[]{:S(2)}) collective-permute-start(bf16[4,8,128,128]{3,2,1,0:T(8,128)(2,1)S(1)} %pad_maximum_fusion.own), channel_id=1, source_target_pairs={{0,1},{1,0},{2,3},{3,2},{4,5},{5,4},{6,7},{7,6},{8,9},{9,8},{10,11... | collective-permute-start | bytes 3145736 | tf_op jit(solution)/shard_map/ppermute | solution.py:44
  48.3 0.1 collective-permute-start.12
  48.4 0.8 collective-permute-start.9
  49.2 1.9 %collective-permute-start.10 = (bf16[2,1088,128]{2,1,0:T(8,128)(2,1)S(1)}, bf16[2,1088,128]{2,1,0:T(8,128)(2,1)S(1)}, u32[]{:S(2)}, u32[]{:S(2)}) collective-permute-start(bf16[2,1088,128]{2,1,0:T(8,128)(2,1)S(1)} %get-tuple-element.125), channel_id=1, source_target_pairs={{0,24},{1,25},{2,26},{3,27},{4,28},{5,29},{6,30},{7,31},{8,0},{9,1... | collective-permute-start | bytes 1671176 | tf_op jit(solution)/shard_map/ppermute | solution.py:44
  51.1 0.0 collective-permute-done.12.root_other
  51.1 0.0 collective-permute-done.11.other
  51.1 9.9 %compute_early.1 = (bf16[2,528,128]{2,1,0:T(8,128)(2,1)S(1)}, bf16[2,528,128]{2,1,0:T(8,128)(2,1)S(1)}, f32[34,128,128]{2,1,0:T(8,128)S(1)}, f32[34,128,128]{2,1,0:T(8,128)S(1)}) custom-call(s32[4]{0:T(128)S(1)} %copy-done.4, s32[8,40]{1,0:T(8,128)S(1)} %get-tuple-element.126.lists, s32[8]{0:T(128)S(1)} %get-tuple-element.127.counts, ...), custom_call_target="tpu_custom_call" | custom-call | flops 10000000000 | bytes 16000000 | tf_op jit(solution)/shard_map/compute_early/pallas_call | solution.py:517
  61.0 2.4 %collective-permute-done.9.refs_0_ = bf16[2,1088,128]{2,1,0:T(8,128)(2,1)S(1)} collective-permute-done((bf16[2,1088,128]{2,1,0:T(8,128)(2,1)S(1)}, bf16[2,1088,128]{2,1,0:T(8,128)(2,1)S(1)}, u32[]{:S(2)}, u32[]{:S(2)}) %collective-permute-start.9) | collective-permute-done | bytes 557088 | tf_op jit(solution)/shard_map/ppermute | solution.py:44
  63.4 2.1 %collective-permute-start.13 = (bf16[2,528,128]{2,1,0:T(8,128)(2,1)S(1)}, bf16[2,528,128]{2,1,0:T(8,128)(2,1)S(1)}, u32[]{:S(2)}, u32[]{:S(2)}) collective-permute-start(bf16[2,528,128]{2,1,0:T(8,128)(2,1)S(1)} %get-tuple-element.142), channel_id=1, source_target_pairs={{0,16},{1,17},{2,18},{3,19},{4,20},{5,21},{6,22},{7,23},{8,24},{9,... | collective-permute-start | bytes 811016 | tf_op jit(solution)/shard_map/ppermute | solution.py:44
  65.6 15.1 %compute_late.1 = (bf16[2,528,128]{2,1,0:T(8,128)(2,1)S(1)}, bf16[2,528,128]{2,1,0:T(8,128)(2,1)S(1)}, f32[32,128,128]{2,1,0:T(8,128)S(1)}, bf16[32,128,128]{2,1...) custom-call(s32[4]{0:T(128)S(1)} %copy-done.4, s32[8,40]{1,0:T(8,128)S(1)} %get-tuple-element.126.lists, ...), custom_call_target="tpu_custom_call" | custom-call | flops 10000000000 | bytes 16000000 | tf_op jit(solution)/shard_map/compute_late/pallas_call | solution.py:517
  80.7 0.0 collective-permute-done.13.refs_2_
  80.7 1.9 %collective-permute-start.14 = (bf16[32,128,128]{2,1,0:T(8,128)(2,1)S(1)}, bf16[32,128,128]{2,1,0:T(8,128)(2,1)S(1)}, u32[]{:S(2)}, u32[]{:S(2)}) collective-permute-start(bf16[32,128,128]{2,1,0:T(8,128)(2,1)S(1)} %get-tuple-element.154), channel_id=1, source_target_pairs={{0,1},{1,0},{2,3},{3,2},{4,5},{5,4},{6,7},{7,6},{8,9},{9,8},{10,11... | collective-permute-start | bytes 3145736 | tf_op jit(solution)/shard_map/ppermute | solution.py:44
  82.6 0.1 collective-permute-start.15
  82.7 2.4 %collective-permute-done.15 = f32[32,8,128]{2,1,0:T(8,128)S(1)} collective-permute-done((f32[32,8,128]{2,1,0:T(8,128)S(1)}, f32[32,8,128]{2,1,0:T(8,128)S(1)}, u32[]{:S(2)}, u32[]{:S(2)}) %collective-permute-start.15) | collective-permute-done | bytes 131104 | tf_op jit(solution)/shard_map/ppermute | solution.py:44
  85.1 0.3 join_cores.1
  85.4 0.3 collective-permute-start.16
  85.7 1.0 collective-permute-start.17
  86.7 0.7 collective-permute-start.18
  87.4 14.9 %all_to_all.11.roots = f32[32,8,128]{2,1,0:T(8,128)S(1)} all-to-all(f32[32,8,128]{2,1,0:T(8,128)S(1)} %add.3), channel_id=1, replica_groups=mesh['leaf'=8,'x'=4,'y'=4,'core'=2] {'leaf','y'}, dimensions={0} | all-to-all | bytes 262144 | tf_op jit(solution)/shard_map/all_to_all | solution.py:644
  102.3 0.0 collective-permute-done.17.r2
  102.4 0.0 collective-permute-done.18.r3
  102.4 0.1 collective-permute-start.19
  102.4 1.5 %collective-permute-start.20 = (bf16[2,528,128]{2,1,0:T(8,128)(2,1)S(1)}, bf16[2,528,128]{2,1,0:T(8,128)(2,1)S(1)}, u32[]{:S(2)}, u32[]{:S(2)}) collective-permute-start(bf16[2,528,128]{2,1,0:T(8,128)(2,1)S(1)} %get-tuple-element.169), channel_id=1, source_target_pairs={{0,8},{1,9},{2,10},{3,11},{4,12},{5,13},{6,14},{7,15},{8,16},{9,17... | collective-permute-start | bytes 811016 | tf_op jit(solution)/shard_map/ppermute | solution.py:44
  103.9 0.7 sum_pairs.1
  104.6 0.1 collective-permute-start.21
  104.7 2.5 %collective-permute-start.22 = (f32[2,136,128]{2,1,0:T(8,128)S(1)}, f32[2,136,128]{2,1,0:T(8,128)S(1)}, u32[]{:S(2)}, u32[]{:S(2)}) collective-permute-start(f32[2,136,128]{2,1,0:T(8,128)S(1)} %get-tuple-element.177), channel_id=1, source_target_pairs={{0,16},{1,17},{2,18},{3,19},{4,20},{5,21},{6,22},{7,23},{8,24},{9,... | collective-permute-start | bytes 417800 | tf_op jit(solution)/shard_map/ppermute | solution.py:44
  107.1 0.2 collective-permute-start.23
  107.4 6.2 %collective-permute-done.21.refs_6_ = f32[2,136,128]{2,1,0:T(8,128)S(1)} collective-permute-done((f32[2,136,128]{2,1,0:T(8,128)S(1)}, f32[2,136,128]{2,1,0:T(8,128)S(1)}, u32[]{:S(2)}, u32[]{:S(2)}) %collective-permute-start.21) | collective-permute-done | bytes 139296 | tf_op jit(solution)/shard_map/ppermute | solution.py:44
  113.6 0.6 collective-permute-done.22.refs_7_
  114.2 1.0 collective-permute-done.23.refs_8_
  115.2 0.1 pad_maximum_fusion.1
  115.3 3.5 %collective-permute-start.24 = (bf16[4,528,128]{2,1,0:T(8,128)(2,1)S(1)}, bf16[4,528,128]{2,1,0:T(8,128)(2,1)S(1)}, u32[]{:S(2)}, u32[]{:S(2)}) collective-permute-start(bf16[4,528,128]{2,1,0:T(8,128)(2,1)S(1)} %pad_maximum_fusion.1), channel_id=1, source_target_pairs={{0,1},{1,0},{2,3},{3,2},{4,5},{5,4},{6,7},{7,6},{8,9},{9,8},{10,11... | collective-permute-start | bytes 1622024 | tf_op jit(solution)/shard_map/ppermute | solution.py:44
  118.9 0.1 collective-permute-start.25
  119.0 1.8 %collective-permute-done.25.refs_9_ = f32[4,136,128]{2,1,0:T(8,128)S(1)} collective-permute-done((f32[4,136,128]{2,1,0:T(8,128)S(1)}, f32[4,136,128]{2,1,0:T(8,128)S(1)}, u32[]{:S(2)}, u32[]{:S(2)}) %collective-permute-start.25) | collective-permute-done | bytes 278560 | tf_op jit(solution)/shard_map/ppermute | solution.py:44
  120.8 0.0 collective-permute-done.24.refs_4_
  120.8 2.8 %unpack.1 = (f32[128,4096]{1,0:T(8,128)}, f32[8,4,128]{2,1,0:T(4,128)}, f32[128,1024]{1,0:T(8,128)}, f32[1,1024]{1,0:T(1,128)}) custom-call(s32[4]{0:T(128)S(1)} %copy-done.4, bf16[2,528,128]{2,1,0:T(8,128)(2,1)S(1)} %get-tuple-element.141.refs_0_, bf16[2,528,128]{2,1,0:T(8,128)(2,1)S(1)} %collective-permute-done.19.refs_1_, ...), custom_call_target="tpu_custom_call" | custom-call | tf_op jit(solution)/shard_map/unpack/pallas_call | solution.py:623
  (34 shorter events, 0.2 us)
Async XLA Ops:
  0.6 14.7 %copy-start.6 = (s32[1,24]{1,0:T(1,128)S(1)}, s32[1,24]{1,0:T(1,128)}, u32[]{:S(2)}) copy-start(s32[1,24]{1,0:T(1,128)} %parent.1) | copy-start | bytes 292
  0.6 14.7 %copy-start.7 = (s32[1,24]{1,0:T(1,128)S(1)}, s32[1,24]{1,0:T(1,128)}, u32[]{:S(2)}) copy-start(s32[1,24]{1,0:T(1,128)} %length.1) | copy-start | bytes 292
  0.7 1.0 copy-start.1
  1.7 0.7 copy-start.5
  2.4 6.4 %copy-start.2 = (s32[4]{0:T(128)}, s32[4]{0:T(128)S(1)}, u32[]{:S(2)}) copy-start(s32[4]{0:T(128)S(1)} %pad_add_fusion.ids) | copy-start | bytes 52
  3.0 10.5 %collective-permute-start = (bf16[2,144,128]{2,1,0:T(8,128)(2,1)S(1)}, bf16[2,144,128]{2,1,0:T(8,128)(2,1)S(1)}, u32[]{:S(2)}, u32[]{:S(2)}) collective-permute-start(bf16[2,144,128]{2,1,0:T(8,128)(2,1)S(1)} %get-tuple-element.100), channel_id=1, source_target_pairs={{0,8},{1,9},{2,10},{3,11},{4,12},{5,13},{6,14},{7,15},{8,16},{9,17... | collective-permute-start | bytes 221192 | tf_op jit(solution)/shard_map/ppermute | solution.py:44
  5.1 8.4 %collective-permute-start.1 = (bf16[2,144,128]{2,1,0:T(8,128)(2,1)S(1)}, bf16[2,144,128]{2,1,0:T(8,128)(2,1)S(1)}, u32[]{:S(2)}, u32[]{:S(2)}) collective-permute-start(bf16[2,144,128]{2,1,0:T(8,128)(2,1)S(1)} %get-tuple-element.101), channel_id=1, source_target_pairs={{0,16},{1,17},{2,18},{3,19},{4,20},{5,21},{6,22},{7,23},{8,24},{9,... | collective-permute-start | bytes 221192 | tf_op jit(solution)/shard_map/ppermute | solution.py:44
  7.6 5.9 %collective-permute-start.2 = (bf16[2,144,128]{2,1,0:T(8,128)(2,1)S(1)}, bf16[2,144,128]{2,1,0:T(8,128)(2,1)S(1)}, u32[]{:S(2)}, u32[]{:S(2)}) collective-permute-start(bf16[2,144,128]{2,1,0:T(8,128)(2,1)S(1)} %get-tuple-element.102), channel_id=1, source_target_pairs={{0,24},{1,25},{2,26},{3,27},{4,28},{5,29},{6,30},{7,31},{8,0},{9,1... | collective-permute-start | bytes 221192 | tf_op jit(solution)/shard_map/ppermute | solution.py:44
  13.5 6.5 %collective-permute-start.4 = (bf16[4,1088,128]{2,1,0:T(8,128)(2,1)}, bf16[4,1088,128]{2,1,0:T(8,128)(2,1)S(1)}, u32[]{:S(2)}, u32[]{:S(2)}) collective-permute-start(bf16[4,1088,128]{2,1,0:T(8,128)(2,1)} %get-tuple-element.110), channel_id=1, source_target_pairs={{0,1},{1,0},{2,3},{3,2},{4,5},{5,4},{6,7},{7,6},{8,9},{9,8},{10,11... | collective-permute-start | bytes 3342344 | tf_op jit(solution)/shard_map/ppermute | solution.py:44
  15.2 4.3 %collective-permute-start.3 = (bf16[4,144,128]{2,1,0:T(8,128)(2,1)S(1)}, bf16[4,144,128]{2,1,0:T(8,128)(2,1)S(1)}, u32[]{:S(2)}, u32[]{:S(2)}) collective-permute-start(bf16[4,144,128]{2,1,0:T(8,128)(2,1)S(1)} %pad_maximum_fusion.3), channel_id=1, source_target_pairs={{0,1},{1,0},{2,3},{3,2},{4,5},{5,4},{6,7},{7,6},{8,9},{9,8},{10,11... | collective-permute-start | bytes 442376 | tf_op jit(solution)/shard_map/ppermute | solution.py:44
  15.3 0.7 copy-start.3
  20.1 1.3 %copy-start = (bf16[4,1088,128]{2,1,0:T(8,128)(2,1)S(1)}, bf16[4,1088,128]{2,1,0:T(8,128)(2,1)}, u32[]{:S(2)}) copy-start(bf16[4,1088,128]{2,1,0:T(8,128)(2,1)} %get-tuple-element.109.keep) | copy-start | bytes 3342340
  21.3 29.8 %copy-start.4 = (s32[4]{0:T(128)S(1)}, s32[4]{0:T(128)}, u32[]{:S(2)}) copy-start(s32[4]{0:T(128)} %copy-done.2) | copy-start | bytes 52
  21.5 23.5 %collective-permute-start.5 = (bf16[2,1088,128]{2,1,0:T(8,128)(2,1)S(1)}, bf16[2,1088,128]{2,1,0:T(8,128)(2,1)S(1)}, u32[]{:S(2)}, u32[]{:S(2)}) collective-permute-start(bf16[2,1088,128]{2,1,0:T(8,128)(2,1)S(1)} %get-tuple-element.119), channel_id=1, source_target_pairs={{0,16},{1,17},{2,18},{3,19},{4,20},{5,21},{6,22},{7,23},{8,24},{9,... | collective-permute-start | bytes 1671176 | tf_op jit(solution)/shard_map/ppermute | solution.py:44
  23.5 21.5 %collective-permute-start.6 = (bf16[8,128,128]{2,1,0:T(8,128)(2,1)S(1)}, bf16[8,128,128]{2,1,0:T(8,128)(2,1)S(1)}, u32[]{:S(2)}, u32[]{:S(2)}) collective-permute-start(bf16[8,128,128]{2,1,0:T(8,128)(2,1)S(1)} %get-tuple-element.130), channel_id=1, source_target_pairs={{0,2},{1,3},{2,4},{3,5},{4,6},{5,7},{6,0},{7,1},{8,10},{9,11},{10,... | collective-permute-start | bytes 786440 | tf_op jit(solution)/shard_map/ppermute | solution.py:44
  23.5 21.5 %collective-permute-start.7 = (bf16[8,128,128]{2,1,0:T(8,128)(2,1)S(1)}, bf16[8,128,128]{2,1,0:T(8,128)(2,1)S(1)}, u32[]{:S(2)}, u32[]{:S(2)}) collective-permute-start(bf16[8,128,128]{2,1,0:T(8,128)(2,1)S(1)} %get-tuple-element.130), channel_id=1, source_target_pairs={{0,4},{1,5},{2,6},{3,7},{4,0},{5,1},{6,2},{7,3},{8,12},{9,13},{10,... | collective-permute-start | bytes 786440 | tf_op jit(solution)/shard_map/ppermute | solution.py:44
  26.0 18.9 %collective-permute-start.8 = (bf16[8,128,128]{2,1,0:T(8,128)(2,1)S(1)}, bf16[8,128,128]{2,1,0:T(8,128)(2,1)S(1)}, u32[]{:S(2)}, u32[]{:S(2)}) collective-permute-start(bf16[8,128,128]{2,1,0:T(8,128)(2,1)S(1)} %get-tuple-element.130), channel_id=1, source_target_pairs={{0,6},{1,7},{2,0},{3,1},{4,2},{5,3},{6,4},{7,5},{8,14},{9,15},{10,... | collective-permute-start | bytes 786440 | tf_op jit(solution)/shard_map/ppermute | solution.py:44
  45.1 6.0 %collective-permute-start.11 = (bf16[4,8,128,128]{3,2,1,0:T(8,128)(2,1)S(1)}, bf16[4,8,128,128]{3,2,1,0:T(8,128)(2,1)S(1)}, u32[]{:S(2)}, u32[]{:S(2)}) collective-permute-start(bf16[4,8,128,128]{3,2,1,0:T(8,128)(2,1)S(1)} %pad_maximum_fusion.own), channel_id=1, source_target_pairs={{0,1},{1,0},{2,3},{3,2},{4,5},{5,4},{6,7},{7,6},{8,9},{9,8},{10,11... | collective-permute-start | bytes 3145736 | tf_op jit(solution)/shard_map/ppermute | solution.py:44
  48.3 2.8 %collective-permute-start.12 = (bf16[32,16,128]{2,1,0:T(8,128)(2,1)S(1)}, bf16[32,16,128]{2,1,0:T(8,128)(2,1)S(1)}, u32[]{:S(2)}, u32[]{:S(2)}) collective-permute-start(bf16[32,16,128]{2,1,0:T(8,128)(2,1)S(1)} %all_to_all.10.root_own), channel_id=1, source_target_pairs={{0,1},{1,0},{2,3},{3,2},{4,5},{5,4},{6,7},{7,6},{8,9},{9,8},{10,11... | collective-permute-start | bytes 393224 | tf_op jit(solution)/shard_map/ppermute | solution.py:44
  48.4 15.0 %collective-permute-start.9 = (bf16[2,1088,128]{2,1,0:T(8,128)(2,1)S(1)}, bf16[2,1088,128]{2,1,0:T(8,128)(2,1)S(1)}, u32[]{:S(2)}, u32[]{:S(2)}) collective-permute-start(bf16[2,1088,128]{2,1,0:T(8,128)(2,1)S(1)} %get-tuple-element.124), channel_id=1, source_target_pairs={{0,8},{1,9},{2,10},{3,11},{4,12},{5,13},{6,14},{7,15},{8,16},{9,17... | collective-permute-start | bytes 1671176 | tf_op jit(solution)/shard_map/ppermute | solution.py:44
  49.2 14.2 %collective-permute-start.10 = (bf16[2,1088,128]{2,1,0:T(8,128)(2,1)S(1)}, bf16[2,1088,128]{2,1,0:T(8,128)(2,1)S(1)}, u32[]{:S(2)}, u32[]{:S(2)}) collective-permute-start(bf16[2,1088,128]{2,1,0:T(8,128)(2,1)S(1)} %get-tuple-element.125), channel_id=1, source_target_pairs={{0,24},{1,25},{2,26},{3,27},{4,28},{5,29},{6,30},{7,31},{8,0},{9,1... | collective-permute-start | bytes 1671176 | tf_op jit(solution)/shard_map/ppermute | solution.py:44
  63.4 17.3 %collective-permute-start.13 = (bf16[2,528,128]{2,1,0:T(8,128)(2,1)S(1)}, bf16[2,528,128]{2,1,0:T(8,128)(2,1)S(1)}, u32[]{:S(2)}, u32[]{:S(2)}) collective-permute-start(bf16[2,528,128]{2,1,0:T(8,128)(2,1)S(1)} %get-tuple-element.142), channel_id=1, source_target_pairs={{0,16},{1,17},{2,18},{3,19},{4,20},{5,21},{6,22},{7,23},{8,24},{9,... | collective-permute-start | bytes 811016 | tf_op jit(solution)/shard_map/ppermute | solution.py:44
  80.7 4.4 %collective-permute-start.14 = (bf16[32,128,128]{2,1,0:T(8,128)(2,1)S(1)}, bf16[32,128,128]{2,1,0:T(8,128)(2,1)S(1)}, u32[]{:S(2)}, u32[]{:S(2)}) collective-permute-start(bf16[32,128,128]{2,1,0:T(8,128)(2,1)S(1)} %get-tuple-element.154), channel_id=1, source_target_pairs={{0,1},{1,0},{2,3},{3,2},{4,5},{5,4},{6,7},{7,6},{8,9},{9,8},{10,11... | collective-permute-start | bytes 3145736 | tf_op jit(solution)/shard_map/ppermute | solution.py:44
  82.6 2.5 %collective-permute-start.15 = (f32[32,8,128]{2,1,0:T(8,128)S(1)}, f32[32,8,128]{2,1,0:T(8,128)S(1)}, u32[]{:S(2)}, u32[]{:S(2)}) collective-permute-start(f32[32,8,128]{2,1,0:T(8,128)S(1)} %get-tuple-element.157), channel_id=1, source_target_pairs={{0,1},{1,0},{2,3},{3,2},{4,5},{5,4},{6,7},{7,6},{8,9},{9,8},{10,11... | collective-permute-start | bytes 393224 | tf_op jit(solution)/shard_map/ppermute | solution.py:44
  85.4 16.9 %collective-permute-start.16 = (bf16[8,128,128]{2,1,0:T(8,128)(2,1)S(1)}, bf16[8,128,128]{2,1,0:T(8,128)(2,1)S(1)}, u32[]{:S(2)}, u32[]{:S(2)}) collective-permute-start(bf16[8,128,128]{2,1,0:T(8,128)(2,1)S(1)} %get-tuple-element.165), channel_id=1, source_target_pairs={{0,6},{1,7},{2,0},{3,1},{4,2},{5,3},{6,4},{7,5},{8,14},{9,15},{10,... | collective-permute-start | bytes 786440 | tf_op jit(solution)/shard_map/ppermute | solution.py:44
  85.7 16.6 %collective-permute-start.17 = (bf16[8,128,128]{2,1,0:T(8,128)(2,1)S(1)}, bf16[8,128,128]{2,1,0:T(8,128)(2,1)S(1)}, u32[]{:S(2)}, u32[]{:S(2)}) collective-permute-start(bf16[8,128,128]{2,1,0:T(8,128)(2,1)S(1)} %get-tuple-element.166), channel_id=1, source_target_pairs={{0,4},{1,5},{2,6},{3,7},{4,0},{5,1},{6,2},{7,3},{8,12},{9,13},{10,... | collective-permute-start | bytes 786440 | tf_op jit(solution)/shard_map/ppermute | solution.py:44
  86.7 15.6 %collective-permute-start.18 = (bf16[8,128,128]{2,1,0:T(8,128)(2,1)S(1)}, bf16[8,128,128]{2,1,0:T(8,128)(2,1)S(1)}, u32[]{:S(2)}, u32[]{:S(2)}) collective-permute-start(bf16[8,128,128]{2,1,0:T(8,128)(2,1)S(1)} %get-tuple-element.167), channel_id=1, source_target_pairs={{0,2},{1,3},{2,4},{3,5},{4,6},{5,7},{6,0},{7,1},{8,10},{9,11},{10,... | collective-permute-start | bytes 786440 | tf_op jit(solution)/shard_map/ppermute | solution.py:44
  102.4 12.8 %collective-permute-start.19 = (bf16[2,528,128]{2,1,0:T(8,128)(2,1)S(1)}, bf16[2,528,128]{2,1,0:T(8,128)(2,1)S(1)}, u32[]{:S(2)}, u32[]{:S(2)}) collective-permute-start(bf16[2,528,128]{2,1,0:T(8,128)(2,1)S(1)} %get-tuple-element.168), channel_id=1, source_target_pairs={{0,24},{1,25},{2,26},{3,27},{4,28},{5,29},{6,30},{7,31},{8,0},{9,1... | collective-permute-start | bytes 811016 | tf_op jit(solution)/shard_map/ppermute | solution.py:44
  102.4 12.7 %collective-permute-start.20 = (bf16[2,528,128]{2,1,0:T(8,128)(2,1)S(1)}, bf16[2,528,128]{2,1,0:T(8,128)(2,1)S(1)}, u32[]{:S(2)}, u32[]{:S(2)}) collective-permute-start(bf16[2,528,128]{2,1,0:T(8,128)(2,1)S(1)} %get-tuple-element.169), channel_id=1, source_target_pairs={{0,8},{1,9},{2,10},{3,11},{4,12},{5,13},{6,14},{7,15},{8,16},{9,17... | collective-permute-start | bytes 811016 | tf_op jit(solution)/shard_map/ppermute | solution.py:44
  104.6 9.0 %collective-permute-start.21 = (f32[2,136,128]{2,1,0:T(8,128)S(1)}, f32[2,136,128]{2,1,0:T(8,128)S(1)}, u32[]{:S(2)}, u32[]{:S(2)}) collective-permute-start(f32[2,136,128]{2,1,0:T(8,128)S(1)} %get-tuple-element.176), channel_id=1, source_target_pairs={{0,8},{1,9},{2,10},{3,11},{4,12},{5,13},{6,14},{7,15},{8,16},{9,17... | collective-permute-start | bytes 417800 | tf_op jit(solution)/shard_map/ppermute | solution.py:44
  104.7 9.5 %collective-permute-start.22 = (f32[2,136,128]{2,1,0:T(8,128)S(1)}, f32[2,136,128]{2,1,0:T(8,128)S(1)}, u32[]{:S(2)}, u32[]{:S(2)}) collective-permute-start(f32[2,136,128]{2,1,0:T(8,128)S(1)} %get-tuple-element.177), channel_id=1, source_target_pairs={{0,16},{1,17},{2,18},{3,19},{4,20},{5,21},{6,22},{7,23},{8,24},{9,... | collective-permute-start | bytes 417800 | tf_op jit(solution)/shard_map/ppermute | solution.py:44
  107.1 8.0 %collective-permute-start.23 = (f32[2,136,128]{2,1,0:T(8,128)S(1)}, f32[2,136,128]{2,1,0:T(8,128)S(1)}, u32[]{:S(2)}, u32[]{:S(2)}) collective-permute-start(f32[2,136,128]{2,1,0:T(8,128)S(1)} %get-tuple-element.178), channel_id=1, source_target_pairs={{0,24},{1,25},{2,26},{3,27},{4,28},{5,29},{6,30},{7,31},{8,0},{9,1... | collective-permute-start | bytes 417800 | tf_op jit(solution)/shard_map/ppermute | solution.py:44
  115.3 5.5 %collective-permute-start.24 = (bf16[4,528,128]{2,1,0:T(8,128)(2,1)S(1)}, bf16[4,528,128]{2,1,0:T(8,128)(2,1)S(1)}, u32[]{:S(2)}, u32[]{:S(2)}) collective-permute-start(bf16[4,528,128]{2,1,0:T(8,128)(2,1)S(1)} %pad_maximum_fusion.1), channel_id=1, source_target_pairs={{0,1},{1,0},{2,3},{3,2},{4,5},{5,4},{6,7},{7,6},{8,9},{9,8},{10,11... | collective-permute-start | bytes 1622024 | tf_op jit(solution)/shard_map/ppermute | solution.py:44
  118.9 1.9 %collective-permute-start.25 = (f32[4,136,128]{2,1,0:T(8,128)S(1)}, f32[4,136,128]{2,1,0:T(8,128)S(1)}, u32[]{:S(2)}, u32[]{:S(2)}) collective-permute-start(f32[4,136,128]{2,1,0:T(8,128)S(1)} %pad_maximum_fusion.2), channel_id=1, source_target_pairs={{0,1},{1,0},{2,3},{3,2},{4,5},{5,4},{6,7},{7,6},{8,9},{9,8},{10,11... | collective-permute-start | bytes 835592 | tf_op jit(solution)/shard_map/ppermute | solution.py:44

commit v4 on v3

--- a/solution.py
+++ b/solution.py
@@ -80,6 +80,7 @@
         if n > 0:
             bits = bits | anc[parent[0, n]]
         anc[n] = bits
+        begin = total
         first = total // BLK
         total = total + length[0, n]
         last = (total - 1) // BLK
@@ -87,20 +88,17 @@
         def mark(block, carry):
             kmask[block] = kmask[block] | jnp.int32(1 << n)
             qmask[block] = qmask[block] | bits
+            inside = iota((BLK, BLK), 0) + block * BLK >= begin
+            kbit[block] = jnp.where(inside, jnp.int32(1 << n), kbit[block])
             return carry
 
         lax.fori_loop(first, last + 1, mark, 0)
     positions = iota((TREE_BLOCKS, BLK), 0) * BLK + iota((TREE_BLOCKS, BLK), 1)
     table = jnp.full((TREE_BLOCKS, BLK), ROOT_BIT, jnp.int32)
-    own_bits = jnp.zeros((TREE_BLOCKS, BLK), jnp.int32)
     for n in range(NODES):
         inside = positions >= start[n]
         table = jnp.where(inside, anc[n] | ROOT_BIT, table)
-        own_bits = jnp.where(inside, jnp.int32(1 << n), own_bits)
     qanc[...] = table
-    for block in range(TREE_BLOCKS):
-        row = jnp.broadcast_to(own_bits[block : block + 1, :], (BLK, BLK))
-        kbit[block] = row.T
     kbit[TREE_BLOCKS] = jnp.zeros((BLK, BLK), jnp.int32)
     for block in range(ROOT_BLOCK, ALL_BLOCKS):
         kbit[block] = jnp.full((BLK, BLK), ROOT_BIT, jnp.int32)
@@ -588,21 +586,37 @@
     )(ids, stay, *received, roots)
 
 
-def unpack_kernel(ids, *refs):
+def unpack_pairs_kernel(ids, s0, s1, s2, s3, crossed, out, root_out):
     x, c = ids[0], ids[2]
-    back, crossed, sums, crossed_sums = refs[0:4], refs[4], refs[5:9], refs[9]
-    out, root_out, pair_out, root_pair_out, held, pairs, sems = refs[10:]
-    for k in range(4):
+    for k, straight in enumerate((s0, s1, s2, s3)):
         for dc in range(2):
             kind = flip(c, dc)
-            part = crossed_sums[k] if dc else sums[k][0]
+            part = crossed[k] if dc else straight[0]
             scale = jnp.where(kind == 0, FACTOR, 1.0).astype(F4)
             col = kind * 512 + lax.rem(x - k + 4, 4) * HD
             cols = pl.ds(pl.multiple_of(col, HD), HD)
-            pairs[:, cols] = part[0:BLK] * scale
-            root_pair_out[:, cols] = part[BLK : BLK + 1] * scale
-    copies = [pltpu.make_async_copy(pairs, pair_out, sems.at[8])]
-    copies[0].start()
+            out[:, cols] = part[0:BLK] * scale
+            root_out[:, cols] = part[BLK : BLK + 1] * scale
+
+
+def unpack_pairs(ids, sums, crossed):
+    return pl.pallas_call(
+        unpack_pairs_kernel,
+        in_specs=[smem()] + [vmem()] * 5,
+        out_specs=[vmem()] * 2,
+        out_shape=[
+            jax.ShapeDtypeStruct((BLK, 1024), F4),
+            jax.ShapeDtypeStruct((1, 1024), F4),
+        ],
+        compiler_params=params(),
+        name="unpack_pairs",
+    )(ids, *sums, crossed)
+
+
+def unpack_query_kernel(ids, *refs):
+    x, c = ids[0], ids[2]
+    back, crossed, out, root_out, held, sems = refs[0:4], *refs[4:]
+    copies = []
     for i in range(8):
         k, dc = i // 2, i % 2
         dest = lax.rem(x + k, 4) * 2 + flip(c, dc)
@@ -618,26 +632,22 @@
         copy.wait()
 
 
-def unpack(ids, back, crossed, sums, crossed_sums):
-    anywhere = pl.BlockSpec(memory_space=pl.ANY)
-    return pl.pallas_call(
-        unpack_kernel,
-        in_specs=[smem()] + [vmem()] * 10,
-        out_specs=[anywhere, vmem(), anywhere, vmem()],
+def unpack_query(ids, back, crossed):
+    return pl.pallas_call(
+        unpack_query_kernel,
+        in_specs=[smem()] + [vmem()] * 5,
+        out_specs=[pl.BlockSpec(memory_space=pl.ANY), vmem()],
         out_shape=[
             jax.ShapeDtypeStruct((BLK, 4096), F4),
             jax.ShapeDtypeStruct((8, 4, HD), F4),
-            jax.ShapeDtypeStruct((BLK, 1024), F4),
-            jax.ShapeDtypeStruct((1, 1024), F4),
         ],
-        scratch_shapes=[
-            pltpu.VMEM((BLK, 4096), F4),
-            pltpu.VMEM((BLK, 1024), F4),
-            pltpu.SemaphoreType.DMA((9,)),
-        ],
+        scratch_shapes=[pltpu.VMEM((BLK, 4096), F4), pltpu.SemaphoreType.DMA((8,))],
         compiler_params=params(),
-        name="unpack",
-    )(ids, *back, crossed, *sums, crossed_sums)
+        cost_estimate=pl.CostEstimate(
+            flops=10**6, bytes_accessed=4 * 10**6, transcendentals=0
+        ),
+        name="unpack_query",
+    )(ids, *back, crossed)
 
 
 def along(array):
@@ -710,20 +720,19 @@
     stay, root_sums, *low = together((stay, root_sums, *low))
 
     received = [shift(low[ky - 1], dy=-ky) for ky in range(1, 4)]
+    back1, back3 = shift(part1, dx=-1), shift(part3, dx=-3)
     roots = along(root_sums)
-    stay, roots, part1, part3, *received = together((stay, roots, part1, part3, *received))
+    stay, roots, back1, back3, *received = together((stay, roots, back1, back3, *received))
 
     sums = sum_pairs(ids, stay, received, roots)
     sums = [sums[0]] + [shift(sums[k], dx=k) for k in range(1, 4)]
-    back1, back3 = shift(part1, dx=-1), shift(part3, dx=-3)
-    back1, back3, *sums = together((back1, back3, *sums))
-
     back = [part0, back1, back2, back3]
     crossed = shift(jnp.stack([part[1] for part in back], axis=0), dc=1)
+    grad_query, grad_query_root = unpack_query(ids, back, crossed)
+    grad_query, grad_query_root, *sums = together((grad_query, grad_query_root, *sums))
+
     crossed_sums = shift(jnp.stack([part[1] for part in sums], axis=0), dc=1)
-    grad_query, grad_query_root, grad_pairs, grad_root = unpack(
-        ids, back, crossed, sums, crossed_sums
-    )
+    grad_pairs, grad_root = unpack_pairs(ids, sums, crossed_sums)
     return grad_query, grad_query_root.reshape(1, 4096), grad_pairs, grad_root
 
 

time: 124 us -> 124 us (level)
  blocking collectives: 32.9 us -> 18 us
  starting transfers between devices: 33.1 us -> 44.5 us
  waiting for transfers between devices: 14.4 us -> 18 us
  other arithmetic: 0.35 us -> 1.91 us
  Pallas kernels: 38.3 us -> 36.9 us
    all_to_all x2 -> x1, blocking collectives: 32.9 us -> 18 us  [along(): return lax.all_to_all(array, ('leaf', 'y'), 0, 0, tiled=True)]
    all_to_all x0 -> x1, starting transfers between devices: none -> 9.09 us  [along(): return lax.all_to_all(array, ('leaf', 'y'), 0, 0, tiled=True)]
    all_to_all x0 -> x1, waiting for transfers between devices: none -> 8.66 us  [along(): return lax.all_to_all(array, ('leaf', 'y'), 0, 0, tiled=True)]
    ppermute x26, waiting for transfers between devices: 14.4 us -> 9.34 us  [shift(): return lax.ppermute(array, ('x', 'y', 'core'), perm(dx, dy, dc))]
    pallas_call x2, Pallas kernels: 25 us -> 22 us  [compute(): pl.pallas_call(functools.partial(compute_kernel, ks), in_specs=[smem()] *...]
    ppermute x26, starting transfers between devices: 33.1 us -> 35.4 us  [shift(): return lax.ppermute(array, ('x', 'y', 'core'), perm(dx, dy, dc))]
    pallas_call x1 -> x2, Pallas kernels: 2.8 us -> 3.99 us  [the longest x1 2.58 us: unpack_query(): pl.pallas_call(unpack_query_kernel, in_specs=[smem()] + [vmem()] * 5, out...]
  transfers between devices with their start and end apart: 26 -> 27, of which waited for: 6 -> 7; matrix products, arithmetic and copies ran while one was open for 0% -> 1% of each run, Pallas kernels for 28% -> 28%
where the time goes in v4:
time: 124 us
  starting transfers between devices  44.5 us (36%)
  Pallas kernels  36.9 us (30%)
  waiting for transfers between devices  18 us (15%)
  blocking collectives  18 us (15%)
  local copies, waits for them, and re-layouts  4.28 us (3%)
  other arithmetic  1.91 us (2%)
    ppermute x26, starting transfers between devices, shift(): return lax.ppermute(array, ('x', 'y', 'core'), perm(dx, dy, dc))  35.4 us
    pallas_call x2, Pallas kernels, compute(): pl.pallas_call(functools.partial(compute_kernel, ks), in_specs=[smem()] *...  22 us
    all_to_all x1, blocking collectives, along(): return lax.all_to_all(array, ('leaf', 'y'), 0, 0, tiled=True)  18 us
    ppermute x26, waiting for transfers between devices, shift(): return lax.ppermute(array, ('x', 'y', 'core'), perm(dx, dy, dc))  9.34 us
    all_to_all x1, starting transfers between devices, along(): return lax.all_to_all(array, ('leaf', 'y'), 0, 0, tiled=True)  9.09 us
    all_to_all x1, waiting for transfers between devices, along(): return lax.all_to_all(array, ('leaf', 'y'), 0, 0, tiled=True)  8.66 us
    pallas_call x1, Pallas kernels, pack_rows(): pl.pallas_call(pack_rows_kernel, in_specs=[smem()] + [pl.BlockSpec(memory...  4.72 us
    unnamed x16, local copies, waits for them, and re-layouts  3.55 us
  transfers between devices with their start and end apart: 27, of which 7 were waited for; matrix products, arithmetic and copies ran while one was open for 1% of the time, Pallas kernels for 28%

profile of v4, /device:TPU:1, one launch (start us, length us, event | category | flops | bytes accessed | tf_op | source)
XLA Modules:
  0.0 124.4 jit_solution(616170025146978920)
XLA Ops:
  0.7 0.1 pad_add_fusion.ids
  0.7 0.9 copy-done.1
  1.7 0.7 copy-done.5
  2.4 0.6 pack_pairs.1
  3.0 2.1 %collective-permute-start = (bf16[2,144,128]{2,1,0:T(8,128)(2,1)S(1)}, bf16[2,144,128]{2,1,0:T(8,128)(2,1)S(1)}, u32[]{:S(2)}, u32[]{:S(2)}) collective-permute-start(bf16[2,144,128]{2,1,0:T(8,128)(2,1)S(1)} %get-tuple-element.100), channel_id=1, source_target_pairs={{0,8},{1,9},{2,10},{3,11},{4,12},{5,13},{6,14},{7,15},{8,16},{9,17... | collective-permute-start | bytes 221192 | tf_op jit(solution)/shard_map/ppermute | solution.py:44
  5.1 2.5 %collective-permute-start.1 = (bf16[2,144,128]{2,1,0:T(8,128)(2,1)S(1)}, bf16[2,144,128]{2,1,0:T(8,128)(2,1)S(1)}, u32[]{:S(2)}, u32[]{:S(2)}) collective-permute-start(bf16[2,144,128]{2,1,0:T(8,128)(2,1)S(1)} %get-tuple-element.101), channel_id=1, source_target_pairs={{0,16},{1,17},{2,18},{3,19},{4,20},{5,21},{6,22},{7,23},{8,24},{9,... | collective-permute-start | bytes 221192 | tf_op jit(solution)/shard_map/ppermute | solution.py:44
  7.6 1.2 collective-permute-start.2
  8.7 4.7 %pack_rows.1 = (bf16[4,1088,128]{2,1,0:T(8,128)(2,1)}, bf16[4,1088,128]{2,1,0:T(8,128)(2,1)}) custom-call(s32[4]{0:T(128)} %copy-done.2, bf16[128,4096]{1,0:T(8,128)(2,1)} %refs_0_.1, bf16[128,4096]{1,0:T(8,128)(2,1)} %refs_1_.1, bf16[128,4096]{1,0:T(8,128)(2,1)} %refs_2_.1, f32[32,128]{1,0:T(8,128)} %refs_3_.1, bf16[1,4096]{1,0:T(2,128)(2,1)} %refs_4_.1, ...), custom_call_target="tpu_custom_call" | custom-call | tf_op jit(solution)/shard_map/pack_rows/pallas_call | solution.py:255
  13.5 0.0 collective-permute-done.g1
  13.5 0.0 collective-permute-done.1.g2
  13.5 0.0 collective-permute-done.2.g3
  13.5 1.6 %collective-permute-start.4 = (bf16[4,1088,128]{2,1,0:T(8,128)(2,1)}, bf16[4,1088,128]{2,1,0:T(8,128)(2,1)S(1)}, u32[]{:S(2)}, u32[]{:S(2)}) collective-permute-start(bf16[4,1088,128]{2,1,0:T(8,128)(2,1)} %get-tuple-element.110), channel_id=1, source_target_pairs={{0,1},{1,0},{2,3},{3,2},{4,5},{5,4},{6,7},{7,6},{8,9},{9,8},{10,11... | collective-permute-start | bytes 3342344 | tf_op jit(solution)/shard_map/ppermute | solution.py:44
  15.2 0.1 collective-permute-start.3
  15.3 0.0 copy-start.3
  15.3 0.6 copy-done.3
  15.9 3.2 %tables.1 = (s32[35,128,128]{2,1,0:T(8,128)S(1)}, s32[32,128]{1,0:T(8,128)S(1)}, s32[8,40]{1,0:T(8,128)S(1)}, s32[8]{0:T(128)S(1)}) custom-call(s32[4]{0:T(128)S(1)} %copy-done.3, s32[1,24]{1,0:T(1,128)S(1)} %copy-done.6, s32[1,24]{1,0:T(1,128)S(1)} %copy-done.7), custom_call_target="tpu_custom_call" | custom-call | flops 1000000 | bytes 4000000 | tf_op jit(solution)/shard_map/tables/pallas_call | solution.py:122
  19.2 0.6 join_pairs.1
  19.8 0.0 copy-start
  19.8 1.2 copy-done
  21.0 0.1 merge_rows.1
  21.2 2.0 %collective-permute-start.5 = (bf16[2,1088,128]{2,1,0:T(8,128)(2,1)S(1)}, bf16[2,1088,128]{2,1,0:T(8,128)(2,1)S(1)}, u32[]{:S(2)}, u32[]{:S(2)}) collective-permute-start(bf16[2,1088,128]{2,1,0:T(8,128)(2,1)S(1)} %get-tuple-element.119), channel_id=1, source_target_pairs={{0,16},{1,17},{2,18},{3,19},{4,20},{5,21},{6,22},{7,23},{8,24},{9,... | collective-permute-start | bytes 1671176 | tf_op jit(solution)/shard_map/ppermute | solution.py:44
  23.2 2.6 %collective-permute-start.7 = (bf16[8,128,128]{2,1,0:T(8,128)(2,1)S(1)}, bf16[8,128,128]{2,1,0:T(8,128)(2,1)S(1)}, u32[]{:S(2)}, u32[]{:S(2)}) collective-permute-start(bf16[8,128,128]{2,1,0:T(8,128)(2,1)S(1)} %get-tuple-element.130), channel_id=1, source_target_pairs={{0,4},{1,5},{2,6},{3,7},{4,0},{5,1},{6,2},{7,3},{8,12},{9,13},{10,... | collective-permute-start | bytes 786440 | tf_op jit(solution)/shard_map/ppermute | solution.py:44
  25.8 0.9 collective-permute-start.8
  26.7 18.0 %all_to_all.10.root_own = bf16[32,16,128]{2,1,0:T(8,128)(2,1)S(1)} all-to-all(bf16[32,16,128]{2,1,0:T(8,128)(2,1)S(1)} %get-tuple-element.122), channel_id=1, replica_groups=mesh['leaf'=8,'x'=4,'y'=4,'core'=2] {'leaf','y'}, dimensions={0} | all-to-all | bytes 262144 | tf_op jit(solution)/shard_map/all_to_all | solution.py:654
  44.7 0.0 collective-permute-done.5.refs_1_
  44.7 0.1 pad_maximum_fusion.own
  44.8 3.2 %collective-permute-start.11 = (bf16[4,8,128,128]{3,2,1,0:T(8,128)(2,1)S(1)}, bf16[4,8,128,128]{3,2,1,0:T(8,128)(2,1)S(1)}, u32[]{:S(2)}, u32[]{:S(2)}) collective-permute-start(bf16[4,8,128,128]{3,2,1,0:T(8,128)(2,1)S(1)} %pad_maximum_fusion.own), channel_id=1, source_target_pairs={{0,1},{1,0},{2,3},{3,2},{4,5},{5,4},{6,7},{7,6},{8,9},{9,8},{10,11... | collective-permute-start | bytes 3145736 | tf_op jit(solution)/shard_map/ppermute | solution.py:44
  48.0 0.1 collective-permute-start.12
  48.1 0.8 collective-permute-start.9
  48.9 1.9 %collective-permute-start.10 = (bf16[2,1088,128]{2,1,0:T(8,128)(2,1)S(1)}, bf16[2,1088,128]{2,1,0:T(8,128)(2,1)S(1)}, u32[]{:S(2)}, u32[]{:S(2)}) collective-permute-start(bf16[2,1088,128]{2,1,0:T(8,128)(2,1)S(1)} %get-tuple-element.125), channel_id=1, source_target_pairs={{0,24},{1,25},{2,26},{3,27},{4,28},{5,29},{6,30},{7,31},{8,0},{9,1... | collective-permute-start | bytes 1671176 | tf_op jit(solution)/shard_map/ppermute | solution.py:44
  50.8 0.0 collective-permute-done.11.other
  50.8 9.1 %compute_early.1 = (bf16[2,528,128]{2,1,0:T(8,128)(2,1)S(1)}, bf16[2,528,128]{2,1,0:T(8,128)(2,1)S(1)}, f32[34,128,128]{2,1,0:T(8,128)S(1)}, f32[34,128,128]{2,1,0:T(8,128)S(1)}) custom-call(s32[4]{0:T(128)S(1)} %copy-done.4, s32[8,40]{1,0:T(8,128)S(1)} %get-tuple-element.126.lists, s32[8]{0:T(128)S(1)} %get-tuple-element.127.counts, ...), custom_call_target="tpu_custom_call" | custom-call | flops 10000000000 | bytes 16000000 | tf_op jit(solution)/shard_map/compute_early/pallas_call | solution.py:515
  59.9 3.2 %collective-permute-done.9.refs_0_ = bf16[2,1088,128]{2,1,0:T(8,128)(2,1)S(1)} collective-permute-done((bf16[2,1088,128]{2,1,0:T(8,128)(2,1)S(1)}, bf16[2,1088,128]{2,1,0:T(8,128)(2,1)S(1)}, u32[]{:S(2)}, u32[]{:S(2)}) %collective-permute-start.9) | collective-permute-done | bytes 557088 | tf_op jit(solution)/shard_map/ppermute | solution.py:44
  63.1 2.1 %collective-permute-start.13 = (bf16[2,528,128]{2,1,0:T(8,128)(2,1)S(1)}, bf16[2,528,128]{2,1,0:T(8,128)(2,1)S(1)}, u32[]{:S(2)}, u32[]{:S(2)}) collective-permute-start(bf16[2,528,128]{2,1,0:T(8,128)(2,1)S(1)} %get-tuple-element.142), channel_id=1, source_target_pairs={{0,16},{1,17},{2,18},{3,19},{4,20},{5,21},{6,22},{7,23},{8,24},{9,... | collective-permute-start | bytes 811016 | tf_op jit(solution)/shard_map/ppermute | solution.py:44
  65.3 12.9 %compute_late.1 = (bf16[2,528,128]{2,1,0:T(8,128)(2,1)S(1)}, bf16[2,528,128]{2,1,0:T(8,128)(2,1)S(1)}, f32[32,128,128]{2,1,0:T(8,128)S(1)}, bf16[32,128,128]{2,1...) custom-call(s32[4]{0:T(128)S(1)} %copy-done.4, s32[8,40]{1,0:T(8,128)S(1)} %get-tuple-element.126.lists, ...), custom_call_target="tpu_custom_call" | custom-call | flops 10000000000 | bytes 16000000 | tf_op jit(solution)/shard_map/compute_late/pallas_call | solution.py:515
  78.2 1.9 %collective-permute-start.14 = (bf16[32,128,128]{2,1,0:T(8,128)(2,1)S(1)}, bf16[32,128,128]{2,1,0:T(8,128)(2,1)S(1)}, u32[]{:S(2)}, u32[]{:S(2)}) collective-permute-start(bf16[32,128,128]{2,1,0:T(8,128)(2,1)S(1)} %get-tuple-element.154), channel_id=1, source_target_pairs={{0,1},{1,0},{2,3},{3,2},{4,5},{5,4},{6,7},{7,6},{8,9},{9,8},{10,11... | collective-permute-start | bytes 3145736 | tf_op jit(solution)/shard_map/ppermute | solution.py:44
  80.1 0.1 collective-permute-start.15
  80.2 0.0 collective-permute-start.16
  80.2 1.5 %collective-permute-start.17 = (bf16[2,528,128]{2,1,0:T(8,128)(2,1)S(1)}, bf16[2,528,128]{2,1,0:T(8,128)(2,1)S(1)}, u32[]{:S(2)}, u32[]{:S(2)}) collective-permute-start(bf16[2,528,128]{2,1,0:T(8,128)(2,1)S(1)} %get-tuple-element.164), channel_id=1, source_target_pairs={{0,8},{1,9},{2,10},{3,11},{4,12},{5,13},{6,14},{7,15},{8,16},{9,17... | collective-permute-start | bytes 811016 | tf_op jit(solution)/shard_map/ppermute | solution.py:44
  81.7 0.9 collective-permute-done.15
  82.6 0.7 add.3
  83.3 0.9 join_cores.1
  84.2 0.0 collective-permute-start.18
  84.2 3.8 %collective-permute-start.19 = (bf16[8,128,128]{2,1,0:T(8,128)(2,1)}, bf16[8,128,128]{2,1,0:T(8,128)(2,1)S(1)}, u32[]{:S(2)}, u32[]{:S(2)}) collective-permute-start(bf16[8,128,128]{2,1,0:T(8,128)(2,1)} %get-tuple-element.166), channel_id=1, source_target_pairs={{0,4},{1,5},{2,6},{3,7},{4,0},{5,1},{6,2},{7,3},{8,12},{9,13},{10,... | collective-permute-start | bytes 786440 | tf_op jit(solution)/shard_map/ppermute | solution.py:44
  88.1 9.1 %all-to-all-start.1 = ((f32[32,8,128]{2,1,0:T(8,128)}), f32[32,8,128]{2,1,0:T(8,128)S(1)}, u32[]{:S(2)}, u32[]{:S(2)}) async-start(f32[32,8,128]{2,1,0:T(8,128)} %add.3), calls=%async_computation.1 | async-start | bytes 262144 | tf_op jit(solution)/shard_map/all_to_all | solution.py:654
  97.2 0.7 slice.42
  97.8 0.0 collective-permute-done.16.refs_1_
  97.9 8.7 %all-to-all-done.1.roots = f32[32,8,128]{2,1,0:T(8,128)S(1)} async-done(((f32[32,8,128]{2,1,0:T(8,128)}), f32[32,8,128]{2,1,0:T(8,128)S(1)}, u32[]{:S(2)}, u32[]{:S(2)}) %all-to-all-start.1) | async-done | bytes 131104 | tf_op jit(solution)/shard_map/all_to_all | solution.py:654
  106.5 0.0 collective-permute-done.18.r1
  106.5 0.0 collective-permute-done.19.r2
  106.5 0.0 collective-permute-done.20.r3
  106.6 1.0 pad_maximum_fusion.1
  107.5 2.5 %collective-permute-start.21 = (bf16[4,528,128]{2,1,0:T(8,128)(2,1)S(1)}, bf16[4,528,128]{2,1,0:T(8,128)(2,1)S(1)}, u32[]{:S(2)}, u32[]{:S(2)}) collective-permute-start(bf16[4,528,128]{2,1,0:T(8,128)(2,1)S(1)} %pad_maximum_fusion.1), channel_id=1, source_target_pairs={{0,1},{1,0},{2,3},{3,2},{4,5},{5,4},{6,7},{7,6},{8,9},{9,8},{10,11... | collective-permute-start | bytes 1622024 | tf_op jit(solution)/shard_map/ppermute | solution.py:44
  110.0 0.7 sum_pairs.1
  110.7 0.4 collective-permute-start.22
  111.1 2.3 %collective-permute-start.23 = (f32[2,136,128]{2,1,0:T(8,128)S(1)}, f32[2,136,128]{2,1,0:T(8,128)S(1)}, u32[]{:S(2)}, u32[]{:S(2)}) collective-permute-start(f32[2,136,128]{2,1,0:T(8,128)S(1)} %get-tuple-element.180), channel_id=1, source_target_pairs={{0,16},{1,17},{2,18},{3,19},{4,20},{5,21},{6,22},{7,23},{8,24},{9,... | collective-permute-start | bytes 417800 | tf_op jit(solution)/shard_map/ppermute | solution.py:44
  113.4 0.6 collective-permute-start.24
  114.0 2.6 %unpack_query.1 = (f32[128,4096]{1,0:T(8,128)}, f32[8,4,128]{2,1,0:T(4,128)}) custom-call(s32[4]{0:T(128)S(1)} %copy-done.4, bf16[2,528,128]{2,1,0:T(8,128)(2,1)S(1)} %get-tuple-element.141.refs_0_, bf16[2,528,128]{2,1,0:T(8,128)(2,1)S(1)} %collective-permute-done.16.refs_1_, bf16[2,528,128]{2,1,0:T(8,128)(2,1)S(1)} %collective-permute-done.13.refs_2_, ...), custom_call_target="tpu_custom_call" | custom-call | flops 1000000 | bytes 4000000 | tf_op jit(solution)/shard_map/unpack_query/pallas_call | solution.py:636
  116.6 0.8 collective-permute-done.22.s1
  117.4 2.9 %collective-permute-done.23.s2 = f32[2,136,128]{2,1,0:T(8,128)S(1)} collective-permute-done((f32[2,136,128]{2,1,0:T(8,128)S(1)}, f32[2,136,128]{2,1,0:T(8,128)S(1)}, u32[]{:S(2)}, u32[]{:S(2)}) %collective-permute-start.23) | collective-permute-done | bytes 139296 | tf_op jit(solution)/shard_map/ppermute | solution.py:44
  120.2 0.4 collective-permute-done.24.s3
  120.7 1.2 collective-permute-start.25
  121.9 1.2 collective-permute-done.25.crossed
  123.0 1.4 %unpack_pairs.1 = (f32[128,1024]{1,0:T(8,128)}, f32[1,1024]{1,0:T(1,128)}) custom-call(s32[4]{0:T(128)S(1)} %copy-done.4, f32[2,136,128]{2,1,0:T(8,128)S(1)} %get-tuple-element.184.s0, f32[2,136,128]{2,1,0:T(8,128)S(1)} %collective-permute-done.22.s1, f32[2,136,128]{2,1,0:T(8,128)S(1)} %collective-permute-done.23.s2, ...), custom_call_target="tpu_custom_call" | custom-call | tf_op jit(solution)/shard_map/unpack_pairs/pallas_call | solution.py:603
  (36 shorter events, 0.2 us)
Async XLA Ops:
  0.6 14.7 %copy-start.6 = (s32[1,24]{1,0:T(1,128)S(1)}, s32[1,24]{1,0:T(1,128)}, u32[]{:S(2)}) copy-start(s32[1,24]{1,0:T(1,128)} %parent.1) | copy-start | bytes 292
  0.6 14.6 %copy-start.7 = (s32[1,24]{1,0:T(1,128)S(1)}, s32[1,24]{1,0:T(1,128)}, u32[]{:S(2)}) copy-start(s32[1,24]{1,0:T(1,128)} %length.1) | copy-start | bytes 292
  0.7 1.0 copy-start.1
  1.7 0.7 copy-start.5
  2.4 6.4 %copy-start.2 = (s32[4]{0:T(128)}, s32[4]{0:T(128)S(1)}, u32[]{:S(2)}) copy-start(s32[4]{0:T(128)S(1)} %pad_add_fusion.ids) | copy-start | bytes 52
  3.0 10.5 %collective-permute-start = (bf16[2,144,128]{2,1,0:T(8,128)(2,1)S(1)}, bf16[2,144,128]{2,1,0:T(8,128)(2,1)S(1)}, u32[]{:S(2)}, u32[]{:S(2)}) collective-permute-start(bf16[2,144,128]{2,1,0:T(8,128)(2,1)S(1)} %get-tuple-element.100), channel_id=1, source_target_pairs={{0,8},{1,9},{2,10},{3,11},{4,12},{5,13},{6,14},{7,15},{8,16},{9,17... | collective-permute-start | bytes 221192 | tf_op jit(solution)/shard_map/ppermute | solution.py:44
  5.1 8.4 %collective-permute-start.1 = (bf16[2,144,128]{2,1,0:T(8,128)(2,1)S(1)}, bf16[2,144,128]{2,1,0:T(8,128)(2,1)S(1)}, u32[]{:S(2)}, u32[]{:S(2)}) collective-permute-start(bf16[2,144,128]{2,1,0:T(8,128)(2,1)S(1)} %get-tuple-element.101), channel_id=1, source_target_pairs={{0,16},{1,17},{2,18},{3,19},{4,20},{5,21},{6,22},{7,23},{8,24},{9,... | collective-permute-start | bytes 221192 | tf_op jit(solution)/shard_map/ppermute | solution.py:44
  7.6 5.9 %collective-permute-start.2 = (bf16[2,144,128]{2,1,0:T(8,128)(2,1)S(1)}, bf16[2,144,128]{2,1,0:T(8,128)(2,1)S(1)}, u32[]{:S(2)}, u32[]{:S(2)}) collective-permute-start(bf16[2,144,128]{2,1,0:T(8,128)(2,1)S(1)} %get-tuple-element.102), channel_id=1, source_target_pairs={{0,24},{1,25},{2,26},{3,27},{4,28},{5,29},{6,30},{7,31},{8,0},{9,1... | collective-permute-start | bytes 221192 | tf_op jit(solution)/shard_map/ppermute | solution.py:44
  13.5 6.3 %collective-permute-start.4 = (bf16[4,1088,128]{2,1,0:T(8,128)(2,1)}, bf16[4,1088,128]{2,1,0:T(8,128)(2,1)S(1)}, u32[]{:S(2)}, u32[]{:S(2)}) collective-permute-start(bf16[4,1088,128]{2,1,0:T(8,128)(2,1)} %get-tuple-element.110), channel_id=1, source_target_pairs={{0,1},{1,0},{2,3},{3,2},{4,5},{5,4},{6,7},{7,6},{8,9},{9,8},{10,11... | collective-permute-start | bytes 3342344 | tf_op jit(solution)/shard_map/ppermute | solution.py:44
  15.2 4.0 %collective-permute-start.3 = (bf16[4,144,128]{2,1,0:T(8,128)(2,1)S(1)}, bf16[4,144,128]{2,1,0:T(8,128)(2,1)S(1)}, u32[]{:S(2)}, u32[]{:S(2)}) collective-permute-start(bf16[4,144,128]{2,1,0:T(8,128)(2,1)S(1)} %pad_maximum_fusion.3), channel_id=1, source_target_pairs={{0,1},{1,0},{2,3},{3,2},{4,5},{5,4},{6,7},{7,6},{8,9},{9,8},{10,11... | collective-permute-start | bytes 442376 | tf_op jit(solution)/shard_map/ppermute | solution.py:44
  15.3 0.7 copy-start.3
  19.8 1.3 %copy-start = (bf16[4,1088,128]{2,1,0:T(8,128)(2,1)S(1)}, bf16[4,1088,128]{2,1,0:T(8,128)(2,1)}, u32[]{:S(2)}) copy-start(bf16[4,1088,128]{2,1,0:T(8,128)(2,1)} %get-tuple-element.109.keep) | copy-start | bytes 3342340
  21.0 29.8 %copy-start.4 = (s32[4]{0:T(128)S(1)}, s32[4]{0:T(128)}, u32[]{:S(2)}) copy-start(s32[4]{0:T(128)} %copy-done.2) | copy-start | bytes 52
  21.2 23.5 %collective-permute-start.5 = (bf16[2,1088,128]{2,1,0:T(8,128)(2,1)S(1)}, bf16[2,1088,128]{2,1,0:T(8,128)(2,1)S(1)}, u32[]{:S(2)}, u32[]{:S(2)}) collective-permute-start(bf16[2,1088,128]{2,1,0:T(8,128)(2,1)S(1)} %get-tuple-element.119), channel_id=1, source_target_pairs={{0,16},{1,17},{2,18},{3,19},{4,20},{5,21},{6,22},{7,23},{8,24},{9,... | collective-permute-start | bytes 1671176 | tf_op jit(solution)/shard_map/ppermute | solution.py:44
  23.2 21.5 %collective-permute-start.6 = (bf16[8,128,128]{2,1,0:T(8,128)(2,1)S(1)}, bf16[8,128,128]{2,1,0:T(8,128)(2,1)S(1)}, u32[]{:S(2)}, u32[]{:S(2)}) collective-permute-start(bf16[8,128,128]{2,1,0:T(8,128)(2,1)S(1)} %get-tuple-element.130), channel_id=1, source_target_pairs={{0,2},{1,3},{2,4},{3,5},{4,6},{5,7},{6,0},{7,1},{8,10},{9,11},{10,... | collective-permute-start | bytes 786440 | tf_op jit(solution)/shard_map/ppermute | solution.py:44
  23.2 21.5 %collective-permute-start.7 = (bf16[8,128,128]{2,1,0:T(8,128)(2,1)S(1)}, bf16[8,128,128]{2,1,0:T(8,128)(2,1)S(1)}, u32[]{:S(2)}, u32[]{:S(2)}) collective-permute-start(bf16[8,128,128]{2,1,0:T(8,128)(2,1)S(1)} %get-tuple-element.130), channel_id=1, source_target_pairs={{0,4},{1,5},{2,6},{3,7},{4,0},{5,1},{6,2},{7,3},{8,12},{9,13},{10,... | collective-permute-start | bytes 786440 | tf_op jit(solution)/shard_map/ppermute | solution.py:44
  25.8 18.9 %collective-permute-start.8 = (bf16[8,128,128]{2,1,0:T(8,128)(2,1)S(1)}, bf16[8,128,128]{2,1,0:T(8,128)(2,1)S(1)}, u32[]{:S(2)}, u32[]{:S(2)}) collective-permute-start(bf16[8,128,128]{2,1,0:T(8,128)(2,1)S(1)} %get-tuple-element.130), channel_id=1, source_target_pairs={{0,6},{1,7},{2,0},{3,1},{4,2},{5,3},{6,4},{7,5},{8,14},{9,15},{10,... | collective-permute-start | bytes 786440 | tf_op jit(solution)/shard_map/ppermute | solution.py:44
  44.8 6.0 %collective-permute-start.11 = (bf16[4,8,128,128]{3,2,1,0:T(8,128)(2,1)S(1)}, bf16[4,8,128,128]{3,2,1,0:T(8,128)(2,1)S(1)}, u32[]{:S(2)}, u32[]{:S(2)}) collective-permute-start(bf16[4,8,128,128]{3,2,1,0:T(8,128)(2,1)S(1)} %pad_maximum_fusion.own), channel_id=1, source_target_pairs={{0,1},{1,0},{2,3},{3,2},{4,5},{5,4},{6,7},{7,6},{8,9},{9,8},{10,11... | collective-permute-start | bytes 3145736 | tf_op jit(solution)/shard_map/ppermute | solution.py:44
  48.0 2.8 %collective-permute-start.12 = (bf16[32,16,128]{2,1,0:T(8,128)(2,1)S(1)}, bf16[32,16,128]{2,1,0:T(8,128)(2,1)S(1)}, u32[]{:S(2)}, u32[]{:S(2)}) collective-permute-start(bf16[32,16,128]{2,1,0:T(8,128)(2,1)S(1)} %all_to_all.10.root_own), channel_id=1, source_target_pairs={{0,1},{1,0},{2,3},{3,2},{4,5},{5,4},{6,7},{7,6},{8,9},{9,8},{10,11... | collective-permute-start | bytes 393224 | tf_op jit(solution)/shard_map/ppermute | solution.py:44
  48.1 15.0 %collective-permute-start.9 = (bf16[2,1088,128]{2,1,0:T(8,128)(2,1)S(1)}, bf16[2,1088,128]{2,1,0:T(8,128)(2,1)S(1)}, u32[]{:S(2)}, u32[]{:S(2)}) collective-permute-start(bf16[2,1088,128]{2,1,0:T(8,128)(2,1)S(1)} %get-tuple-element.124), channel_id=1, source_target_pairs={{0,8},{1,9},{2,10},{3,11},{4,12},{5,13},{6,14},{7,15},{8,16},{9,17... | collective-permute-start | bytes 1671176 | tf_op jit(solution)/shard_map/ppermute | solution.py:44
  48.9 14.2 %collective-permute-start.10 = (bf16[2,1088,128]{2,1,0:T(8,128)(2,1)S(1)}, bf16[2,1088,128]{2,1,0:T(8,128)(2,1)S(1)}, u32[]{:S(2)}, u32[]{:S(2)}) collective-permute-start(bf16[2,1088,128]{2,1,0:T(8,128)(2,1)S(1)} %get-tuple-element.125), channel_id=1, source_target_pairs={{0,24},{1,25},{2,26},{3,27},{4,28},{5,29},{6,30},{7,31},{8,0},{9,1... | collective-permute-start | bytes 1671176 | tf_op jit(solution)/shard_map/ppermute | solution.py:44
  63.1 15.1 %collective-permute-start.13 = (bf16[2,528,128]{2,1,0:T(8,128)(2,1)S(1)}, bf16[2,528,128]{2,1,0:T(8,128)(2,1)S(1)}, u32[]{:S(2)}, u32[]{:S(2)}) collective-permute-start(bf16[2,528,128]{2,1,0:T(8,128)(2,1)S(1)} %get-tuple-element.142), channel_id=1, source_target_pairs={{0,16},{1,17},{2,18},{3,19},{4,20},{5,21},{6,22},{7,23},{8,24},{9,... | collective-permute-start | bytes 811016 | tf_op jit(solution)/shard_map/ppermute | solution.py:44
  78.2 5.1 %collective-permute-start.14 = (bf16[32,128,128]{2,1,0:T(8,128)(2,1)S(1)}, bf16[32,128,128]{2,1,0:T(8,128)(2,1)S(1)}, u32[]{:S(2)}, u32[]{:S(2)}) collective-permute-start(bf16[32,128,128]{2,1,0:T(8,128)(2,1)S(1)} %get-tuple-element.154), channel_id=1, source_target_pairs={{0,1},{1,0},{2,3},{3,2},{4,5},{5,4},{6,7},{7,6},{8,9},{9,8},{10,11... | collective-permute-start | bytes 3145736 | tf_op jit(solution)/shard_map/ppermute | solution.py:44
  80.1 2.5 %collective-permute-start.15 = (f32[32,8,128]{2,1,0:T(8,128)S(1)}, f32[32,8,128]{2,1,0:T(8,128)S(1)}, u32[]{:S(2)}, u32[]{:S(2)}) collective-permute-start(f32[32,8,128]{2,1,0:T(8,128)S(1)} %get-tuple-element.157), channel_id=1, source_target_pairs={{0,1},{1,0},{2,3},{3,2},{4,5},{5,4},{6,7},{7,6},{8,9},{9,8},{10,11... | collective-permute-start | bytes 393224 | tf_op jit(solution)/shard_map/ppermute | solution.py:44
  80.2 17.6 %collective-permute-start.16 = (bf16[2,528,128]{2,1,0:T(8,128)(2,1)S(1)}, bf16[2,528,128]{2,1,0:T(8,128)(2,1)S(1)}, u32[]{:S(2)}, u32[]{:S(2)}) collective-permute-start(bf16[2,528,128]{2,1,0:T(8,128)(2,1)S(1)} %get-tuple-element.163), channel_id=1, source_target_pairs={{0,24},{1,25},{2,26},{3,27},{4,28},{5,29},{6,30},{7,31},{8,0},{9,1... | collective-permute-start | bytes 811016 | tf_op jit(solution)/shard_map/ppermute | solution.py:44
  80.2 17.6 %collective-permute-start.17 = (bf16[2,528,128]{2,1,0:T(8,128)(2,1)S(1)}, bf16[2,528,128]{2,1,0:T(8,128)(2,1)S(1)}, u32[]{:S(2)}, u32[]{:S(2)}) collective-permute-start(bf16[2,528,128]{2,1,0:T(8,128)(2,1)S(1)} %get-tuple-element.164), channel_id=1, source_target_pairs={{0,8},{1,9},{2,10},{3,11},{4,12},{5,13},{6,14},{7,15},{8,16},{9,17... | collective-permute-start | bytes 811016 | tf_op jit(solution)/shard_map/ppermute | solution.py:44
  84.2 22.3 %collective-permute-start.18 = (bf16[8,128,128]{2,1,0:T(8,128)(2,1)}, bf16[8,128,128]{2,1,0:T(8,128)(2,1)S(1)}, u32[]{:S(2)}, u32[]{:S(2)}) collective-permute-start(bf16[8,128,128]{2,1,0:T(8,128)(2,1)} %get-tuple-element.165), channel_id=1, source_target_pairs={{0,6},{1,7},{2,0},{3,1},{4,2},{5,3},{6,4},{7,5},{8,14},{9,15},{10,... | collective-permute-start | bytes 786440 | tf_op jit(solution)/shard_map/ppermute | solution.py:44
  84.2 22.3 %collective-permute-start.19 = (bf16[8,128,128]{2,1,0:T(8,128)(2,1)}, bf16[8,128,128]{2,1,0:T(8,128)(2,1)S(1)}, u32[]{:S(2)}, u32[]{:S(2)}) collective-permute-start(bf16[8,128,128]{2,1,0:T(8,128)(2,1)} %get-tuple-element.166), channel_id=1, source_target_pairs={{0,4},{1,5},{2,6},{3,7},{4,0},{5,1},{6,2},{7,3},{8,12},{9,13},{10,... | collective-permute-start | bytes 786440 | tf_op jit(solution)/shard_map/ppermute | solution.py:44
  88.1 18.5 %collective-permute-start.20 = (bf16[8,128,128]{2,1,0:T(8,128)(2,1)S(1)}, bf16[8,128,128]{2,1,0:T(8,128)(2,1)S(1)}, u32[]{:S(2)}, u32[]{:S(2)}) collective-permute-start(bf16[8,128,128]{2,1,0:T(8,128)(2,1)S(1)} %get-tuple-element.167), channel_id=1, source_target_pairs={{0,2},{1,3},{2,4},{3,5},{4,6},{5,7},{6,0},{7,1},{8,10},{9,11},{10,... | collective-permute-start | bytes 786440 | tf_op jit(solution)/shard_map/ppermute | solution.py:44
  88.1 18.4 %all-to-all-start.1 = ((f32[32,8,128]{2,1,0:T(8,128)}), f32[32,8,128]{2,1,0:T(8,128)S(1)}, u32[]{:S(2)}, u32[]{:S(2)}) async-start(f32[32,8,128]{2,1,0:T(8,128)} %add.3), calls=%async_computation.1 | async-start | bytes 262144 | tf_op jit(solution)/shard_map/all_to_all | solution.py:654
  107.5 6.4 %collective-permute-start.21 = (bf16[4,528,128]{2,1,0:T(8,128)(2,1)S(1)}, bf16[4,528,128]{2,1,0:T(8,128)(2,1)S(1)}, u32[]{:S(2)}, u32[]{:S(2)}) collective-permute-start(bf16[4,528,128]{2,1,0:T(8,128)(2,1)S(1)} %pad_maximum_fusion.1), channel_id=1, source_target_pairs={{0,1},{1,0},{2,3},{3,2},{4,5},{5,4},{6,7},{7,6},{8,9},{9,8},{10,11... | collective-permute-start | bytes 1622024 | tf_op jit(solution)/shard_map/ppermute | solution.py:44
  110.7 6.7 %collective-permute-start.22 = (f32[2,136,128]{2,1,0:T(8,128)S(1)}, f32[2,136,128]{2,1,0:T(8,128)S(1)}, u32[]{:S(2)}, u32[]{:S(2)}) collective-permute-start(f32[2,136,128]{2,1,0:T(8,128)S(1)} %get-tuple-element.179), channel_id=1, source_target_pairs={{0,8},{1,9},{2,10},{3,11},{4,12},{5,13},{6,14},{7,15},{8,16},{9,17... | collective-permute-start | bytes 417800 | tf_op jit(solution)/shard_map/ppermute | solution.py:44
  111.1 9.1 %collective-permute-start.23 = (f32[2,136,128]{2,1,0:T(8,128)S(1)}, f32[2,136,128]{2,1,0:T(8,128)S(1)}, u32[]{:S(2)}, u32[]{:S(2)}) collective-permute-start(f32[2,136,128]{2,1,0:T(8,128)S(1)} %get-tuple-element.180), channel_id=1, source_target_pairs={{0,16},{1,17},{2,18},{3,19},{4,20},{5,21},{6,22},{7,23},{8,24},{9,... | collective-permute-start | bytes 417800 | tf_op jit(solution)/shard_map/ppermute | solution.py:44
  113.4 7.2 %collective-permute-start.24 = (f32[2,136,128]{2,1,0:T(8,128)S(1)}, f32[2,136,128]{2,1,0:T(8,128)S(1)}, u32[]{:S(2)}, u32[]{:S(2)}) collective-permute-start(f32[2,136,128]{2,1,0:T(8,128)S(1)} %get-tuple-element.181), channel_id=1, source_target_pairs={{0,24},{1,25},{2,26},{3,27},{4,28},{5,29},{6,30},{7,31},{8,0},{9,1... | collective-permute-start | bytes 417800 | tf_op jit(solution)/shard_map/ppermute | solution.py:44
  120.7 2.4 %collective-permute-start.25 = (f32[4,136,128]{2,1,0:T(8,128)S(1)}, f32[4,136,128]{2,1,0:T(8,128)S(1)}, u32[]{:S(2)}, u32[]{:S(2)}) collective-permute-start(f32[4,136,128]{2,1,0:T(8,128)S(1)} %pad_maximum_fusion.2), channel_id=1, source_target_pairs={{0,1},{1,0},{2,3},{3,2},{4,5},{5,4},{6,7},{7,6},{8,9},{9,8},{10,11... | collective-permute-start | bytes 835592 | tf_op jit(solution)/shard_map/ppermute | solution.py:44

commit v5 on v4

--- a/solution.py
+++ b/solution.py
@@ -1,4 +1,3 @@
-import functools
 import math
 
 import jax
@@ -328,23 +327,8 @@
     return jnp.concatenate([terms[start + h : start + h + 1, :] for h in range(4)], axis=1)
 
 
-def compute_kernel(ks, ids, lists, counts, kbit, qanc, own, other, root_own, root_other, *refs):
-    msgs, refs = refs[0:2], refs[2:]
-    prior, refs = (refs[0:2], refs[2:]) if ks[0] else ((), refs)
-    outs, refs = refs[0:2], refs[2:]
-    if prior:
-        keep, send, root_keep, root_send, refs = *refs[0:4], refs[4:]
-        keep_held, send_held, sems = refs[7:10]
-        copies = [
-            pltpu.make_async_copy(prior[0], keep_held, sems.at[0]),
-            pltpu.make_async_copy(prior[1], send_held, sems.at[1]),
-        ]
-        for copy in copies:
-            copy.start()
-    else:
-        keep, send, refs = refs[0], refs[1], refs[2:]
-    keys, values, keys_t, root_rows, acc, dk, dv = refs[0:7]
-    x, y, c, z = ids[0], ids[1], ids[2], ids[3]
+def arrange(ids, own, other, root_own, root_other, keys, values, keys_t):
+    y, c = ids[1], ids[2]
     first = c == 0
 
     def load(key_ref, value_ref):
@@ -367,8 +351,6 @@
     keys[TREE_BLOCKS] = jnp.zeros((BLK, HD), BF)
     keys_t[TREE_BLOCKS] = jnp.zeros((BLK, HD), BF)
     values[TREE_BLOCKS] = jnp.zeros((BLK, HD), BF)
-    dk[...] = jnp.zeros(dk.shape, F4)
-    dv[...] = jnp.zeros(dv.shape, F4)
 
     rows_own = root_own[...].astype(F4)[:, 0:8, :].reshape(256, HD)
     rows_other = root_other[...].astype(F4)[:, 0:8, :].reshape(256, HD)
@@ -381,6 +363,49 @@
         values[ROOT_BLOCK + n] = rvalue[rows]
         keys_t[ROOT_BLOCK + n] = rkey_t[:, rows]
 
+
+def early_kernel(ids, lists, counts, kbit, qanc, own, other, root_own, root_other, m0, m1,
+                 o0, o1, dk, dv, keys, values, keys_t, root_rows, acc):
+    arrange(ids, own, other, root_own, root_other, keys, values, keys_t)
+    dk[...] = jnp.zeros(dk.shape, F4)
+    dv[...] = jnp.zeros(dv.shape, F4)
+    work((0, 2), ids, lists, counts, kbit, qanc, keys, values, keys_t, (m0, m1), (o0, o1),
+         root_rows, acc, dk, dv)
+
+
+def late_kernel(ids, lists, counts, kbit, qanc, keys, values, keys_t, dk0, dv0, m0, m1,
+                o0, o1, keep, send, root_keep, root_send, root_rows, acc, dk, dv):
+    dk[...] = dk0[...]
+    dv[...] = dv0[...]
+    work((1, 3), ids, lists, counts, kbit, qanc, keys, values, keys_t, (m0, m1), (o0, o1),
+         root_rows, acc, dk, dv)
+    y = ids[1]
+
+    def store(keep_from, send_from):
+        rows = slice(ROOT_BLOCK, ROOT_BLOCK + 2)
+        for ky in range(4):
+            for block in range(8):
+                at, to = place(y, ky, block), ky * 8 + block
+                keep[to] = keep_from[at]
+                send[to] = send_from[at].astype(BF)
+        root_keep[...] = keep_from[rows].reshape(32, 8, HD)
+        root_send[...] = send_from[rows].reshape(32, 8, HD)
+
+    @pl.when(ids[2] == 0)
+    def _():
+        store(dk, dv)
+
+    @pl.when(ids[2] != 0)
+    def _():
+        store(dv, dk)
+
+
+def work(ks, ids, lists, counts, kbit, qanc, keys, values, keys_t, msgs, outs, root_rows, acc,
+         dk, dv):
+    x, y, c, z = ids[0], ids[1], ids[2], ids[3]
+    rkey = jnp.concatenate([keys[ROOT_BLOCK], keys[ROOT_BLOCK + 1]], axis=0)
+    rvalue = jnp.concatenate([values[ROOT_BLOCK], values[ROOT_BLOCK + 1]], axis=0)
+    rkey_t = jnp.concatenate([keys_t[ROOT_BLOCK], keys_t[ROOT_BLOCK + 1]], axis=1)
     root_rows[...] = jnp.zeros(root_rows.shape, F4)
     special = jnp.zeros((16, HD), F4)
     for i in [2 * k + dc for k in ks for dc in range(2)]:
@@ -402,8 +427,9 @@
     mask = here & (root_key_pos <= root_query_pos)
     prob = jnp.where(mask, jnp.exp2(nt(rkey, query) * SCALE2 - special[8:9, :]), 0.0)
     dscore = (prob * (nt(rvalue, grad) - special[9:10, :])).astype(BF)
-    dv[ROOT_BLOCK : ROOT_BLOCK + 2] = nn(prob.astype(BF), grad).reshape(2, BLK, HD)
-    dk[ROOT_BLOCK : ROOT_BLOCK + 2] = nn(dscore, query).reshape(2, BLK, HD)
+    rows = slice(ROOT_BLOCK, ROOT_BLOCK + 2)
+    dv[rows] = dv[rows] + nn(prob.astype(BF), grad).reshape(2, BLK, HD)
+    dk[rows] = dk[rows] + nn(dscore, query).reshape(2, BLK, HD)
     root_dq = nn(rkey_t, dscore).T * FACTOR
 
     pad = jnp.zeros((12, HD), F4)
@@ -468,73 +494,38 @@
 
         lax.fori_loop(0, 2, query_block, 0)
 
-    def store(keep_from, send_from):
-        rows = slice(ROOT_BLOCK, ROOT_BLOCK + 2)
-        for ky in range(4):
-            for block in range(8):
-                at, to = place(y, ky, block), ky * 8 + block
-                if prior:
-                    keep[to] = keep_from[at] + keep_held[to]
-                    send[to] = (send_from[at] + send_held[to]).astype(BF)
-                else:
-                    keep[to] = keep_from[at]
-                    send[to] = send_from[at]
-        if prior:
-            root_keep[...] = (keep_from[rows] + keep_held[32:34]).reshape(32, 8, HD)
-            root_send[...] = (send_from[rows] + send_held[32:34]).reshape(32, 8, HD)
-        else:
-            keep[32:34] = keep_from[rows]
-            send[32:34] = send_from[rows]
-
-    if prior:
-        for copy in copies:
-            copy.wait()
-
-    @pl.when(first)
-    def _():
-        store(dk, dv)
-
-    @pl.when(c != 0)
-    def _():
-        store(dv, dk)
-
-
-def compute(ks, shared, msgs, prior):
-    blocks = pltpu.VMEM((ALL_BLOCKS, BLK, HD), BF)
-    sums = pltpu.VMEM((ALL_BLOCKS, BLK, HD), F4)
+
+def compute(kernel, name, arrays, outs, scratch):
     part = jax.ShapeDtypeStruct((2, 528, HD), BF)
-    half = jax.ShapeDtypeStruct((34, BLK, HD), F4)
-    held = pltpu.VMEM((34, BLK, HD), F4)
-    if prior:
-        sides = [
-            jax.ShapeDtypeStruct((TREE_BLOCKS, BLK, HD), F4),
-            jax.ShapeDtypeStruct((TREE_BLOCKS, BLK, HD), BF),
-        ] + [jax.ShapeDtypeStruct((32, 8, HD), F4)] * 2
-    else:
-        sides = [half, half]
-    return pl.pallas_call(
-        functools.partial(compute_kernel, ks),
-        in_specs=[smem()] * 3
-        + [vmem()] * 8
-        + [pl.BlockSpec(memory_space=pl.ANY)] * len(prior),
-        out_specs=[vmem()] * (2 + len(sides)),
-        out_shape=[part, part] + sides,
-        scratch_shapes=[
-            blocks,
-            blocks,
-            blocks,
-            pltpu.VMEM((2, HD, HD), F4),
-            pltpu.VMEM((HD, 512), F4),
-            sums,
-            sums,
-        ]
-        + ([held, held, pltpu.SemaphoreType.DMA((2,))] if prior else []),
+    return pl.pallas_call(
+        kernel,
+        in_specs=[smem()] * 3 + [vmem()] * (len(arrays) - 3),
+        out_specs=[vmem()] * (2 + len(outs)),
+        out_shape=[part, part] + outs,
+        scratch_shapes=[pltpu.VMEM((2, HD, HD), F4), pltpu.VMEM((HD, 512), F4)] + scratch,
         compiler_params=params(32 * 1024 * 1024),
         cost_estimate=pl.CostEstimate(
             flops=10**10, bytes_accessed=16 * 10**6, transcendentals=8 * 10**6
         ),
-        name="compute_late" if prior else "compute_early",
-    )(*shared, *msgs, *prior)
+        name=name,
+    )(*arrays)
+
+
+def compute_early(shared, pairs, msgs):
+    sums = jax.ShapeDtypeStruct((ALL_BLOCKS, BLK, HD), F4)
+    blocks = jax.ShapeDtypeStruct((ALL_BLOCKS, BLK, HD), BF)
+    outs = [sums, sums, blocks, blocks, blocks]
+    return compute(early_kernel, "compute_early", (*shared, *pairs, *msgs), outs, [])
+
+
+def compute_late(shared, arranged, sums, msgs):
+    outs = [
+        jax.ShapeDtypeStruct((TREE_BLOCKS, BLK, HD), F4),
+        jax.ShapeDtypeStruct((TREE_BLOCKS, BLK, HD), BF),
+    ] + [jax.ShapeDtypeStruct((32, 8, HD), F4)] * 2
+    held = pltpu.VMEM((ALL_BLOCKS, BLK, HD), F4)
+    arrays = (*shared, *arranged, *sums, *msgs)
+    return compute(late_kernel, "compute_late", arrays, outs, [held, held])
 
 
 def join_cores_kernel(keep, other, stay, *outs):
@@ -705,11 +696,14 @@
     msgs = [merged[0], shift(merged[1], dx=1), msg2, shift(merged[3], dx=3)]
     own = jnp.stack(own, axis=0)
     other, root_other = shift(own, dc=1), shift(root_own, dc=1)
-    shared = (ids, lists, counts, kbit, qanc, own, other, root_own, root_other)
-    part0, part2, *prior = compute((0, 2), shared, (msgs[0], msgs[2]), ())
-    msg1, msg3, part0, part2, *prior = together((msgs[1], msgs[3], part0, part2, *prior))
-
-    part1, part3, keep, send, root_keep, root_send = compute((1, 3), shared, (msg1, msg3), prior)
+    shared = (ids, lists, counts, kbit, qanc)
+    pairs = (own, other, root_own, root_other)
+    part0, part2, *state = compute_early(shared, pairs, (msgs[0], msgs[2]))
+    msg1, msg3, part0, part2, *state = together((msgs[1], msgs[3], part0, part2, *state))
+
+    part1, part3, keep, send, root_keep, root_send = compute_late(
+        shared, state[2:5], state[0:2], (msg1, msg3)
+    )
     back2 = shift(part2, dx=-2)
     back2, part1, part3, keep, send, root_keep, root_send = together(
         (back2, part1, part3, keep, send, root_keep, root_send)

time: 124 us -> 122 us (0.984); the launches traced: 124 us -> 121 us
  starting transfers between devices: 44.5 us -> 39.6 us
    all_to_all x1, starting transfers between devices: 9.09 us -> 3.84 us  [along(): return lax.all_to_all(array, ('leaf', 'y'), 0, 0, tiled=True)]
  transfers between devices with their start and end apart: 27 -> 27, of which waited for: 7 -> 6; matrix products, arithmetic and copies ran while one was open for 1% -> 1% of each run, Pallas kernels for 28% -> 29%
where the time goes in v5:
time: 122 us; the launch traced here: 121 us
  starting transfers between devices  39.6 us (32%)
  Pallas kernels  37.6 us (31%)
  waiting for transfers between devices  18.3 us (15%)
  blocking collectives  17.9 us (15%)
  local copies, waits for them, and re-layouts  4.28 us (4%)
  other arithmetic  1.91 us (2%)
    ppermute x26, starting transfers between devices, shift(): return lax.ppermute(array, ('x', 'y', 'core'), perm(dx, dy, dc))  35.8 us
    pallas_call x2, Pallas kernels, compute(): pl.pallas_call(kernel, in_specs=[smem()] * 3 + [vmem()] * (len(arrays) -...  22.5 us
    all_to_all x1, blocking collectives, along(): return lax.all_to_all(array, ('leaf', 'y'), 0, 0, tiled=True)  17.9 us
    ppermute x26, waiting for transfers between devices, shift(): return lax.ppermute(array, ('x', 'y', 'core'), perm(dx, dy, dc))  9.59 us
    all_to_all x1, waiting for transfers between devices, along(): return lax.all_to_all(array, ('leaf', 'y'), 0, 0, tiled=True)  8.72 us
    pallas_call x1, Pallas kernels, pack_rows(): pl.pallas_call(pack_rows_kernel, in_specs=[smem()] + [pl.BlockSpec(memory...  4.85 us
    all_to_all x1, starting transfers between devices, along(): return lax.all_to_all(array, ('leaf', 'y'), 0, 0, tiled=True)  3.84 us
    unnamed x16, local copies, waits for them, and re-layouts  3.55 us
  transfers between devices with their start and end apart: 27, of which 6 were waited for; matrix products, arithmetic and copies ran while one was open for 1% of the time, Pallas kernels for 29%

profile of v5, /device:TPU:1, one launch (start us, length us, event | category | flops | bytes accessed | tf_op | source)
XLA Modules:
  0.0 120.6 jit_solution(17151999340089293239)
XLA Ops:
  0.6 0.1 pad_add_fusion.ids
  0.7 0.9 copy-done.1
  1.7 0.7 copy-done.5
  2.4 0.6 pack_pairs.1
  3.0 2.1 %collective-permute-start = (bf16[2,144,128]{2,1,0:T(8,128)(2,1)S(1)}, bf16[2,144,128]{2,1,0:T(8,128)(2,1)S(1)}, u32[]{:S(2)}, u32[]{:S(2)}) collective-permute-start(bf16[2,144,128]{2,1,0:T(8,128)(2,1)S(1)} %get-tuple-element.106), channel_id=1, source_target_pairs={{0,8},{1,9},{2,10},{3,11},{4,12},{5,13},{6,14},{7,15},{8,16},{9,17... | collective-permute-start | bytes 221192 | tf_op jit(solution)/shard_map/ppermute | solution.py:43
  5.1 2.5 %collective-permute-start.1 = (bf16[2,144,128]{2,1,0:T(8,128)(2,1)S(1)}, bf16[2,144,128]{2,1,0:T(8,128)(2,1)S(1)}, u32[]{:S(2)}, u32[]{:S(2)}) collective-permute-start(bf16[2,144,128]{2,1,0:T(8,128)(2,1)S(1)} %get-tuple-element.107), channel_id=1, source_target_pairs={{0,16},{1,17},{2,18},{3,19},{4,20},{5,21},{6,22},{7,23},{8,24},{9,... | collective-permute-start | bytes 221192 | tf_op jit(solution)/shard_map/ppermute | solution.py:43
  7.6 1.2 collective-permute-start.2
  8.7 4.9 %pack_rows.1 = (bf16[4,1088,128]{2,1,0:T(8,128)(2,1)}, bf16[4,1088,128]{2,1,0:T(8,128)(2,1)}) custom-call(s32[4]{0:T(128)} %copy-done.2, bf16[128,4096]{1,0:T(8,128)(2,1)} %refs_0_.1, bf16[128,4096]{1,0:T(8,128)(2,1)} %refs_1_.1, bf16[128,4096]{1,0:T(8,128)(2,1)} %refs_2_.1, f32[32,128]{1,0:T(8,128)} %refs_3_.1, bf16[1,4096]{1,0:T(2,128)(2,1)} %refs_4_.1, ...), custom_call_target="tpu_custom_call" | custom-call | tf_op jit(solution)/shard_map/pack_rows/pallas_call | solution.py:254
  13.6 0.0 collective-permute-done.g1
  13.6 0.0 collective-permute-done.1.g2
  13.6 1.6 %collective-permute-start.4 = (bf16[4,1088,128]{2,1,0:T(8,128)(2,1)}, bf16[4,1088,128]{2,1,0:T(8,128)(2,1)S(1)}, u32[]{:S(2)}, u32[]{:S(2)}) collective-permute-start(bf16[4,1088,128]{2,1,0:T(8,128)(2,1)} %get-tuple-element.116), channel_id=1, source_target_pairs={{0,1},{1,0},{2,3},{3,2},{4,5},{5,4},{6,7},{7,6},{8,9},{9,8},{10,11... | collective-permute-start | bytes 3342344 | tf_op jit(solution)/shard_map/ppermute | solution.py:43
  15.3 0.1 collective-permute-start.3
  15.4 0.0 copy-start.3
  15.4 0.6 copy-done.3
  16.1 3.2 %tables.1 = (s32[35,128,128]{2,1,0:T(8,128)S(1)}, s32[32,128]{1,0:T(8,128)S(1)}, s32[8,40]{1,0:T(8,128)S(1)}, s32[8]{0:T(128)S(1)}) custom-call(s32[4]{0:T(128)S(1)} %copy-done.3, s32[1,24]{1,0:T(1,128)S(1)} %copy-done.6, s32[1,24]{1,0:T(1,128)S(1)} %copy-done.7), custom_call_target="tpu_custom_call" | custom-call | flops 1000000 | bytes 4000000 | tf_op jit(solution)/shard_map/tables/pallas_call | solution.py:121
  19.3 0.0 collective-permute-done.3.crossed
  19.3 0.6 join_pairs.1
  19.9 0.0 collective-permute-done.4.other
  19.9 0.0 copy-start
  19.9 1.2 %copy-done = bf16[4,1088,128]{2,1,0:T(8,128)(2,1)S(1)} copy-done((bf16[4,1088,128]{2,1,0:T(8,128)(2,1)S(1)}, bf16[4,1088,128]{2,1,0:T(8,128)(2,1)}, u32[]{:S(2)}) %copy-start) | copy-done | bytes 1114136
  21.1 0.1 merge_rows.1
  21.3 0.0 copy-start.4
  21.3 2.0 %collective-permute-start.5 = (bf16[2,1088,128]{2,1,0:T(8,128)(2,1)S(1)}, bf16[2,1088,128]{2,1,0:T(8,128)(2,1)S(1)}, u32[]{:S(2)}, u32[]{:S(2)}) collective-permute-start(bf16[2,1088,128]{2,1,0:T(8,128)(2,1)S(1)} %get-tuple-element.125), channel_id=1, source_target_pairs={{0,16},{1,17},{2,18},{3,19},{4,20},{5,21},{6,22},{7,23},{8,24},{9,... | collective-permute-start | bytes 1671176 | tf_op jit(solution)/shard_map/ppermute | solution.py:43
  23.3 0.0 collective-permute-start.6
  23.3 2.6 %collective-permute-start.7 = (bf16[8,128,128]{2,1,0:T(8,128)(2,1)S(1)}, bf16[8,128,128]{2,1,0:T(8,128)(2,1)S(1)}, u32[]{:S(2)}, u32[]{:S(2)}) collective-permute-start(bf16[8,128,128]{2,1,0:T(8,128)(2,1)S(1)} %get-tuple-element.136), channel_id=1, source_target_pairs={{0,4},{1,5},{2,6},{3,7},{4,0},{5,1},{6,2},{7,3},{8,12},{9,13},{10,... | collective-permute-start | bytes 786440 | tf_op jit(solution)/shard_map/ppermute | solution.py:43
  25.9 0.9 collective-permute-start.8
  26.8 17.9 %all_to_all.10.root_own = bf16[32,16,128]{2,1,0:T(8,128)(2,1)S(1)} all-to-all(bf16[32,16,128]{2,1,0:T(8,128)(2,1)S(1)} %get-tuple-element.128), channel_id=1, replica_groups=mesh['leaf'=8,'x'=4,'y'=4,'core'=2] {'leaf','y'}, dimensions={0} | all-to-all | bytes 262144 | tf_op jit(solution)/shard_map/all_to_all | solution.py:645
  44.8 0.0 collective-permute-done.6
  44.8 0.0 collective-permute-done.7
  44.8 0.0 collective-permute-done.8
  44.8 0.0 collective-permute-done.5.m1
  44.8 0.1 pad_maximum_fusion.own
  44.9 3.2 %collective-permute-start.11 = (bf16[4,8,128,128]{3,2,1,0:T(8,128)(2,1)S(1)}, bf16[4,8,128,128]{3,2,1,0:T(8,128)(2,1)S(1)}, u32[]{:S(2)}, u32[]{:S(2)}) collective-permute-start(bf16[4,8,128,128]{3,2,1,0:T(8,128)(2,1)S(1)} %pad_maximum_fusion.own), channel_id=1, source_target_pairs={{0,1},{1,0},{2,3},{3,2},{4,5},{5,4},{6,7},{7,6},{8,9},{9,8},{10,11... | collective-permute-start | bytes 3145736 | tf_op jit(solution)/shard_map/ppermute | solution.py:43
  48.1 0.1 collective-permute-start.12
  48.2 0.6 collective-permute-start.9
  48.9 2.0 %collective-permute-start.10 = (bf16[2,1088,128]{2,1,0:T(8,128)(2,1)S(1)}, bf16[2,1088,128]{2,1,0:T(8,128)(2,1)S(1)}, u32[]{:S(2)}, u32[]{:S(2)}) collective-permute-start(bf16[2,1088,128]{2,1,0:T(8,128)(2,1)S(1)} %get-tuple-element.131), channel_id=1, source_target_pairs={{0,24},{1,25},{2,26},{3,27},{4,28},{5,29},{6,30},{7,31},{8,0},{9,1... | collective-permute-start | bytes 1671176 | tf_op jit(solution)/shard_map/ppermute | solution.py:43
  50.9 0.0 collective-permute-done.12.root_other
  50.9 9.4 %compute_early.1 = (bf16[2,528,128]{2,1,0:T(8,128)(2,1)S(1)}, bf16[2,528,128]{2,1,0:T(8,128)(2,1)S(1)}, f32[35,128,128]{2,1,0:T(8,128)S(1)}, f32[35,128,128]{2,1...) custom-call(s32[4]{0:T(128)S(1)} %copy-done.4, ...), custom_call_target="tpu_custom_call" | custom-call | flops 10000000000 | bytes 16000000 | tf_op jit(solution)/shard_map/compute_early/pallas_call | solution.py:500
  60.3 2.9 %collective-permute-done.9.m0 = bf16[2,1088,128]{2,1,0:T(8,128)(2,1)S(1)} collective-permute-done((bf16[2,1088,128]{2,1,0:T(8,128)(2,1)S(1)}, bf16[2,1088,128]{2,1,0:T(8,128)(2,1)S(1)}, u32[]{:S(2)}, u32[]{:S(2)}) %collective-permute-start.9) | collective-permute-done | bytes 557088 | tf_op jit(solution)/shard_map/ppermute | solution.py:43
  63.3 2.1 %collective-permute-start.13 = (bf16[2,528,128]{2,1,0:T(8,128)(2,1)S(1)}, bf16[2,528,128]{2,1,0:T(8,128)(2,1)S(1)}, u32[]{:S(2)}, u32[]{:S(2)}) collective-permute-start(bf16[2,528,128]{2,1,0:T(8,128)(2,1)S(1)} %get-tuple-element.151), channel_id=1, source_target_pairs={{0,16},{1,17},{2,18},{3,19},{4,20},{5,21},{6,22},{7,23},{8,24},{9,... | collective-permute-start | bytes 811016 | tf_op jit(solution)/shard_map/ppermute | solution.py:43
  65.4 13.2 %compute_late.1 = (bf16[2,528,128]{2,1,0:T(8,128)(2,1)S(1)}, bf16[2,528,128]{2,1,0:T(8,128)(2,1)S(1)}, f32[32,128,128]{2,1,0:T(8,128)S(1)}, bf16[32,128,128]{2,1...) custom-call(s32[4]{0:T(128)S(1)} %copy-done.4, s32[8,40]{1,0:T(8,128)S(1)} %get-tuple-element.132.lists, ...), custom_call_target="tpu_custom_call" | custom-call | flops 10000000000 | bytes 16000000 | tf_op jit(solution)/shard_map/compute_late/pallas_call | solution.py:500
  78.6 1.9 %collective-permute-start.14 = (bf16[32,128,128]{2,1,0:T(8,128)(2,1)S(1)}, bf16[32,128,128]{2,1,0:T(8,128)(2,1)S(1)}, u32[]{:S(2)}, u32[]{:S(2)}) collective-permute-start(bf16[32,128,128]{2,1,0:T(8,128)(2,1)S(1)} %get-tuple-element.166), channel_id=1, source_target_pairs={{0,1},{1,0},{2,3},{3,2},{4,5},{5,4},{6,7},{7,6},{8,9},{9,8},{10,11... | collective-permute-start | bytes 3145736 | tf_op jit(solution)/shard_map/ppermute | solution.py:43
  80.5 0.1 collective-permute-start.15
  80.6 1.5 %collective-permute-start.17 = (bf16[2,528,128]{2,1,0:T(8,128)(2,1)S(1)}, bf16[2,528,128]{2,1,0:T(8,128)(2,1)S(1)}, u32[]{:S(2)}, u32[]{:S(2)}) collective-permute-start(bf16[2,528,128]{2,1,0:T(8,128)(2,1)S(1)} %get-tuple-element.176), channel_id=1, source_target_pairs={{0,8},{1,9},{2,10},{3,11},{4,12},{5,13},{6,14},{7,15},{8,16},{9,17... | collective-permute-start | bytes 811016 | tf_op jit(solution)/shard_map/ppermute | solution.py:43
  82.1 0.9 collective-permute-done.15
  83.0 0.7 add.3
  83.7 1.0 join_cores.1
  84.6 4.0 %collective-permute-start.19 = (bf16[8,128,128]{2,1,0:T(8,128)(2,1)}, bf16[8,128,128]{2,1,0:T(8,128)(2,1)S(1)}, u32[]{:S(2)}, u32[]{:S(2)}) collective-permute-start(bf16[8,128,128]{2,1,0:T(8,128)(2,1)} %get-tuple-element.178), channel_id=1, source_target_pairs={{0,4},{1,5},{2,6},{3,7},{4,0},{5,1},{6,2},{7,3},{8,12},{9,13},{10,... | collective-permute-start | bytes 786440 | tf_op jit(solution)/shard_map/ppermute | solution.py:43
  88.6 0.9 collective-permute-start.20
  89.5 3.8 %all-to-all-start.1 = ((f32[32,8,128]{2,1,0:T(8,128)}), f32[32,8,128]{2,1,0:T(8,128)S(1)}, u32[]{:S(2)}, u32[]{:S(2)}) async-start(f32[32,8,128]{2,1,0:T(8,128)} %add.3), calls=%async_computation.1 | async-start | bytes 262144 | tf_op jit(solution)/shard_map/all_to_all | solution.py:645
  93.3 0.7 slice.42
  94.0 8.7 %all-to-all-done.1.roots = f32[32,8,128]{2,1,0:T(8,128)S(1)} async-done(((f32[32,8,128]{2,1,0:T(8,128)}), f32[32,8,128]{2,1,0:T(8,128)S(1)}, u32[]{:S(2)}, u32[]{:S(2)}) %all-to-all-start.1) | async-done | bytes 131104 | tf_op jit(solution)/shard_map/all_to_all | solution.py:645
  102.8 1.0 pad_maximum_fusion.1
  103.8 2.5 %collective-permute-start.21 = (bf16[4,528,128]{2,1,0:T(8,128)(2,1)S(1)}, bf16[4,528,128]{2,1,0:T(8,128)(2,1)S(1)}, u32[]{:S(2)}, u32[]{:S(2)}) collective-permute-start(bf16[4,528,128]{2,1,0:T(8,128)(2,1)S(1)} %pad_maximum_fusion.1), channel_id=1, source_target_pairs={{0,1},{1,0},{2,3},{3,2},{4,5},{5,4},{6,7},{7,6},{8,9},{9,8},{10,11... | collective-permute-start | bytes 1622024 | tf_op jit(solution)/shard_map/ppermute | solution.py:43
  106.2 0.7 sum_pairs.1
  106.9 0.1 collective-permute-start.22
  107.0 1.8 %collective-permute-start.23 = (f32[2,136,128]{2,1,0:T(8,128)S(1)}, f32[2,136,128]{2,1,0:T(8,128)S(1)}, u32[]{:S(2)}, u32[]{:S(2)}) collective-permute-start(f32[2,136,128]{2,1,0:T(8,128)S(1)} %get-tuple-element.192), channel_id=1, source_target_pairs={{0,16},{1,17},{2,18},{3,19},{4,20},{5,21},{6,22},{7,23},{8,24},{9,... | collective-permute-start | bytes 417800 | tf_op jit(solution)/shard_map/ppermute | solution.py:43
  108.8 0.9 collective-permute-start.24
  109.6 2.6 %unpack_query.1 = (f32[128,4096]{1,0:T(8,128)}, f32[8,4,128]{2,1,0:T(4,128)}) custom-call(s32[4]{0:T(128)S(1)} %copy-done.4, bf16[2,528,128]{2,1,0:T(8,128)(2,1)S(1)} %get-tuple-element.150.refs_0_, bf16[2,528,128]{2,1,0:T(8,128)(2,1)S(1)} %collective-permute-done.16.refs_1_, bf16[2,528,128]{2,1,0:T(8,128)(2,1)S(1)} %collective-permute-done.13.refs_2_, ...), custom_call_target="tpu_custom_call" | custom-call | flops 1000000 | bytes 4000000 | tf_op jit(solution)/shard_map/unpack_query/pallas_call | solution.py:627
  112.2 4.2 %collective-permute-done.22.s1 = f32[2,136,128]{2,1,0:T(8,128)S(1)} collective-permute-done((f32[2,136,128]{2,1,0:T(8,128)S(1)}, f32[2,136,128]{2,1,0:T(8,128)S(1)}, u32[]{:S(2)}, u32[]{:S(2)}) %collective-permute-start.22) | collective-permute-done | bytes 139296 | tf_op jit(solution)/shard_map/ppermute | solution.py:43
  116.4 0.3 collective-permute-done.24.s3
  116.8 1.2 collective-permute-start.25
  118.0 1.2 collective-permute-done.25.crossed
  119.2 1.4 %unpack_pairs.1 = (f32[128,1024]{1,0:T(8,128)}, f32[1,1024]{1,0:T(1,128)}) custom-call(s32[4]{0:T(128)S(1)} %copy-done.4, f32[2,136,128]{2,1,0:T(8,128)S(1)} %get-tuple-element.196.s0, f32[2,136,128]{2,1,0:T(8,128)S(1)} %collective-permute-done.22.s1, f32[2,136,128]{2,1,0:T(8,128)S(1)} %collective-permute-done.23.s2, ...), custom_call_target="tpu_custom_call" | custom-call | tf_op jit(solution)/shard_map/unpack_pairs/pallas_call | solution.py:594
  (36 shorter events, 0.2 us)
Async XLA Ops:
  0.7 1.0 copy-start.1
  1.7 0.7 copy-start.5
  2.4 6.4 %copy-start.2 = (s32[4]{0:T(128)}, s32[4]{0:T(128)S(1)}, u32[]{:S(2)}) copy-start(s32[4]{0:T(128)S(1)} %pad_add_fusion.ids) | copy-start | bytes 52
  3.0 10.6 %collective-permute-start = (bf16[2,144,128]{2,1,0:T(8,128)(2,1)S(1)}, bf16[2,144,128]{2,1,0:T(8,128)(2,1)S(1)}, u32[]{:S(2)}, u32[]{:S(2)}) collective-permute-start(bf16[2,144,128]{2,1,0:T(8,128)(2,1)S(1)} %get-tuple-element.106), channel_id=1, source_target_pairs={{0,8},{1,9},{2,10},{3,11},{4,12},{5,13},{6,14},{7,15},{8,16},{9,17... | collective-permute-start | bytes 221192 | tf_op jit(solution)/shard_map/ppermute | solution.py:43
  5.1 8.5 %collective-permute-start.1 = (bf16[2,144,128]{2,1,0:T(8,128)(2,1)S(1)}, bf16[2,144,128]{2,1,0:T(8,128)(2,1)S(1)}, u32[]{:S(2)}, u32[]{:S(2)}) collective-permute-start(bf16[2,144,128]{2,1,0:T(8,128)(2,1)S(1)} %get-tuple-element.107), channel_id=1, source_target_pairs={{0,16},{1,17},{2,18},{3,19},{4,20},{5,21},{6,22},{7,23},{8,24},{9,... | collective-permute-start | bytes 221192 | tf_op jit(solution)/shard_map/ppermute | solution.py:43
  7.6 6.0 %collective-permute-start.2 = (bf16[2,144,128]{2,1,0:T(8,128)(2,1)S(1)}, bf16[2,144,128]{2,1,0:T(8,128)(2,1)S(1)}, u32[]{:S(2)}, u32[]{:S(2)}) collective-permute-start(bf16[2,144,128]{2,1,0:T(8,128)(2,1)S(1)} %get-tuple-element.108), channel_id=1, source_target_pairs={{0,24},{1,25},{2,26},{3,27},{4,28},{5,29},{6,30},{7,31},{8,0},{9,1... | collective-permute-start | bytes 221192 | tf_op jit(solution)/shard_map/ppermute | solution.py:43
  8.7 6.7 %copy-start.6 = (s32[1,24]{1,0:T(1,128)S(1)}, s32[1,24]{1,0:T(1,128)}, u32[]{:S(2)}) copy-start(s32[1,24]{1,0:T(1,128)} %parent.1) | copy-start | bytes 292
  8.7 6.7 %copy-start.7 = (s32[1,24]{1,0:T(1,128)S(1)}, s32[1,24]{1,0:T(1,128)}, u32[]{:S(2)}) copy-start(s32[1,24]{1,0:T(1,128)} %length.1) | copy-start | bytes 292
  13.6 6.3 %collective-permute-start.4 = (bf16[4,1088,128]{2,1,0:T(8,128)(2,1)}, bf16[4,1088,128]{2,1,0:T(8,128)(2,1)S(1)}, u32[]{:S(2)}, u32[]{:S(2)}) collective-permute-start(bf16[4,1088,128]{2,1,0:T(8,128)(2,1)} %get-tuple-element.116), channel_id=1, source_target_pairs={{0,1},{1,0},{2,3},{3,2},{4,5},{5,4},{6,7},{7,6},{8,9},{9,8},{10,11... | collective-permute-start | bytes 3342344 | tf_op jit(solution)/shard_map/ppermute | solution.py:43
  15.3 4.0 %collective-permute-start.3 = (bf16[4,144,128]{2,1,0:T(8,128)(2,1)S(1)}, bf16[4,144,128]{2,1,0:T(8,128)(2,1)S(1)}, u32[]{:S(2)}, u32[]{:S(2)}) collective-permute-start(bf16[4,144,128]{2,1,0:T(8,128)(2,1)S(1)} %pad_maximum_fusion.3), channel_id=1, source_target_pairs={{0,1},{1,0},{2,3},{3,2},{4,5},{5,4},{6,7},{7,6},{8,9},{9,8},{10,11... | collective-permute-start | bytes 442376 | tf_op jit(solution)/shard_map/ppermute | solution.py:43
  15.4 0.7 copy-start.3
  19.9 1.3 %copy-start = (bf16[4,1088,128]{2,1,0:T(8,128)(2,1)S(1)}, bf16[4,1088,128]{2,1,0:T(8,128)(2,1)}, u32[]{:S(2)}) copy-start(bf16[4,1088,128]{2,1,0:T(8,128)(2,1)} %get-tuple-element.115.keep) | copy-start | bytes 3342340
  21.3 29.6 %copy-start.4 = (s32[4]{0:T(128)S(1)}, s32[4]{0:T(128)}, u32[]{:S(2)}) copy-start(s32[4]{0:T(128)} %copy-done.2) | copy-start | bytes 52
  21.3 23.5 %collective-permute-start.5 = (bf16[2,1088,128]{2,1,0:T(8,128)(2,1)S(1)}, bf16[2,1088,128]{2,1,0:T(8,128)(2,1)S(1)}, u32[]{:S(2)}, u32[]{:S(2)}) collective-permute-start(bf16[2,1088,128]{2,1,0:T(8,128)(2,1)S(1)} %get-tuple-element.125), channel_id=1, source_target_pairs={{0,16},{1,17},{2,18},{3,19},{4,20},{5,21},{6,22},{7,23},{8,24},{9,... | collective-permute-start | bytes 1671176 | tf_op jit(solution)/shard_map/ppermute | solution.py:43
  23.3 21.4 %collective-permute-start.6 = (bf16[8,128,128]{2,1,0:T(8,128)(2,1)S(1)}, bf16[8,128,128]{2,1,0:T(8,128)(2,1)S(1)}, u32[]{:S(2)}, u32[]{:S(2)}) collective-permute-start(bf16[8,128,128]{2,1,0:T(8,128)(2,1)S(1)} %get-tuple-element.136), channel_id=1, source_target_pairs={{0,2},{1,3},{2,4},{3,5},{4,6},{5,7},{6,0},{7,1},{8,10},{9,11},{10,... | collective-permute-start | bytes 786440 | tf_op jit(solution)/shard_map/ppermute | solution.py:43
  23.3 21.4 %collective-permute-start.7 = (bf16[8,128,128]{2,1,0:T(8,128)(2,1)S(1)}, bf16[8,128,128]{2,1,0:T(8,128)(2,1)S(1)}, u32[]{:S(2)}, u32[]{:S(2)}) collective-permute-start(bf16[8,128,128]{2,1,0:T(8,128)(2,1)S(1)} %get-tuple-element.136), channel_id=1, source_target_pairs={{0,4},{1,5},{2,6},{3,7},{4,0},{5,1},{6,2},{7,3},{8,12},{9,13},{10,... | collective-permute-start | bytes 786440 | tf_op jit(solution)/shard_map/ppermute | solution.py:43
  25.9 18.9 %collective-permute-start.8 = (bf16[8,128,128]{2,1,0:T(8,128)(2,1)S(1)}, bf16[8,128,128]{2,1,0:T(8,128)(2,1)S(1)}, u32[]{:S(2)}, u32[]{:S(2)}) collective-permute-start(bf16[8,128,128]{2,1,0:T(8,128)(2,1)S(1)} %get-tuple-element.136), channel_id=1, source_target_pairs={{0,6},{1,7},{2,0},{3,1},{4,2},{5,3},{6,4},{7,5},{8,14},{9,15},{10,... | collective-permute-start | bytes 786440 | tf_op jit(solution)/shard_map/ppermute | solution.py:43
  44.9 6.0 %collective-permute-start.11 = (bf16[4,8,128,128]{3,2,1,0:T(8,128)(2,1)S(1)}, bf16[4,8,128,128]{3,2,1,0:T(8,128)(2,1)S(1)}, u32[]{:S(2)}, u32[]{:S(2)}) collective-permute-start(bf16[4,8,128,128]{3,2,1,0:T(8,128)(2,1)S(1)} %pad_maximum_fusion.own), channel_id=1, source_target_pairs={{0,1},{1,0},{2,3},{3,2},{4,5},{5,4},{6,7},{7,6},{8,9},{9,8},{10,11... | collective-permute-start | bytes 3145736 | tf_op jit(solution)/shard_map/ppermute | solution.py:43
  48.1 2.8 %collective-permute-start.12 = (bf16[32,16,128]{2,1,0:T(8,128)(2,1)S(1)}, bf16[32,16,128]{2,1,0:T(8,128)(2,1)S(1)}, u32[]{:S(2)}, u32[]{:S(2)}) collective-permute-start(bf16[32,16,128]{2,1,0:T(8,128)(2,1)S(1)} %all_to_all.10.root_own), channel_id=1, source_target_pairs={{0,1},{1,0},{2,3},{3,2},{4,5},{5,4},{6,7},{7,6},{8,9},{9,8},{10,11... | collective-permute-start | bytes 393224 | tf_op jit(solution)/shard_map/ppermute | solution.py:43
  48.2 15.0 %collective-permute-start.9 = (bf16[2,1088,128]{2,1,0:T(8,128)(2,1)S(1)}, bf16[2,1088,128]{2,1,0:T(8,128)(2,1)S(1)}, u32[]{:S(2)}, u32[]{:S(2)}) collective-permute-start(bf16[2,1088,128]{2,1,0:T(8,128)(2,1)S(1)} %get-tuple-element.130), channel_id=1, source_target_pairs={{0,8},{1,9},{2,10},{3,11},{4,12},{5,13},{6,14},{7,15},{8,16},{9,17... | collective-permute-start | bytes 1671176 | tf_op jit(solution)/shard_map/ppermute | solution.py:43
  48.9 14.4 %collective-permute-start.10 = (bf16[2,1088,128]{2,1,0:T(8,128)(2,1)S(1)}, bf16[2,1088,128]{2,1,0:T(8,128)(2,1)S(1)}, u32[]{:S(2)}, u32[]{:S(2)}) collective-permute-start(bf16[2,1088,128]{2,1,0:T(8,128)(2,1)S(1)} %get-tuple-element.131), channel_id=1, source_target_pairs={{0,24},{1,25},{2,26},{3,27},{4,28},{5,29},{6,30},{7,31},{8,0},{9,1... | collective-permute-start | bytes 1671176 | tf_op jit(solution)/shard_map/ppermute | solution.py:43
  63.3 15.3 %collective-permute-start.13 = (bf16[2,528,128]{2,1,0:T(8,128)(2,1)S(1)}, bf16[2,528,128]{2,1,0:T(8,128)(2,1)S(1)}, u32[]{:S(2)}, u32[]{:S(2)}) collective-permute-start(bf16[2,528,128]{2,1,0:T(8,128)(2,1)S(1)} %get-tuple-element.151), channel_id=1, source_target_pairs={{0,16},{1,17},{2,18},{3,19},{4,20},{5,21},{6,22},{7,23},{8,24},{9,... | collective-permute-start | bytes 811016 | tf_op jit(solution)/shard_map/ppermute | solution.py:43
  78.6 5.1 %collective-permute-start.14 = (bf16[32,128,128]{2,1,0:T(8,128)(2,1)S(1)}, bf16[32,128,128]{2,1,0:T(8,128)(2,1)S(1)}, u32[]{:S(2)}, u32[]{:S(2)}) collective-permute-start(bf16[32,128,128]{2,1,0:T(8,128)(2,1)S(1)} %get-tuple-element.166), channel_id=1, source_target_pairs={{0,1},{1,0},{2,3},{3,2},{4,5},{5,4},{6,7},{7,6},{8,9},{9,8},{10,11... | collective-permute-start | bytes 3145736 | tf_op jit(solution)/shard_map/ppermute | solution.py:43
  80.5 2.5 %collective-permute-start.15 = (f32[32,8,128]{2,1,0:T(8,128)S(1)}, f32[32,8,128]{2,1,0:T(8,128)S(1)}, u32[]{:S(2)}, u32[]{:S(2)}) collective-permute-start(f32[32,8,128]{2,1,0:T(8,128)S(1)} %get-tuple-element.169), channel_id=1, source_target_pairs={{0,1},{1,0},{2,3},{3,2},{4,5},{5,4},{6,7},{7,6},{8,9},{9,8},{10,11... | collective-permute-start | bytes 393224 | tf_op jit(solution)/shard_map/ppermute | solution.py:43
  80.6 13.4 %collective-permute-start.16 = (bf16[2,528,128]{2,1,0:T(8,128)(2,1)S(1)}, bf16[2,528,128]{2,1,0:T(8,128)(2,1)S(1)}, u32[]{:S(2)}, u32[]{:S(2)}) collective-permute-start(bf16[2,528,128]{2,1,0:T(8,128)(2,1)S(1)} %get-tuple-element.175), channel_id=1, source_target_pairs={{0,24},{1,25},{2,26},{3,27},{4,28},{5,29},{6,30},{7,31},{8,0},{9,1... | collective-permute-start | bytes 811016 | tf_op jit(solution)/shard_map/ppermute | solution.py:43
  80.6 13.4 %collective-permute-start.17 = (bf16[2,528,128]{2,1,0:T(8,128)(2,1)S(1)}, bf16[2,528,128]{2,1,0:T(8,128)(2,1)S(1)}, u32[]{:S(2)}, u32[]{:S(2)}) collective-permute-start(bf16[2,528,128]{2,1,0:T(8,128)(2,1)S(1)} %get-tuple-element.176), channel_id=1, source_target_pairs={{0,8},{1,9},{2,10},{3,11},{4,12},{5,13},{6,14},{7,15},{8,16},{9,17... | collective-permute-start | bytes 811016 | tf_op jit(solution)/shard_map/ppermute | solution.py:43
  84.6 18.1 %collective-permute-start.18 = (bf16[8,128,128]{2,1,0:T(8,128)(2,1)}, bf16[8,128,128]{2,1,0:T(8,128)(2,1)S(1)}, u32[]{:S(2)}, u32[]{:S(2)}) collective-permute-start(bf16[8,128,128]{2,1,0:T(8,128)(2,1)} %get-tuple-element.177), channel_id=1, source_target_pairs={{0,6},{1,7},{2,0},{3,1},{4,2},{5,3},{6,4},{7,5},{8,14},{9,15},{10,... | collective-permute-start | bytes 786440 | tf_op jit(solution)/shard_map/ppermute | solution.py:43
  84.6 18.1 %collective-permute-start.19 = (bf16[8,128,128]{2,1,0:T(8,128)(2,1)}, bf16[8,128,128]{2,1,0:T(8,128)(2,1)S(1)}, u32[]{:S(2)}, u32[]{:S(2)}) collective-permute-start(bf16[8,128,128]{2,1,0:T(8,128)(2,1)} %get-tuple-element.178), channel_id=1, source_target_pairs={{0,4},{1,5},{2,6},{3,7},{4,0},{5,1},{6,2},{7,3},{8,12},{9,13},{10,... | collective-permute-start | bytes 786440 | tf_op jit(solution)/shard_map/ppermute | solution.py:43
  88.6 14.1 %collective-permute-start.20 = (bf16[8,128,128]{2,1,0:T(8,128)(2,1)S(1)}, bf16[8,128,128]{2,1,0:T(8,128)(2,1)S(1)}, u32[]{:S(2)}, u32[]{:S(2)}) collective-permute-start(bf16[8,128,128]{2,1,0:T(8,128)(2,1)S(1)} %get-tuple-element.179), channel_id=1, source_target_pairs={{0,2},{1,3},{2,4},{3,5},{4,6},{5,7},{6,0},{7,1},{8,10},{9,11},{10,... | collective-permute-start | bytes 786440 | tf_op jit(solution)/shard_map/ppermute | solution.py:43
  89.5 13.3 %all-to-all-start.1 = ((f32[32,8,128]{2,1,0:T(8,128)}), f32[32,8,128]{2,1,0:T(8,128)S(1)}, u32[]{:S(2)}, u32[]{:S(2)}) async-start(f32[32,8,128]{2,1,0:T(8,128)} %add.3), calls=%async_computation.1 | async-start | bytes 262144 | tf_op jit(solution)/shard_map/all_to_all | solution.py:645
  103.8 5.9 %collective-permute-start.21 = (bf16[4,528,128]{2,1,0:T(8,128)(2,1)S(1)}, bf16[4,528,128]{2,1,0:T(8,128)(2,1)S(1)}, u32[]{:S(2)}, u32[]{:S(2)}) collective-permute-start(bf16[4,528,128]{2,1,0:T(8,128)(2,1)S(1)} %pad_maximum_fusion.1), channel_id=1, source_target_pairs={{0,1},{1,0},{2,3},{3,2},{4,5},{5,4},{6,7},{7,6},{8,9},{9,8},{10,11... | collective-permute-start | bytes 1622024 | tf_op jit(solution)/shard_map/ppermute | solution.py:43
  106.9 9.6 %collective-permute-start.22 = (f32[2,136,128]{2,1,0:T(8,128)S(1)}, f32[2,136,128]{2,1,0:T(8,128)S(1)}, u32[]{:S(2)}, u32[]{:S(2)}) collective-permute-start(f32[2,136,128]{2,1,0:T(8,128)S(1)} %get-tuple-element.191), channel_id=1, source_target_pairs={{0,8},{1,9},{2,10},{3,11},{4,12},{5,13},{6,14},{7,15},{8,16},{9,17... | collective-permute-start | bytes 417800 | tf_op jit(solution)/shard_map/ppermute | solution.py:43
  107.0 9.5 %collective-permute-start.23 = (f32[2,136,128]{2,1,0:T(8,128)S(1)}, f32[2,136,128]{2,1,0:T(8,128)S(1)}, u32[]{:S(2)}, u32[]{:S(2)}) collective-permute-start(f32[2,136,128]{2,1,0:T(8,128)S(1)} %get-tuple-element.192), channel_id=1, source_target_pairs={{0,16},{1,17},{2,18},{3,19},{4,20},{5,21},{6,22},{7,23},{8,24},{9,... | collective-permute-start | bytes 417800 | tf_op jit(solution)/shard_map/ppermute | solution.py:43
  108.8 8.0 %collective-permute-start.24 = (f32[2,136,128]{2,1,0:T(8,128)S(1)}, f32[2,136,128]{2,1,0:T(8,128)S(1)}, u32[]{:S(2)}, u32[]{:S(2)}) collective-permute-start(f32[2,136,128]{2,1,0:T(8,128)S(1)} %get-tuple-element.193), channel_id=1, source_target_pairs={{0,24},{1,25},{2,26},{3,27},{4,28},{5,29},{6,30},{7,31},{8,0},{9,1... | collective-permute-start | bytes 417800 | tf_op jit(solution)/shard_map/ppermute | solution.py:43
  116.8 2.4 %collective-permute-start.25 = (f32[4,136,128]{2,1,0:T(8,128)S(1)}, f32[4,136,128]{2,1,0:T(8,128)S(1)}, u32[]{:S(2)}, u32[]{:S(2)}) collective-permute-start(f32[4,136,128]{2,1,0:T(8,128)S(1)} %pad_maximum_fusion.2), channel_id=1, source_target_pairs={{0,1},{1,0},{2,3},{3,2},{4,5},{5,4},{6,7},{7,6},{8,9},{9,8},{10,11... | collective-permute-start | bytes 835592 | tf_op jit(solution)/shard_map/ppermute | solution.py:43

commit v6 on v5

--- a/solution.py
+++ b/solution.py
@@ -107,12 +107,11 @@
         lists[i, 0] = ROOT_BLOCK
         lists[i, 1] = ROOT_BLOCK + 1
 
-        def scan(block, found):
-            hit = (seen & kmask[block]) != 0
+        found = jnp.int32(2)
+        for block in range(TREE_BLOCKS):
+            hit = ((seen & kmask[block]) != 0) & (block <= mine)
             lists[i, found] = block
-            return found + hit.astype(jnp.int32)
-
-        found = lax.fori_loop(0, mine + 1, scan, jnp.int32(2))
+            found = found + hit.astype(jnp.int32)
         lists[i, found] = TREE_BLOCKS
         counts[i] = (found + 1) // 2
 
@@ -641,6 +640,23 @@
     )(ids, *back, crossed)
 
 
+def stack_kernel(*refs):
+    out = refs[-1]
+    for n, part in enumerate(refs[:-1]):
+        out[n] = part[1] if part.shape[0] == 2 else part[...]
+
+
+def stack(parts, shape):
+    return pl.pallas_call(
+        stack_kernel,
+        in_specs=[vmem()] * len(parts),
+        out_specs=vmem(),
+        out_shape=jax.ShapeDtypeStruct((len(parts), *shape), parts[0].dtype),
+        compiler_params=params(),
+        name="stack",
+    )(*parts)
+
+
 def along(array):
     return lax.all_to_all(array, ("leaf", "y"), 0, 0, tiled=True)
 
@@ -679,7 +695,7 @@
     keep, send, *pair_parts = together((keep, send, *pair_parts))
 
     merged = merge_rows(keep, shift(send, dc=1))
-    crossed = shift(jnp.stack([part[1] for part in pair_parts], axis=0), dc=1)
+    crossed = shift(stack(pair_parts, (PAIR, HD)), dc=1)
     joined, root_rows = join_pairs(ids, pair_parts, crossed)
     tables = make_tables(ids, parent, node_length)
     joined, root_rows, *rest = together((joined, root_rows, *merged, *tables))
@@ -694,7 +710,7 @@
     )
 
     msgs = [merged[0], shift(merged[1], dx=1), msg2, shift(merged[3], dx=3)]
-    own = jnp.stack(own, axis=0)
+    own = stack(own, (8, BLK, HD))
     other, root_other = shift(own, dc=1), shift(root_own, dc=1)
     shared = (ids, lists, counts, kbit, qanc)
     pairs = (own, other, root_own, root_other)
@@ -721,11 +737,11 @@
     sums = sum_pairs(ids, stay, received, roots)
     sums = [sums[0]] + [shift(sums[k], dx=k) for k in range(1, 4)]
     back = [part0, back1, back2, back3]
-    crossed = shift(jnp.stack([part[1] for part in back], axis=0), dc=1)
+    crossed = shift(stack(back, (528, HD)), dc=1)
     grad_query, grad_query_root = unpack_query(ids, back, crossed)
     grad_query, grad_query_root, *sums = together((grad_query, grad_query_root, *sums))
 
-    crossed_sums = shift(jnp.stack([part[1] for part in sums], axis=0), dc=1)
+    crossed_sums = shift(stack(sums, (BLK + 8, HD)), dc=1)
     grad_pairs, grad_root = unpack_pairs(ids, sums, crossed_sums)
     return grad_query, grad_query_root.reshape(1, 4096), grad_pairs, grad_root
 

time: 122 us -> 120 us (0.984); the launches traced: 121 us -> 120 us
  starting transfers between devices: 39.6 us -> 36.6 us
  Pallas kernels: 37.6 us -> 39.7 us
  blocking collectives: 17.9 us -> 19.4 us
    ppermute x26, starting transfers between devices: 35.8 us -> 32.1 us  [shift(): return lax.ppermute(array, ('x', 'y', 'core'), perm(dx, dy, dc))]
    all_to_all x1, waiting for transfers between devices: 8.72 us -> 10.8 us  [along(): return lax.all_to_all(array, ('leaf', 'y'), 0, 0, tiled=True)]
    pallas_call x2, Pallas kernels: 22.5 us -> 24.4 us  [compute(): pl.pallas_call(kernel, in_specs=[smem()] * 3 + [vmem()] * (len(arrays) -...]
    all_to_all x1, blocking collectives: 17.9 us -> 19.4 us  [along(): return lax.all_to_all(array, ('leaf', 'y'), 0, 0, tiled=True)]
  transfers between devices with their start and end apart: 27 -> 27, of which waited for: 6 -> 6; matrix products, arithmetic and copies ran while one was open for 1% -> 1% of each run, Pallas kernels for 29% -> 31%
where the time goes in v6:
time: 120 us
  Pallas kernels  39.7 us (33%)
  starting transfers between devices  36.6 us (30%)
  blocking collectives  19.4 us (16%)
  waiting for transfers between devices  19.2 us (16%)
  local copies, waits for them, and re-layouts  3.55 us (3%)
    ppermute x26, starting transfers between devices, shift(): return lax.ppermute(array, ('x', 'y', 'core'), perm(dx, dy, dc))  32.1 us
    pallas_call x2, Pallas kernels, compute(): pl.pallas_call(kernel, in_specs=[smem()] * 3 + [vmem()] * (len(arrays) -...  24.4 us
    all_to_all x1, blocking collectives, along(): return lax.all_to_all(array, ('leaf', 'y'), 0, 0, tiled=True)  19.4 us
    all_to_all x1, waiting for transfers between devices, along(): return lax.all_to_all(array, ('leaf', 'y'), 0, 0, tiled=True)  10.8 us
    ppermute x26, waiting for transfers between devices, shift(): return lax.ppermute(array, ('x', 'y', 'core'), perm(dx, dy, dc))  8.41 us
    pallas_call x1, Pallas kernels, pack_rows(): pl.pallas_call(pack_rows_kernel, in_specs=[smem()] + [pl.BlockSpec(memory...  4.85 us
    all_to_all x1, starting transfers between devices, along(): return lax.all_to_all(array, ('leaf', 'y'), 0, 0, tiled=True)  4.53 us
    unnamed x16, local copies, waits for them, and re-layouts  3.55 us
  transfers between devices with their start and end apart: 27, of which 6 were waited for; matrix products, arithmetic and copies ran while one was open for 1% of the time, Pallas kernels for 31%

profile of v6, /device:TPU:1, one launch (start us, length us, event | category | flops | bytes accessed | tf_op | source)
XLA Modules:
  0.0 120.2 jit_solution(7867205308384753966)
XLA Ops:
  0.6 0.1 pad_add_fusion.ids
  0.7 0.9 copy-done.1
  1.7 0.7 copy-done.5
  2.4 0.6 pack_pairs.1
  3.0 2.1 %collective-permute-start = (bf16[2,144,128]{2,1,0:T(8,128)(2,1)S(1)}, bf16[2,144,128]{2,1,0:T(8,128)(2,1)S(1)}, u32[]{:S(2)}, u32[]{:S(2)}) collective-permute-start(bf16[2,144,128]{2,1,0:T(8,128)(2,1)S(1)} %get-tuple-element.106), channel_id=1, source_target_pairs={{0,8},{1,9},{2,10},{3,11},{4,12},{5,13},{6,14},{7,15},{8,16},{9,17... | collective-permute-start | bytes 221192 | tf_op jit(solution)/shard_map/ppermute | solution.py:43
  5.1 2.5 %collective-permute-start.1 = (bf16[2,144,128]{2,1,0:T(8,128)(2,1)S(1)}, bf16[2,144,128]{2,1,0:T(8,128)(2,1)S(1)}, u32[]{:S(2)}, u32[]{:S(2)}) collective-permute-start(bf16[2,144,128]{2,1,0:T(8,128)(2,1)S(1)} %get-tuple-element.107), channel_id=1, source_target_pairs={{0,16},{1,17},{2,18},{3,19},{4,20},{5,21},{6,22},{7,23},{8,24},{9,... | collective-permute-start | bytes 221192 | tf_op jit(solution)/shard_map/ppermute | solution.py:43
  7.6 1.2 collective-permute-start.2
  8.7 4.9 %pack_rows.1 = (bf16[4,1088,128]{2,1,0:T(8,128)(2,1)}, bf16[4,1088,128]{2,1,0:T(8,128)(2,1)}) custom-call(s32[4]{0:T(128)} %copy-done.2, bf16[128,4096]{1,0:T(8,128)(2,1)} %refs_0_.1, bf16[128,4096]{1,0:T(8,128)(2,1)} %refs_1_.1, bf16[128,4096]{1,0:T(8,128)(2,1)} %refs_2_.1, f32[32,128]{1,0:T(8,128)} %refs_3_.1, bf16[1,4096]{1,0:T(2,128)(2,1)} %refs_4_.1, ...), custom_call_target="tpu_custom_call" | custom-call | tf_op jit(solution)/shard_map/pack_rows/pallas_call | solution.py:253
  13.6 0.0 collective-permute-done.1.refs_2_.g2
  13.6 0.0 collective-permute-done.2.refs_3_.g3
  13.6 1.6 %collective-permute-start.4 = (bf16[4,1088,128]{2,1,0:T(8,128)(2,1)}, bf16[4,1088,128]{2,1,0:T(8,128)(2,1)S(1)}, u32[]{:S(2)}, u32[]{:S(2)}) collective-permute-start(bf16[4,1088,128]{2,1,0:T(8,128)(2,1)} %get-tuple-element.116), channel_id=1, source_target_pairs={{0,1},{1,0},{2,3},{3,2},{4,5},{5,4},{6,7},{7,6},{8,9},{9,8},{10,11... | collective-permute-start | bytes 3342344 | tf_op jit(solution)/shard_map/ppermute | solution.py:43
  15.2 0.1 collective-permute-start.3
  15.3 0.0 copy-start.3
  15.4 0.6 copy-done.3
  16.0 3.4 %tables.1 = (s32[35,128,128]{2,1,0:T(8,128)S(1)}, s32[32,128]{1,0:T(8,128)S(1)}, s32[8,40]{1,0:T(8,128)S(1)}, s32[8]{0:T(128)S(1)}) custom-call(s32[4]{0:T(128)S(1)} %copy-done.3, s32[1,24]{1,0:T(1,128)S(1)} %copy-done.6, s32[1,24]{1,0:T(1,128)S(1)} %copy-done.7), custom_call_target="tpu_custom_call" | custom-call | flops 1000000 | bytes 4000000 | tf_op jit(solution)/shard_map/tables/pallas_call | solution.py:120
  19.4 0.0 collective-permute-done.3.crossed
  19.4 0.6 join_pairs.1
  20.0 0.0 collective-permute-done.4.other
  20.0 0.0 copy-start
  20.0 1.2 %copy-done = bf16[4,1088,128]{2,1,0:T(8,128)(2,1)S(1)} copy-done((bf16[4,1088,128]{2,1,0:T(8,128)(2,1)S(1)}, bf16[4,1088,128]{2,1,0:T(8,128)(2,1)}, u32[]{:S(2)}) %copy-start) | copy-done | bytes 1114136
  21.2 0.1 merge_rows.1
  21.4 0.0 copy-start.4
  21.4 2.0 %collective-permute-start.5 = (bf16[2,1088,128]{2,1,0:T(8,128)(2,1)S(1)}, bf16[2,1088,128]{2,1,0:T(8,128)(2,1)S(1)}, u32[]{:S(2)}, u32[]{:S(2)}) collective-permute-start(bf16[2,1088,128]{2,1,0:T(8,128)(2,1)S(1)} %get-tuple-element.125), channel_id=1, source_target_pairs={{0,16},{1,17},{2,18},{3,19},{4,20},{5,21},{6,22},{7,23},{8,24},{9,... | collective-permute-start | bytes 1671176 | tf_op jit(solution)/shard_map/ppermute | solution.py:43
  23.4 1.0 collective-permute-start.8
  24.4 0.3 collective-permute-start.7
  24.8 0.7 collective-permute-start.6
  25.5 19.4 %all_to_all.10.root_own = bf16[32,16,128]{2,1,0:T(8,128)(2,1)S(1)} all-to-all(bf16[32,16,128]{2,1,0:T(8,128)(2,1)S(1)} %get-tuple-element.128), channel_id=1, replica_groups=mesh['leaf'=8,'x'=4,'y'=4,'core'=2] {'leaf','y'}, dimensions={0} | all-to-all | bytes 262144 | tf_op jit(solution)/shard_map/all_to_all | solution.py:661
  44.9 0.0 collective-permute-done.5.m1
  44.9 0.1 stack.25.own
  45.0 3.2 %collective-permute-start.11 = (bf16[4,8,128,128]{3,2,1,0:T(8,128)(2,1)S(1)}, bf16[4,8,128,128]{3,2,1,0:T(8,128)(2,1)S(1)}, u32[]{:S(2)}, u32[]{:S(2)}) collective-permute-start(bf16[4,8,128,128]{3,2,1,0:T(8,128)(2,1)S(1)} %stack.25.own), channel_id=1, source_target_pairs={{0,1},{1,0},{2,3},{3,2},{4,5},{5,4},{6,7},{7,6},{8,9},{9,8},{10,11... | collective-permute-start | bytes 3145736 | tf_op jit(solution)/shard_map/ppermute | solution.py:43
  48.2 0.1 collective-permute-start.12
  48.3 0.6 collective-permute-start.9
  48.9 2.0 %collective-permute-start.10 = (bf16[2,1088,128]{2,1,0:T(8,128)(2,1)S(1)}, bf16[2,1088,128]{2,1,0:T(8,128)(2,1)S(1)}, u32[]{:S(2)}, u32[]{:S(2)}) collective-permute-start(bf16[2,1088,128]{2,1,0:T(8,128)(2,1)S(1)} %get-tuple-element.131), channel_id=1, source_target_pairs={{0,24},{1,25},{2,26},{3,27},{4,28},{5,29},{6,30},{7,31},{8,0},{9,1... | collective-permute-start | bytes 1671176 | tf_op jit(solution)/shard_map/ppermute | solution.py:43
  51.0 0.0 collective-permute-done.12.root_other
  51.0 0.0 collective-permute-done.11.other
  51.0 10.4 %compute_early.1 = (bf16[2,528,128]{2,1,0:T(8,128)(2,1)S(1)}, bf16[2,528,128]{2,1,0:T(8,128)(2,1)S(1)}, f32[35,128,128]{2,1,0:T(8,128)S(1)}, f32[35,128,128]{2,1...) custom-call(s32[4]{0:T(128)S(1)} %copy-done.4, ...), custom_call_target="tpu_custom_call" | custom-call | flops 10000000000 | bytes 16000000 | tf_op jit(solution)/shard_map/compute_early/pallas_call | solution.py:499
  61.4 1.9 %collective-permute-done.9.m0 = bf16[2,1088,128]{2,1,0:T(8,128)(2,1)S(1)} collective-permute-done((bf16[2,1088,128]{2,1,0:T(8,128)(2,1)S(1)}, bf16[2,1088,128]{2,1,0:T(8,128)(2,1)S(1)}, u32[]{:S(2)}, u32[]{:S(2)}) %collective-permute-start.9) | collective-permute-done | bytes 557088 | tf_op jit(solution)/shard_map/ppermute | solution.py:43
  63.3 2.1 %collective-permute-start.13 = (bf16[2,528,128]{2,1,0:T(8,128)(2,1)S(1)}, bf16[2,528,128]{2,1,0:T(8,128)(2,1)S(1)}, u32[]{:S(2)}, u32[]{:S(2)}) collective-permute-start(bf16[2,528,128]{2,1,0:T(8,128)(2,1)S(1)} %get-tuple-element.151), channel_id=1, source_target_pairs={{0,16},{1,17},{2,18},{3,19},{4,20},{5,21},{6,22},{7,23},{8,24},{9,... | collective-permute-start | bytes 811016 | tf_op jit(solution)/shard_map/ppermute | solution.py:43
  65.4 13.9 %compute_late.1 = (bf16[2,528,128]{2,1,0:T(8,128)(2,1)S(1)}, bf16[2,528,128]{2,1,0:T(8,128)(2,1)S(1)}, f32[32,128,128]{2,1,0:T(8,128)S(1)}, bf16[32,128,128]{2,1...) custom-call(s32[4]{0:T(128)S(1)} %copy-done.4, s32[8,40]{1,0:T(8,128)S(1)} %get-tuple-element.132.lists, ...), custom_call_target="tpu_custom_call" | custom-call | flops 10000000000 | bytes 16000000 | tf_op jit(solution)/shard_map/compute_late/pallas_call | solution.py:499
  79.4 0.0 collective-permute-done.13.refs_2_
  79.4 1.9 %collective-permute-start.14 = (bf16[32,128,128]{2,1,0:T(8,128)(2,1)S(1)}, bf16[32,128,128]{2,1,0:T(8,128)(2,1)S(1)}, u32[]{:S(2)}, u32[]{:S(2)}) collective-permute-start(bf16[32,128,128]{2,1,0:T(8,128)(2,1)S(1)} %get-tuple-element.166), channel_id=1, source_target_pairs={{0,1},{1,0},{2,3},{3,2},{4,5},{5,4},{6,7},{7,6},{8,9},{9,8},{10,11... | collective-permute-start | bytes 3145736 | tf_op jit(solution)/shard_map/ppermute | solution.py:43
  81.3 0.1 collective-permute-start.15
  81.4 0.0 collective-permute-start.16
  81.4 1.5 %collective-permute-start.17 = (bf16[2,528,128]{2,1,0:T(8,128)(2,1)S(1)}, bf16[2,528,128]{2,1,0:T(8,128)(2,1)S(1)}, u32[]{:S(2)}, u32[]{:S(2)}) collective-permute-start(bf16[2,528,128]{2,1,0:T(8,128)(2,1)S(1)} %get-tuple-element.176), channel_id=1, source_target_pairs={{0,8},{1,9},{2,10},{3,11},{4,12},{5,13},{6,14},{7,15},{8,16},{9,17... | collective-permute-start | bytes 811016 | tf_op jit(solution)/shard_map/ppermute | solution.py:43
  82.8 0.9 collective-permute-done.15
  83.7 0.7 add.3
  84.4 0.0 collective-permute-done.14.other
  84.4 1.0 join_cores.1
  85.4 2.7 %collective-permute-start.18 = (bf16[8,128,128]{2,1,0:T(8,128)(2,1)}, bf16[8,128,128]{2,1,0:T(8,128)(2,1)S(1)}, u32[]{:S(2)}, u32[]{:S(2)}) collective-permute-start(bf16[8,128,128]{2,1,0:T(8,128)(2,1)} %get-tuple-element.177), channel_id=1, source_target_pairs={{0,6},{1,7},{2,0},{3,1},{4,2},{5,3},{6,4},{7,5},{8,14},{9,15},{10,... | collective-permute-start | bytes 786440 | tf_op jit(solution)/shard_map/ppermute | solution.py:43
  88.2 0.0 collective-permute-start.19
  88.2 0.6 collective-permute-start.20
  88.7 4.5 %all-to-all-start.1 = ((f32[32,8,128]{2,1,0:T(8,128)}), f32[32,8,128]{2,1,0:T(8,128)S(1)}, u32[]{:S(2)}, u32[]{:S(2)}) async-start(f32[32,8,128]{2,1,0:T(8,128)} %add.3), calls=%async_computation.1 | async-start | bytes 262144 | tf_op jit(solution)/shard_map/all_to_all | solution.py:661
  93.3 10.8 %all-to-all-done.1.roots = f32[32,8,128]{2,1,0:T(8,128)S(1)} async-done(((f32[32,8,128]{2,1,0:T(8,128)}), f32[32,8,128]{2,1,0:T(8,128)S(1)}, u32[]{:S(2)}, u32[]{:S(2)}) %all-to-all-start.1) | async-done | bytes 131104 | tf_op jit(solution)/shard_map/all_to_all | solution.py:661
  104.2 1.6 %collective-permute-start.21 = (bf16[4,528,128]{2,1,0:T(8,128)(2,1)S(1)}, bf16[4,528,128]{2,1,0:T(8,128)(2,1)S(1)}, u32[]{:S(2)}, u32[]{:S(2)}) collective-permute-start(bf16[4,528,128]{2,1,0:T(8,128)(2,1)S(1)} %stack.26), channel_id=1, source_target_pairs={{0,1},{1,0},{2,3},{3,2},{4,5},{5,4},{6,7},{7,6},{8,9},{9,8},{10,11... | collective-permute-start | bytes 1622024 | tf_op jit(solution)/shard_map/ppermute | solution.py:43
  105.8 0.7 sum_pairs.1
  106.5 0.1 collective-permute-start.22
  106.6 1.9 %collective-permute-start.23 = (f32[2,136,128]{2,1,0:T(8,128)S(1)}, f32[2,136,128]{2,1,0:T(8,128)S(1)}, u32[]{:S(2)}, u32[]{:S(2)}) collective-permute-start(f32[2,136,128]{2,1,0:T(8,128)S(1)} %get-tuple-element.192), channel_id=1, source_target_pairs={{0,16},{1,17},{2,18},{3,19},{4,20},{5,21},{6,22},{7,23},{8,24},{9,... | collective-permute-start | bytes 417800 | tf_op jit(solution)/shard_map/ppermute | solution.py:43
  108.5 0.8 collective-permute-start.24
  109.3 2.6 %unpack_query.1 = (f32[128,4096]{1,0:T(8,128)}, f32[8,4,128]{2,1,0:T(4,128)}) custom-call(s32[4]{0:T(128)S(1)} %copy-done.4, bf16[2,528,128]{2,1,0:T(8,128)(2,1)S(1)} %get-tuple-element.150.refs_0_, bf16[2,528,128]{2,1,0:T(8,128)(2,1)S(1)} %collective-permute-done.16.refs_1_, bf16[2,528,128]{2,1,0:T(8,128)(2,1)S(1)} %collective-permute-done.13.refs_2_, ...), custom_call_target="tpu_custom_call" | custom-call | flops 1000000 | bytes 4000000 | tf_op jit(solution)/shard_map/unpack_query/pallas_call | solution.py:626
  111.9 4.1 %collective-permute-done.22.refs_1_.s1 = f32[2,136,128]{2,1,0:T(8,128)S(1)} collective-permute-done((f32[2,136,128]{2,1,0:T(8,128)S(1)}, f32[2,136,128]{2,1,0:T(8,128)S(1)}, u32[]{:S(2)}, u32[]{:S(2)}) %collective-permute-start.22) | collective-permute-done | bytes 139296 | tf_op jit(solution)/shard_map/ppermute | solution.py:43
  116.0 0.3 collective-permute-done.24.refs_3_.s3
  116.4 1.2 collective-permute-start.25
  117.6 1.2 collective-permute-done.25.crossed
  118.7 1.4 %unpack_pairs.1 = (f32[128,1024]{1,0:T(8,128)}, f32[1,1024]{1,0:T(1,128)}) custom-call(s32[4]{0:T(128)S(1)} %copy-done.4, f32[2,136,128]{2,1,0:T(8,128)S(1)} %get-tuple-element.196.refs_0_.s0, f32[2,136,128]{2,1,0:T(8,128)S(1)} %collective-permute-done.22.refs_1_.s1, f32[2,136,128]{2,1,0:T(8,128)S(1)} %collective-permute-done.23.refs_2_.s2, ...), custom_call_target="tpu_custom_call" | custom-call | tf_op jit(solution)/shard_map/unpack_pairs/pallas_call | solution.py:593
  (24 shorter events, 0.1 us)
Async XLA Ops:
  0.7 1.0 copy-start.1
  1.7 0.7 copy-start.5
  2.4 6.4 %copy-start.2 = (s32[4]{0:T(128)}, s32[4]{0:T(128)S(1)}, u32[]{:S(2)}) copy-start(s32[4]{0:T(128)S(1)} %pad_add_fusion.ids) | copy-start | bytes 52
  3.0 10.6 %collective-permute-start = (bf16[2,144,128]{2,1,0:T(8,128)(2,1)S(1)}, bf16[2,144,128]{2,1,0:T(8,128)(2,1)S(1)}, u32[]{:S(2)}, u32[]{:S(2)}) collective-permute-start(bf16[2,144,128]{2,1,0:T(8,128)(2,1)S(1)} %get-tuple-element.106), channel_id=1, source_target_pairs={{0,8},{1,9},{2,10},{3,11},{4,12},{5,13},{6,14},{7,15},{8,16},{9,17... | collective-permute-start | bytes 221192 | tf_op jit(solution)/shard_map/ppermute | solution.py:43
  5.1 8.5 %collective-permute-start.1 = (bf16[2,144,128]{2,1,0:T(8,128)(2,1)S(1)}, bf16[2,144,128]{2,1,0:T(8,128)(2,1)S(1)}, u32[]{:S(2)}, u32[]{:S(2)}) collective-permute-start(bf16[2,144,128]{2,1,0:T(8,128)(2,1)S(1)} %get-tuple-element.107), channel_id=1, source_target_pairs={{0,16},{1,17},{2,18},{3,19},{4,20},{5,21},{6,22},{7,23},{8,24},{9,... | collective-permute-start | bytes 221192 | tf_op jit(solution)/shard_map/ppermute | solution.py:43
  7.6 6.0 %collective-permute-start.2 = (bf16[2,144,128]{2,1,0:T(8,128)(2,1)S(1)}, bf16[2,144,128]{2,1,0:T(8,128)(2,1)S(1)}, u32[]{:S(2)}, u32[]{:S(2)}) collective-permute-start(bf16[2,144,128]{2,1,0:T(8,128)(2,1)S(1)} %get-tuple-element.108), channel_id=1, source_target_pairs={{0,24},{1,25},{2,26},{3,27},{4,28},{5,29},{6,30},{7,31},{8,0},{9,1... | collective-permute-start | bytes 221192 | tf_op jit(solution)/shard_map/ppermute | solution.py:43
  8.7 6.6 %copy-start.6 = (s32[1,24]{1,0:T(1,128)S(1)}, s32[1,24]{1,0:T(1,128)}, u32[]{:S(2)}) copy-start(s32[1,24]{1,0:T(1,128)} %parent.1) | copy-start | bytes 292
  8.7 6.6 %copy-start.7 = (s32[1,24]{1,0:T(1,128)S(1)}, s32[1,24]{1,0:T(1,128)}, u32[]{:S(2)}) copy-start(s32[1,24]{1,0:T(1,128)} %length.1) | copy-start | bytes 292
  13.6 6.4 %collective-permute-start.4 = (bf16[4,1088,128]{2,1,0:T(8,128)(2,1)}, bf16[4,1088,128]{2,1,0:T(8,128)(2,1)S(1)}, u32[]{:S(2)}, u32[]{:S(2)}) collective-permute-start(bf16[4,1088,128]{2,1,0:T(8,128)(2,1)} %get-tuple-element.116), channel_id=1, source_target_pairs={{0,1},{1,0},{2,3},{3,2},{4,5},{5,4},{6,7},{7,6},{8,9},{9,8},{10,11... | collective-permute-start | bytes 3342344 | tf_op jit(solution)/shard_map/ppermute | solution.py:43
  15.2 4.1 %collective-permute-start.3 = (bf16[4,144,128]{2,1,0:T(8,128)(2,1)S(1)}, bf16[4,144,128]{2,1,0:T(8,128)(2,1)S(1)}, u32[]{:S(2)}, u32[]{:S(2)}) collective-permute-start(bf16[4,144,128]{2,1,0:T(8,128)(2,1)S(1)} %stack.24), channel_id=1, source_target_pairs={{0,1},{1,0},{2,3},{3,2},{4,5},{5,4},{6,7},{7,6},{8,9},{9,8},{10,11... | collective-permute-start | bytes 442376 | tf_op jit(solution)/shard_map/ppermute | solution.py:43
  15.3 0.7 copy-start.3
  20.0 1.3 %copy-start = (bf16[4,1088,128]{2,1,0:T(8,128)(2,1)S(1)}, bf16[4,1088,128]{2,1,0:T(8,128)(2,1)}, u32[]{:S(2)}) copy-start(bf16[4,1088,128]{2,1,0:T(8,128)(2,1)} %get-tuple-element.115.keep) | copy-start | bytes 3342340
  21.4 29.6 %copy-start.4 = (s32[4]{0:T(128)S(1)}, s32[4]{0:T(128)}, u32[]{:S(2)}) copy-start(s32[4]{0:T(128)} %copy-done.2) | copy-start | bytes 52
  21.4 23.5 %collective-permute-start.5 = (bf16[2,1088,128]{2,1,0:T(8,128)(2,1)S(1)}, bf16[2,1088,128]{2,1,0:T(8,128)(2,1)S(1)}, u32[]{:S(2)}, u32[]{:S(2)}) collective-permute-start(bf16[2,1088,128]{2,1,0:T(8,128)(2,1)S(1)} %get-tuple-element.125), channel_id=1, source_target_pairs={{0,16},{1,17},{2,18},{3,19},{4,20},{5,21},{6,22},{7,23},{8,24},{9,... | collective-permute-start | bytes 1671176 | tf_op jit(solution)/shard_map/ppermute | solution.py:43
  23.4 21.5 %collective-permute-start.8 = (bf16[8,128,128]{2,1,0:T(8,128)(2,1)S(1)}, bf16[8,128,128]{2,1,0:T(8,128)(2,1)S(1)}, u32[]{:S(2)}, u32[]{:S(2)}) collective-permute-start(bf16[8,128,128]{2,1,0:T(8,128)(2,1)S(1)} %get-tuple-element.136.refs_0_), channel_id=1, source_target_pairs={{0,6},{1,7},{2,0},{3,1},{4,2},{5,3},{6,4},{7,5},{8,14},{9,15},{10,... | collective-permute-start | bytes 786440 | tf_op jit(solution)/shard_map/ppermute | solution.py:43
  24.4 20.5 %collective-permute-start.7 = (bf16[8,128,128]{2,1,0:T(8,128)(2,1)S(1)}, bf16[8,128,128]{2,1,0:T(8,128)(2,1)S(1)}, u32[]{:S(2)}, u32[]{:S(2)}) collective-permute-start(bf16[8,128,128]{2,1,0:T(8,128)(2,1)S(1)} %get-tuple-element.136.refs_0_), channel_id=1, source_target_pairs={{0,4},{1,5},{2,6},{3,7},{4,0},{5,1},{6,2},{7,3},{8,12},{9,13},{10,... | collective-permute-start | bytes 786440 | tf_op jit(solution)/shard_map/ppermute | solution.py:43
  24.8 20.1 %collective-permute-start.6 = (bf16[8,128,128]{2,1,0:T(8,128)(2,1)S(1)}, bf16[8,128,128]{2,1,0:T(8,128)(2,1)S(1)}, u32[]{:S(2)}, u32[]{:S(2)}) collective-permute-start(bf16[8,128,128]{2,1,0:T(8,128)(2,1)S(1)} %get-tuple-element.136.refs_0_), channel_id=1, source_target_pairs={{0,2},{1,3},{2,4},{3,5},{4,6},{5,7},{6,0},{7,1},{8,10},{9,11},{10,... | collective-permute-start | bytes 786440 | tf_op jit(solution)/shard_map/ppermute | solution.py:43
  45.0 6.0 %collective-permute-start.11 = (bf16[4,8,128,128]{3,2,1,0:T(8,128)(2,1)S(1)}, bf16[4,8,128,128]{3,2,1,0:T(8,128)(2,1)S(1)}, u32[]{:S(2)}, u32[]{:S(2)}) collective-permute-start(bf16[4,8,128,128]{3,2,1,0:T(8,128)(2,1)S(1)} %stack.25.own), channel_id=1, source_target_pairs={{0,1},{1,0},{2,3},{3,2},{4,5},{5,4},{6,7},{7,6},{8,9},{9,8},{10,11... | collective-permute-start | bytes 3145736 | tf_op jit(solution)/shard_map/ppermute | solution.py:43
  48.2 2.8 %collective-permute-start.12 = (bf16[32,16,128]{2,1,0:T(8,128)(2,1)S(1)}, bf16[32,16,128]{2,1,0:T(8,128)(2,1)S(1)}, u32[]{:S(2)}, u32[]{:S(2)}) collective-permute-start(bf16[32,16,128]{2,1,0:T(8,128)(2,1)S(1)} %all_to_all.10.root_own), channel_id=1, source_target_pairs={{0,1},{1,0},{2,3},{3,2},{4,5},{5,4},{6,7},{7,6},{8,9},{9,8},{10,11... | collective-permute-start | bytes 393224 | tf_op jit(solution)/shard_map/ppermute | solution.py:43
  48.3 15.0 %collective-permute-start.9 = (bf16[2,1088,128]{2,1,0:T(8,128)(2,1)S(1)}, bf16[2,1088,128]{2,1,0:T(8,128)(2,1)S(1)}, u32[]{:S(2)}, u32[]{:S(2)}) collective-permute-start(bf16[2,1088,128]{2,1,0:T(8,128)(2,1)S(1)} %get-tuple-element.130), channel_id=1, source_target_pairs={{0,8},{1,9},{2,10},{3,11},{4,12},{5,13},{6,14},{7,15},{8,16},{9,17... | collective-permute-start | bytes 1671176 | tf_op jit(solution)/shard_map/ppermute | solution.py:43
  48.9 14.4 %collective-permute-start.10 = (bf16[2,1088,128]{2,1,0:T(8,128)(2,1)S(1)}, bf16[2,1088,128]{2,1,0:T(8,128)(2,1)S(1)}, u32[]{:S(2)}, u32[]{:S(2)}) collective-permute-start(bf16[2,1088,128]{2,1,0:T(8,128)(2,1)S(1)} %get-tuple-element.131), channel_id=1, source_target_pairs={{0,24},{1,25},{2,26},{3,27},{4,28},{5,29},{6,30},{7,31},{8,0},{9,1... | collective-permute-start | bytes 1671176 | tf_op jit(solution)/shard_map/ppermute | solution.py:43
  63.3 16.1 %collective-permute-start.13 = (bf16[2,528,128]{2,1,0:T(8,128)(2,1)S(1)}, bf16[2,528,128]{2,1,0:T(8,128)(2,1)S(1)}, u32[]{:S(2)}, u32[]{:S(2)}) collective-permute-start(bf16[2,528,128]{2,1,0:T(8,128)(2,1)S(1)} %get-tuple-element.151), channel_id=1, source_target_pairs={{0,16},{1,17},{2,18},{3,19},{4,20},{5,21},{6,22},{7,23},{8,24},{9,... | collective-permute-start | bytes 811016 | tf_op jit(solution)/shard_map/ppermute | solution.py:43
  79.4 5.0 %collective-permute-start.14 = (bf16[32,128,128]{2,1,0:T(8,128)(2,1)S(1)}, bf16[32,128,128]{2,1,0:T(8,128)(2,1)S(1)}, u32[]{:S(2)}, u32[]{:S(2)}) collective-permute-start(bf16[32,128,128]{2,1,0:T(8,128)(2,1)S(1)} %get-tuple-element.166), channel_id=1, source_target_pairs={{0,1},{1,0},{2,3},{3,2},{4,5},{5,4},{6,7},{7,6},{8,9},{9,8},{10,11... | collective-permute-start | bytes 3145736 | tf_op jit(solution)/shard_map/ppermute | solution.py:43
  81.3 2.5 %collective-permute-start.15 = (f32[32,8,128]{2,1,0:T(8,128)S(1)}, f32[32,8,128]{2,1,0:T(8,128)S(1)}, u32[]{:S(2)}, u32[]{:S(2)}) collective-permute-start(f32[32,8,128]{2,1,0:T(8,128)S(1)} %get-tuple-element.169), channel_id=1, source_target_pairs={{0,1},{1,0},{2,3},{3,2},{4,5},{5,4},{6,7},{7,6},{8,9},{9,8},{10,11... | collective-permute-start | bytes 393224 | tf_op jit(solution)/shard_map/ppermute | solution.py:43
  81.4 11.9 %collective-permute-start.16 = (bf16[2,528,128]{2,1,0:T(8,128)(2,1)S(1)}, bf16[2,528,128]{2,1,0:T(8,128)(2,1)S(1)}, u32[]{:S(2)}, u32[]{:S(2)}) collective-permute-start(bf16[2,528,128]{2,1,0:T(8,128)(2,1)S(1)} %get-tuple-element.175), channel_id=1, source_target_pairs={{0,24},{1,25},{2,26},{3,27},{4,28},{5,29},{6,30},{7,31},{8,0},{9,1... | collective-permute-start | bytes 811016 | tf_op jit(solution)/shard_map/ppermute | solution.py:43
  81.4 11.9 %collective-permute-start.17 = (bf16[2,528,128]{2,1,0:T(8,128)(2,1)S(1)}, bf16[2,528,128]{2,1,0:T(8,128)(2,1)S(1)}, u32[]{:S(2)}, u32[]{:S(2)}) collective-permute-start(bf16[2,528,128]{2,1,0:T(8,128)(2,1)S(1)} %get-tuple-element.176), channel_id=1, source_target_pairs={{0,8},{1,9},{2,10},{3,11},{4,12},{5,13},{6,14},{7,15},{8,16},{9,17... | collective-permute-start | bytes 811016 | tf_op jit(solution)/shard_map/ppermute | solution.py:43
  85.4 18.7 %collective-permute-start.18 = (bf16[8,128,128]{2,1,0:T(8,128)(2,1)}, bf16[8,128,128]{2,1,0:T(8,128)(2,1)S(1)}, u32[]{:S(2)}, u32[]{:S(2)}) collective-permute-start(bf16[8,128,128]{2,1,0:T(8,128)(2,1)} %get-tuple-element.177), channel_id=1, source_target_pairs={{0,6},{1,7},{2,0},{3,1},{4,2},{5,3},{6,4},{7,5},{8,14},{9,15},{10,... | collective-permute-start | bytes 786440 | tf_op jit(solution)/shard_map/ppermute | solution.py:43
  88.2 15.9 %collective-permute-start.19 = (bf16[8,128,128]{2,1,0:T(8,128)(2,1)}, bf16[8,128,128]{2,1,0:T(8,128)(2,1)S(1)}, u32[]{:S(2)}, u32[]{:S(2)}) collective-permute-start(bf16[8,128,128]{2,1,0:T(8,128)(2,1)} %get-tuple-element.178), channel_id=1, source_target_pairs={{0,4},{1,5},{2,6},{3,7},{4,0},{5,1},{6,2},{7,3},{8,12},{9,13},{10,... | collective-permute-start | bytes 786440 | tf_op jit(solution)/shard_map/ppermute | solution.py:43
  88.2 15.9 %collective-permute-start.20 = (bf16[8,128,128]{2,1,0:T(8,128)(2,1)S(1)}, bf16[8,128,128]{2,1,0:T(8,128)(2,1)S(1)}, u32[]{:S(2)}, u32[]{:S(2)}) collective-permute-start(bf16[8,128,128]{2,1,0:T(8,128)(2,1)S(1)} %get-tuple-element.179), channel_id=1, source_target_pairs={{0,2},{1,3},{2,4},{3,5},{4,6},{5,7},{6,0},{7,1},{8,10},{9,11},{10,... | collective-permute-start | bytes 786440 | tf_op jit(solution)/shard_map/ppermute | solution.py:43
  88.7 15.4 %all-to-all-start.1 = ((f32[32,8,128]{2,1,0:T(8,128)}), f32[32,8,128]{2,1,0:T(8,128)S(1)}, u32[]{:S(2)}, u32[]{:S(2)}) async-start(f32[32,8,128]{2,1,0:T(8,128)} %add.3), calls=%async_computation.1 | async-start | bytes 262144 | tf_op jit(solution)/shard_map/all_to_all | solution.py:661
  104.2 5.2 %collective-permute-start.21 = (bf16[4,528,128]{2,1,0:T(8,128)(2,1)S(1)}, bf16[4,528,128]{2,1,0:T(8,128)(2,1)S(1)}, u32[]{:S(2)}, u32[]{:S(2)}) collective-permute-start(bf16[4,528,128]{2,1,0:T(8,128)(2,1)S(1)} %stack.26), channel_id=1, source_target_pairs={{0,1},{1,0},{2,3},{3,2},{4,5},{5,4},{6,7},{7,6},{8,9},{9,8},{10,11... | collective-permute-start | bytes 1622024 | tf_op jit(solution)/shard_map/ppermute | solution.py:43
  106.5 9.6 %collective-permute-start.22 = (f32[2,136,128]{2,1,0:T(8,128)S(1)}, f32[2,136,128]{2,1,0:T(8,128)S(1)}, u32[]{:S(2)}, u32[]{:S(2)}) collective-permute-start(f32[2,136,128]{2,1,0:T(8,128)S(1)} %get-tuple-element.191), channel_id=1, source_target_pairs={{0,8},{1,9},{2,10},{3,11},{4,12},{5,13},{6,14},{7,15},{8,16},{9,17... | collective-permute-start | bytes 417800 | tf_op jit(solution)/shard_map/ppermute | solution.py:43
  106.6 9.5 %collective-permute-start.23 = (f32[2,136,128]{2,1,0:T(8,128)S(1)}, f32[2,136,128]{2,1,0:T(8,128)S(1)}, u32[]{:S(2)}, u32[]{:S(2)}) collective-permute-start(f32[2,136,128]{2,1,0:T(8,128)S(1)} %get-tuple-element.192), channel_id=1, source_target_pairs={{0,16},{1,17},{2,18},{3,19},{4,20},{5,21},{6,22},{7,23},{8,24},{9,... | collective-permute-start | bytes 417800 | tf_op jit(solution)/shard_map/ppermute | solution.py:43
  108.5 7.8 %collective-permute-start.24 = (f32[2,136,128]{2,1,0:T(8,128)S(1)}, f32[2,136,128]{2,1,0:T(8,128)S(1)}, u32[]{:S(2)}, u32[]{:S(2)}) collective-permute-start(f32[2,136,128]{2,1,0:T(8,128)S(1)} %get-tuple-element.193), channel_id=1, source_target_pairs={{0,24},{1,25},{2,26},{3,27},{4,28},{5,29},{6,30},{7,31},{8,0},{9,1... | collective-permute-start | bytes 417800 | tf_op jit(solution)/shard_map/ppermute | solution.py:43
  116.4 2.4 %collective-permute-start.25 = (f32[4,136,128]{2,1,0:T(8,128)S(1)}, f32[4,136,128]{2,1,0:T(8,128)S(1)}, u32[]{:S(2)}, u32[]{:S(2)}) collective-permute-start(f32[4,136,128]{2,1,0:T(8,128)S(1)} %stack.27), channel_id=1, source_target_pairs={{0,1},{1,0},{2,3},{3,2},{4,5},{5,4},{6,7},{7,6},{8,9},{9,8},{10,11... | collective-permute-start | bytes 835592 | tf_op jit(solution)/shard_map/ppermute | solution.py:43
